TPU v7x, 32 devices: a whole 2x2x4 slice. The times are simulated.
32 devices in a mesh: fsdp: 32 (over z, y, x, core).
Axes of the slice: x: 2, y: 2, z: 4, core: 2. Of those that a mesh axis runs over, the one named last changes fastest.
Arguments:
- hidden: bfloat16 [32768, 768], P('fsdp'), may hold values from -6 to 6
- lengths: int32 [64], P('fsdp'), may hold values from 100 to 780, as said below
- w_qkv: bfloat16 [768, 2304], P('fsdp'), may hold values from -0.21875 to 0.21875
- bias_q: bfloat16 [768], P('fsdp'), may hold values from -2 to 2
- bias_v: bfloat16 [768], P('fsdp'), may hold values from -2 to 2
- w_out: bfloat16 [768, 768], P('fsdp'), may hold values from -0.75 to 0.75
- bias_out: bfloat16 [768], P('fsdp'), may hold values from -2 to 2
- norm1_gain: bfloat16 [768], P('fsdp'), may hold values from 0.5 to 1.5
- norm1_bias: bfloat16 [768], P('fsdp'), may hold values from -2 to 2
- w_up: bfloat16 [768, 3072], P('fsdp'), may hold values from -0.21875 to 0.21875
- bias_up: bfloat16 [3072], P('fsdp'), may hold values from -3 to 3
- w_down: bfloat16 [3072, 768], P('fsdp'), may hold values from -0.109375 to 0.109375
- bias_down: bfloat16 [768], P('fsdp'), may hold values from -2 to 2
- norm2_gain: bfloat16 [768], P('fsdp'), may hold values from 0.5 to 1.5
- norm2_bias: bfloat16 [768], P('fsdp'), may hold values from -2 to 2
- cotangent: bfloat16 [32768, 768], P('fsdp'), may hold values from -6 to 6
Outputs:
- output: float32 [32768, 768], P('fsdp')
- grad_hidden: float32 [32768, 768], P('fsdp')
- grad_w_qkv: float32 [768, 2304], P('fsdp')
- grad_bias_q: float32 [768], P('fsdp')
- grad_bias_v: float32 [768], P('fsdp')
- grad_w_out: float32 [768, 768], P('fsdp')
- grad_bias_out: float32 [768], P('fsdp')
- grad_norm1_gain: float32 [768], P('fsdp')
- grad_norm1_bias: float32 [768], P('fsdp')
- grad_w_up: float32 [768, 3072], P('fsdp')
- grad_bias_up: float32 [3072], P('fsdp')
- grad_w_down: float32 [3072, 768], P('fsdp')
- grad_bias_down: float32 [768], P('fsdp')
- grad_norm2_gain: float32 [768], P('fsdp')
- grad_norm2_bias: float32 [768], P('fsdp')
Inputs may be any that keep to these rules, and one draw needn't show every extreme that they name: Block b of 1024 frames holds utterances b*2 to (b+1)*2 - 1 in order from its first frame; a block's lengths sum to at most 1024, the rest is padding. In every draw some utterance has exactly 780 frames.
All inputs are finite; a program needn't handle non-finite values.
Results may differ from a plain program's by a relative error of at most 0.013.
Values may be sent and summed in bfloat16 or wider, within the bound.
No kernel may reach another device: no remote copies, remote signals or barrier semaphores. Data moves between devices by JAX's collectives and lax.ppermute only.
A program may use at most 256 MiB of HBM per device.

v0:
```python
import math

import jax
import jax.numpy as jnp
from jax import lax
from jax.sharding import PartitionSpec as P

DH = 64


EPSILON = 1e-05
ROOT_HALF = 0.7071067811865476
INV_ROOT_TWO_PI = 0.3989422804014327


def segments_of(lengths_here, count_rows):
    bounds = jnp.cumsum(lengths_here)
    position = jnp.arange(count_rows, dtype=jnp.int32)
    segment = jnp.sum((position[:, None] >= bounds[None, :]).astype(jnp.int32), axis=1)
    return (segment, (segment < lengths_here.shape[0]).astype(jnp.float32))


def norm_forward(values_in, gain, shift):
    centre = jnp.mean(values_in, axis=-1, keepdims=True)
    centered = values_in - centre
    spread = jnp.mean(centered * centered, axis=-1, keepdims=True)
    rstd_rows = lax.rsqrt(spread + EPSILON)
    normed = centered * rstd_rows
    return (normed * gain + shift, normed, rstd_rows)


def norm_backward(upstream, normed, rstd_rows, gain):
    scaled = upstream * gain
    plain_mean = jnp.mean(scaled, axis=-1, keepdims=True)
    cross_mean = jnp.mean(scaled * normed, axis=-1, keepdims=True)
    grad_in = rstd_rows * (scaled - plain_mean - normed * cross_mean)
    return (grad_in, jnp.sum(upstream * normed, axis=0), jnp.sum(upstream, axis=0))


def gelu_slope(inner):
    normal_cdf = 0.5 * (1.0 + lax.erf(inner * ROOT_HALF))
    return normal_cdf + inner * jnp.exp(-0.5 * inner * inner) * INV_ROOT_TWO_PI


def masked_scores(query_block, key_rows, segment_block, segment, scale):
    scores = (
        jnp.einsum("qhd,khd->hqk", query_block, key_rows, preferred_element_type=jnp.float32)
        * scale
    )
    same = segment_block[:, None] == segment[None, :]
    return jnp.where(same[None], scores, -1e30)


def attention_forward(queries, key_rows, value_rows, segment):
    count_rows = queries.shape[0]
    span = min(512, count_rows)
    number = count_rows // span
    scale = 1.0 / math.sqrt(queries.shape[2])

    def one_block(index):
        start = index * span
        query_block = lax.dynamic_slice_in_dim(queries, start, span, 0)
        segment_block = lax.dynamic_slice_in_dim(segment, start, span, 0)
        scores = masked_scores(query_block, key_rows, segment_block, segment, scale)
        highest = jnp.max(scores, axis=-1, keepdims=True)
        exps = jnp.exp(scores - highest)
        total = jnp.sum(exps, axis=-1, keepdims=True)
        probs = (exps / total).astype(jnp.bfloat16)
        mixed = jnp.einsum("hqk,khd->qhd", probs, value_rows, preferred_element_type=jnp.float32)
        return (mixed.astype(jnp.bfloat16), (highest + jnp.log(total))[..., 0])

    mixed, logsum = lax.map(one_block, jnp.arange(number, dtype=jnp.int32))
    return (mixed.reshape(count_rows, queries.shape[1] * queries.shape[2]), logsum)


def attention_backward(queries, key_rows, value_rows, segment, logsum, grad_mixed):
    count_rows = queries.shape[0]
    span = min(512, count_rows)
    number = count_rows // span
    scale = 1.0 / math.sqrt(queries.shape[2])

    def one_block(carry, index):
        grad_keys, grad_values = carry
        start = index * span
        query_block = lax.dynamic_slice_in_dim(queries, start, span, 0)
        grad_block = lax.dynamic_slice_in_dim(grad_mixed, start, span, 0)
        segment_block = lax.dynamic_slice_in_dim(segment, start, span, 0)
        scores = masked_scores(query_block, key_rows, segment_block, segment, scale)
        probs = jnp.exp(scores - logsum[index][..., None])
        grad_values = grad_values + jnp.einsum(
            "hqk,qhd->khd",
            probs.astype(jnp.bfloat16),
            grad_block,
            preferred_element_type=jnp.float32,
        )
        grad_probs = jnp.einsum(
            "qhd,khd->hqk", grad_block, value_rows, preferred_element_type=jnp.float32
        )
        weighted = jnp.sum(grad_probs * probs, axis=-1, keepdims=True)
        grad_scores = (probs * (grad_probs - weighted)).astype(jnp.bfloat16)
        grad_query = (
            jnp.einsum("hqk,khd->qhd", grad_scores, key_rows, preferred_element_type=jnp.float32)
            * scale
        )
        grad_keys = (
            grad_keys
            + jnp.einsum(
                "hqk,qhd->khd", grad_scores, query_block, preferred_element_type=jnp.float32
            )
            * scale
        )
        return ((grad_keys, grad_values), grad_query)

    zeros = jnp.zeros(key_rows.shape, jnp.float32)
    (grad_keys, grad_values), grad_queries = lax.scan(
        one_block, (zeros, zeros), jnp.arange(number, dtype=jnp.int32)
    )
    return (grad_queries.reshape(key_rows.shape), grad_keys, grad_values)


def on_device(
    hidden,
    lengths,
    w_qkv,
    bias_q,
    bias_v,
    w_out,
    bias_out,
    norm1_gain,
    norm1_bias,
    w_up,
    bias_up,
    w_down,
    bias_down,
    norm2_gain,
    norm2_bias,
    cotangent,
):
    count_rows, width = hidden.shape
    heads = width // DH
    segment, present = segments_of(lengths, count_rows)
    present_col = present[:, None]
    (
        whole_qkv,
        whole_bias_q,
        whole_bias_v,
        whole_out,
        whole_bias_out,
        whole_gain_one,
        whole_shift_one,
    ) = (
        lax.all_gather(w_qkv, "fsdp", axis=0, tiled=True),
        lax.all_gather(bias_q, "fsdp", axis=0, tiled=True),
        lax.all_gather(bias_v, "fsdp", axis=0, tiled=True),
        lax.all_gather(w_out, "fsdp", axis=0, tiled=True),
        lax.all_gather(bias_out, "fsdp", axis=0, tiled=True),
        lax.all_gather(norm1_gain, "fsdp", axis=0, tiled=True),
        lax.all_gather(norm1_bias, "fsdp", axis=0, tiled=True),
    )
    projected = jnp.dot(hidden, whole_qkv, preferred_element_type=jnp.float32)
    query_part = (projected[:, :width] + whole_bias_q.astype(jnp.float32)).astype(jnp.bfloat16)
    key_part = projected[:, width : 2 * width].astype(jnp.bfloat16)
    value_part = (projected[:, 2 * width :] + whole_bias_v.astype(jnp.float32)).astype(jnp.bfloat16)
    queries = query_part.reshape(count_rows, heads, DH)
    key_rows = key_part.reshape(count_rows, heads, DH)
    value_rows = value_part.reshape(count_rows, heads, DH)
    mixed, logsum = attention_forward(queries, key_rows, value_rows, segment)
    branch = jnp.dot(mixed, whole_out, preferred_element_type=jnp.float32) + whole_bias_out.astype(
        jnp.float32
    )
    first, normed_one, rstd_one = norm_forward(
        hidden.astype(jnp.float32) + branch,
        whole_gain_one.astype(jnp.float32),
        whole_shift_one.astype(jnp.float32),
    )
    first_low = first.astype(jnp.bfloat16)
    whole_up, whole_bias_up, whole_down, whole_bias_down, whole_gain_two, whole_shift_two = (
        lax.all_gather(w_up, "fsdp", axis=0, tiled=True),
        lax.all_gather(bias_up, "fsdp", axis=0, tiled=True),
        lax.all_gather(w_down, "fsdp", axis=0, tiled=True),
        lax.all_gather(bias_down, "fsdp", axis=0, tiled=True),
        lax.all_gather(norm2_gain, "fsdp", axis=0, tiled=True),
        lax.all_gather(norm2_bias, "fsdp", axis=0, tiled=True),
    )
    inner = jnp.dot(first_low, whole_up, preferred_element_type=jnp.float32) + whole_bias_up.astype(
        jnp.float32
    )
    activated = jax.nn.gelu(inner, approximate=False).astype(jnp.bfloat16)
    second = jnp.dot(
        activated, whole_down, preferred_element_type=jnp.float32
    ) + whole_bias_down.astype(jnp.float32)
    result, normed_two, rstd_two = norm_forward(
        first + second, whole_gain_two.astype(jnp.float32), whole_shift_two.astype(jnp.float32)
    )
    output = result * present_col
    back_up, back_down, back_gain_two = (
        lax.all_gather(w_up, "fsdp", axis=0, tiled=True),
        lax.all_gather(w_down, "fsdp", axis=0, tiled=True),
        lax.all_gather(norm2_gain, "fsdp", axis=0, tiled=True),
    )
    upstream = cotangent.astype(jnp.float32) * present_col
    grad_second, grad_gain_two, grad_shift_two = norm_backward(
        upstream, normed_two, rstd_two, back_gain_two.astype(jnp.float32)
    )
    grad_branch_two = grad_second.astype(jnp.bfloat16)
    grad_w_down = jnp.einsum(
        "rf,rd->fd", activated, grad_branch_two, preferred_element_type=jnp.float32
    )
    grad_bias_down = jnp.sum(grad_branch_two.astype(jnp.float32), axis=0)
    grad_activated = jnp.einsum(
        "rd,fd->rf", grad_branch_two, back_down, preferred_element_type=jnp.float32
    )
    grad_inner = (grad_activated * gelu_slope(inner)).astype(jnp.bfloat16)
    grad_w_up = jnp.einsum("rd,rf->df", first_low, grad_inner, preferred_element_type=jnp.float32)
    grad_bias_up = jnp.sum(grad_inner.astype(jnp.float32), axis=0)
    grad_first = grad_second + jnp.einsum(
        "rf,df->rd", grad_inner, back_up, preferred_element_type=jnp.float32
    )
    back_qkv, back_out, back_gain_one = (
        lax.all_gather(w_qkv, "fsdp", axis=0, tiled=True),
        lax.all_gather(w_out, "fsdp", axis=0, tiled=True),
        lax.all_gather(norm1_gain, "fsdp", axis=0, tiled=True),
    )
    grad_sum_one, grad_gain_one, grad_shift_one = norm_backward(
        grad_first, normed_one, rstd_one, back_gain_one.astype(jnp.float32)
    )
    grad_branch_one = grad_sum_one.astype(jnp.bfloat16)
    grad_w_out = jnp.einsum("rd,re->de", mixed, grad_branch_one, preferred_element_type=jnp.float32)
    grad_bias_out = jnp.sum(grad_branch_one.astype(jnp.float32), axis=0)
    grad_mixed = jnp.einsum(
        "re,de->rd", grad_branch_one, back_out, preferred_element_type=jnp.float32
    ).astype(jnp.bfloat16)
    grad_queries, grad_keys, grad_values = attention_backward(
        queries, key_rows, value_rows, segment, logsum, grad_mixed.reshape(count_rows, heads, DH)
    )
    grad_stack = jnp.concatenate(
        [
            grad_queries.reshape(count_rows, width),
            grad_keys.reshape(count_rows, width),
            grad_values.reshape(count_rows, width),
        ],
        axis=1,
    ).astype(jnp.bfloat16)
    grad_w_qkv = jnp.einsum("rd,re->de", hidden, grad_stack, preferred_element_type=jnp.float32)
    grad_bias_q = jnp.sum(grad_stack[:, :width].astype(jnp.float32), axis=0)
    grad_bias_v = jnp.sum(grad_stack[:, 2 * width :].astype(jnp.float32), axis=0)
    grad_hidden = grad_sum_one + jnp.einsum(
        "re,de->rd", grad_stack, back_qkv, preferred_element_type=jnp.float32
    )
    every_sum = (
        lax.psum_scatter(grad_w_qkv, "fsdp", scatter_dimension=0, tiled=True),
        lax.psum_scatter(grad_bias_q, "fsdp", scatter_dimension=0, tiled=True),
        lax.psum_scatter(grad_bias_v, "fsdp", scatter_dimension=0, tiled=True),
        lax.psum_scatter(grad_w_out, "fsdp", scatter_dimension=0, tiled=True),
        lax.psum_scatter(grad_bias_out, "fsdp", scatter_dimension=0, tiled=True),
        lax.psum_scatter(grad_gain_one, "fsdp", scatter_dimension=0, tiled=True),
        lax.psum_scatter(grad_shift_one, "fsdp", scatter_dimension=0, tiled=True),
        lax.psum_scatter(grad_w_up, "fsdp", scatter_dimension=0, tiled=True),
        lax.psum_scatter(grad_bias_up, "fsdp", scatter_dimension=0, tiled=True),
        lax.psum_scatter(grad_w_down, "fsdp", scatter_dimension=0, tiled=True),
        lax.psum_scatter(grad_bias_down, "fsdp", scatter_dimension=0, tiled=True),
        lax.psum_scatter(grad_gain_two, "fsdp", scatter_dimension=0, tiled=True),
        lax.psum_scatter(grad_shift_two, "fsdp", scatter_dimension=0, tiled=True),
    )
    attn_sums = every_sum[:7]
    ffn_sums = every_sum[7:]
    return (
        output,
        grad_hidden,
        attn_sums[0],
        attn_sums[1],
        attn_sums[2],
        attn_sums[3],
        attn_sums[4],
        attn_sums[5],
        attn_sums[6],
        ffn_sums[0],
        ffn_sums[1],
        ffn_sums[2],
        ffn_sums[3],
        ffn_sums[4],
        ffn_sums[5],
    )


def solution(mesh):
    return jax.shard_map(
        on_device,
        mesh=mesh,
        in_specs=(
            P("fsdp", None),
            P("fsdp"),
            P("fsdp", None),
            P("fsdp"),
            P("fsdp"),
            P("fsdp", None),
            P("fsdp"),
            P("fsdp"),
            P("fsdp"),
            P("fsdp", None),
            P("fsdp"),
            P("fsdp", None),
            P("fsdp"),
            P("fsdp"),
            P("fsdp"),
            P("fsdp", None),
        ),
        out_specs=(
            P("fsdp", None),
            P("fsdp", None),
            P("fsdp", None),
            P("fsdp"),
            P("fsdp"),
            P("fsdp", None),
            P("fsdp"),
            P("fsdp"),
            P("fsdp"),
            P("fsdp", None),
            P("fsdp"),
            P("fsdp", None),
            P("fsdp"),
            P("fsdp"),
            P("fsdp"),
        ),
        check_vma=False,
    )
```

profile of v0, /device:TPU:0, one launch (start us, length us, event | category | flops | bytes accessed | tf_op | source)
XLA Modules:
  0.0 923.4 jit_solution(8681289339473029810)
XLA Ops:
  17.7 42.6 %all-reduce.19 = (bf16[768]{0:T(1024)(128)(2,1)S(1)}, bf16[768]{0:T(1024)(128)(2,1)S(1)}, bf16[768]{0:T(1024)(128)(2,1)S(1)}, bf16[768]{0:T(1024)(128)(2,1)S(1)}...) all-reduce(bf16[768]{0:T(1024)(128)(2,1)S(1)} %dynamic-update-slice, ...), channel_id=1, replica_groups=mesh['fsdp'=32] {'fsdp'}, use_global_device_ids=true, to_apply=%add | all-reduce | flops 9216 | bytes 36864
  61.7 2.7 copy.71
  68.0 1.6 copy.77
  70.2 3.7 all-gather.5.cloned.1.call-done
  73.9 5.8 fusion.67
  79.9 1.8 fusion.45
  81.7 2.6 copy.72
  84.3 1.6 copy.74
  86.7 79.1 %while.27 = (s32[]{:T(128)}, bf16[2,512,12,64]{1,3,2,0:T(8,128)(2,1)}, f32[2,12,512]{2,1,0:T(8,128)S(1)}, s32[2]{0:T(128)S(1)}, s32[1024]{0:T(1024)S(1)}, /*inde...) while((s32[]{:T(128)}, ...), condition=%wide.region_5.6_spmd, body=%wide.region_2.5_spmd.sunk | while | flops 1687021568 | bytes 195807504 | solution.py:72
  88.6 12.1 %fusion.111 = (f32[12,512]{1,0:T(8,128)S(1)}, f32[12,512,1024]{2,1,0:T(8,128)}) fusion(pred[512,1024]{1,0:T(8,128)(4,1)S(1)} %broadcast_compare_fusion.4, bf16[1024,12,64]{0,2,1:T(8,128)(2,1)S(1)} %get-tuple-element.479, bf16[1024,12,64]{0,2,1:T(8,128)(2,1)} %get-tuple-element.478, s32[]{:T(128)S(6)} %select_n.60), kind=kOutput, calls=%fused_computation.3.clone.1 | convolution fusion | flops 824174592 | bytes 28073988 | tf_op jit(solution)/shard_map/while/body/eval_jaxpr/qhd,khd->hqk/dot_general | solution.py:47
  100.8 12.3 %fusion.112 = f32[12,512]{1,0:T(8,128)S(1)} fusion(f32[12,512,1024]{2,1,0:T(8,128)} %get-tuple-element.434, f32[12,512]{1,0:T(8,128)S(1)} %get-tuple-element.435, pred[512,1024]{1,0:T(8,128)(4,1)S(1)} %broadcast_compare_fusion.4), kind=kLoop, calls=%fused_computation.4.clone.1 | loop fusion | flops 25159680 | bytes 25739264 | tf_op jit(solution)/shard_map/while/body/eval_jaxpr/reduce_sum | solution.py:67
  113.1 3.0 copy-done
  116.2 9.0 fusion.113
  125.2 1.1 copy-done.17
  128.0 12.2 %fusion.111 = (f32[12,512]{1,0:T(8,128)S(1)}, f32[12,512,1024]{2,1,0:T(8,128)}) fusion(pred[512,1024]{1,0:T(8,128)(4,1)S(1)} %broadcast_compare_fusion.4, bf16[1024,12,64]{0,2,1:T(8,128)(2,1)S(1)} %get-tuple-element.479, bf16[1024,12,64]{0,2,1:T(8,128)(2,1)} %get-tuple-element.478, s32[]{:T(128)S(6)} %select_n.60), kind=kOutput, calls=%fused_computation.3.clone.1 | convolution fusion | flops 824174592 | bytes 28073988 | tf_op jit(solution)/shard_map/while/body/eval_jaxpr/qhd,khd->hqk/dot_general | solution.py:47
  140.3 12.4 %fusion.112 = f32[12,512]{1,0:T(8,128)S(1)} fusion(f32[12,512,1024]{2,1,0:T(8,128)} %get-tuple-element.434, f32[12,512]{1,0:T(8,128)S(1)} %get-tuple-element.435, pred[512,1024]{1,0:T(8,128)(4,1)S(1)} %broadcast_compare_fusion.4), kind=kLoop, calls=%fused_computation.4.clone.1 | loop fusion | flops 25159680 | bytes 25739264 | tf_op jit(solution)/shard_map/while/body/eval_jaxpr/reduce_sum | solution.py:67
  152.6 3.1 copy-done
  155.7 9.0 fusion.113
  164.7 1.1 copy-done.17
  165.9 3.1 copy.75
  169.0 1.6 copy.89
  170.6 3.4 fusion.65
  174.1 1.6 copy-done.4
  176.1 19.1 %all-gather.9.cloned.1.call-done = bf16[768,3072]{1,0:T(8,128)(2,1)} async-done(((bf16[24,3072]{1,0:T(8,128)(2,1)}), bf16[768,3072]{1,0:T(8,128)(2,1)}) %all-gather.9.cloned.1.call-update) | async-done | bytes 4718608 | tf_op jit(solution)/shard_map/all_gather | solution.py:178
  195.3 39.0 %fusion.31 = (bf16[1024,3072]{1,0:T(8,128)(2,1)}, f32[1024,3072]{1,0:T(8,128)}) fusion(f32[3072]{0:T(1024)S(1)} %copy-done.36, bf16[768,3072]{1,0:T(8,128)(2,1)} %all-gather.9.cloned.1.call-done, f32[1024,768]{0,1:T(8,128)} %copy-done.4, f32[768]{0:T(1024)S(1)} %copy-done.38, f32[768]{0:T(1024)S(1)} %copy-done.27, f32[1024]{0:T(1024)S(1)} %add_rsqrt_fusion.1, ...), kind=kOutput, calls=%fused_computation.43 | convolution fusion | flops 5043388416 | bytes 26765312 | tf_op jit(solution)/shard_map/dot_general | solution.py:185
  234.3 26.2 %all-gather.11.cloned.1.call-done = bf16[3072,768]{1,0:T(8,128)(2,1)} async-done(((bf16[96,768]{1,0:T(8,128)(2,1)}), bf16[3072,768]{1,0:T(8,128)(2,1)}) %all-gather.11.cloned.1.call-update) | async-done | bytes 4718608 | tf_op jit(solution)/shard_map/all_gather | solution.py:180
  260.5 9.4 %fusion.66 = (f32[1024]{0:T(1024)S(1)}, f32[1024,768]{0,1:T(8,128)S(1)}) fusion(f32[768]{0:T(1024)S(1)} %copy-done.40, bf16[1024,3072]{1,0:T(8,128)(2,1)} %get-tuple-element.316, bf16[3072,768]{1,0:T(8,128)(2,1)} %all-gather.11.cloned.1.call-done, f32[768]{0:T(1024)S(1)} %copy-done.38, f32[768]{0:T(1024)S(1)} %copy-done.27, f32[1024]{0:T(1024)S(1)} %add_rsqrt_fusion.1, ...), kind=kOutput, calls=%fused_computation.121 | convolution fusion | flops 4837342208 | bytes 17323008 | tf_op jit(solution)/shard_map/dot_general | solution.py:189
  271.3 2.1 multiply_reduce_fusion.1
  273.4 3.7 convert_reduce_fusion.1
  277.1 14.7 %convert_reduce_fusion = (f32[3072]{0:T(1024)}, bf16[1024,3072]{1,0:T(8,128)(2,1)}) fusion(f32[1024,3072]{1,0:T(8,128)} %get-tuple-element.317, f32[3072]{0:T(1024)S(1)} %copy-done.36, bf16[1024,768]{0,1:T(8,128)(2,1)S(1)} %get-tuple-element.302, bf16[3072,768]{1,0:T(8,128)(2,1)S(1)} %copy-done.44), kind=kOutput, calls=%fused_computation.50 | convolution fusion | flops 4872729600 | bytes 25190400 | tf_op jit(solution)/shard_map/rd,fd->rf/dot_general | solution.py:210
  291.9 9.8 %multiply_reduce_fusion.2 = (f32[768]{0:T(1024)}, f32[1024]{0:T(1024)S(1)}, f32[1024]{0:T(1024)S(1)}, f32[768]{0:T(1024)}, f32[1024,768]{0,1:T(8,128)S(1)}) fusion(f32[1024,768]{0,1:T(8,128)S(1)} %copy-done.5, f32[1024]{0:T(1024)S(1)} %add_rsqrt_fusion.1, f32[1024]{0:T(1024)S(1)} %broadcast_multiply_fusion.5, f32[768]{0:T(1024)S(1)} %copy-done.27, ...), kind=kOutput, calls=%fused_computation.75 | convolution fusion | flops 4846776320 | bytes 22069248 | tf_op jit(solution)/shard_map/rf,df->rd/dot_general | solution.py:216
  301.7 1.8 convert_reduce_fusion.2
  303.5 1.8 copy-done.10
  305.2 2.9 fusion.57
  308.2 4.4 convolution_convert_fusion
  312.6 175.6 %while.28 = (s32[]{:T(128)}, f32[1024,12,64]{0,2,1:T(8,128)}, f32[1024,12,64]{0,2,1:T(8,128)}, bf16[2,512,12,64]{1,3,2,0:T(8,128)(2,1)}, s32[2]{0:T(128)S(1)}, /...) while((s32[]{:T(128)}, f32[1024,12,64]{0,2,1:T(8,128)}, ...), condition=%wide.region_16.17_spmd.clone, body=%wide.region_14.16_spmd.clone.sunk | while | flops 4125747200 | bytes 213044000 | solution.py:115
  314.3 11.6 %fusion.123 = f32[12,512,1024]{2,1,0:T(8,128)} fusion(bf16[1024,12,64]{0,2,1:T(8,128)(2,1)S(1)} %get-tuple-element.524, bf16[1024,12,64]{0,2,1:T(8,128)(2,1)} %get-tuple-element.522, s32[]{:T(128)S(6)} %select_n.64), kind=kOutput, calls=%fused_computation.30.clone.1 | convolution fusion | flops 805306368 | bytes 27525124 | tf_op jit(solution)/shard_map/while/body/eval_jaxpr/qhd,khd->hqk/dot_general | solution.py:47
  328.3 18.3 %multiply_reduce_fusion.9 = (f32[12,512]{1,0:T(8,128)S(1)}, f32[12,512,1024]{2,1,0:T(8,128)}) fusion(f32[12,512,1024]{2,1,0:T(8,128)} %fusion.123, f32[12,512]{1,0:T(8,128)S(1)} %dynamic-slice_bitcast_fusion.2, pred[512,1024]{1,0:T(8,128)(4,1)S(1)} %broadcast_compare_fusion.5, bf16[1024,12,64]{0,2,1:T(8,128)(2,1)} %get-tuple-element.527, ...), kind=kOutput, calls=%fused_computation.17.clone.1 | convolution fusion | flops 836757504 | bytes 53264388 | tf_op jit(solution)/shard_map/while/body/eval_jaxpr/qhd,khd->hqk/dot_general | solution.py:96
  346.5 21.5 %multiply_convert_fusion.2 = bf16[12,512,1024]{2,1,0:T(8,128)(2,1)} fusion(f32[12,512,1024]{2,1,0:T(8,128)} %get-tuple-element.447, f32[12,512,1024]{2,1,0:T(8,128)} %fusion.123, f32[12,512]{1,0:T(8,128)S(1)} %get-tuple-element.448, f32[12,512]{1,0:T(8,128)S(1)} %dynamic-slice_bitcast_fusion.2, pred[512,1024]{1,0:T(8,128)(4,1)S(1)} %broadcast_compare_fusion.5), kind=kLoop, calls=%fused_computation.16.clone.1 | loop fusion | flops 37748736 | bytes 63488000 | tf_op jit(solution)/shard_map/while/body/eval_jaxpr/convert_element_type | solution.py:100
  368.1 8.9 bitcast_add_fusion.4
  376.9 9.4 %bitcast_dynamic-update-slice_fusion.5 = bf16[2,512,12,64]{1,3,2,0:T(8,128)(2,1)} fusion(bf16[2,512,12,64]{1,3,2,0:T(8,128)(2,1)} %get-tuple-element.504, s32[]{:T(128)} %get-tuple-element.501, bf16[12,512,1024]{2,1,0:T(8,128)(2,1)} %multiply_convert_fusion.2, bf16[1024,12,64]{0,2,1:T(8,128)(2,1)S(1)} %get-tuple-element.524), kind=kOutput, calls=%fused_computation.24.clone.1 | convolution fusion | flops 805699584 | bytes 15729152 | tf_op jit(solution)/shard_map/while/body/eval_jaxpr/hqk,khd->qhd/dot_general | solution.py:102
  386.4 13.7 %bitcast_add_fusion.5 = f32[1024,12,64]{0,2,1:T(8,128)} fusion(f32[1024,12,64]{0,2,1:T(8,128)} %get-tuple-element.503, f32[12,512,1024]{2,1,0:T(8,128)} %fusion.123, f32[12,512]{1,0:T(8,128)S(1)} %dynamic-slice_bitcast_fusion.2, pred[512,1024]{1,0:T(8,128)(4,1)S(1)} %broadcast_compare_fusion.5, pred[]{:T(512)S(6)} %compare.3, ...), kind=kOutput, calls=%fused_computation.22.clone.1 | convolution fusion | flops 832045056 | bytes 32792580 | tf_op jit(solution)/shard_map/while/body/eval_jaxpr/hqk,qhd->khd/dot_general | solution.py:90
  401.3 11.4 %fusion.123 = f32[12,512,1024]{2,1,0:T(8,128)} fusion(bf16[1024,12,64]{0,2,1:T(8,128)(2,1)S(1)} %get-tuple-element.524, bf16[1024,12,64]{0,2,1:T(8,128)(2,1)} %get-tuple-element.522, s32[]{:T(128)S(6)} %select_n.64), kind=kOutput, calls=%fused_computation.30.clone.1 | convolution fusion | flops 805306368 | bytes 27525124 | tf_op jit(solution)/shard_map/while/body/eval_jaxpr/qhd,khd->hqk/dot_general | solution.py:47
  415.1 18.1 %multiply_reduce_fusion.9 = (f32[12,512]{1,0:T(8,128)S(1)}, f32[12,512,1024]{2,1,0:T(8,128)}) fusion(f32[12,512,1024]{2,1,0:T(8,128)} %fusion.123, f32[12,512]{1,0:T(8,128)S(1)} %dynamic-slice_bitcast_fusion.2, pred[512,1024]{1,0:T(8,128)(4,1)S(1)} %broadcast_compare_fusion.5, bf16[1024,12,64]{0,2,1:T(8,128)(2,1)} %get-tuple-element.527, ...), kind=kOutput, calls=%fused_computation.17.clone.1 | convolution fusion | flops 836757504 | bytes 53264388 | tf_op jit(solution)/shard_map/while/body/eval_jaxpr/qhd,khd->hqk/dot_general | solution.py:96
  433.1 21.2 %multiply_convert_fusion.2 = bf16[12,512,1024]{2,1,0:T(8,128)(2,1)} fusion(f32[12,512,1024]{2,1,0:T(8,128)} %get-tuple-element.447, f32[12,512,1024]{2,1,0:T(8,128)} %fusion.123, f32[12,512]{1,0:T(8,128)S(1)} %get-tuple-element.448, f32[12,512]{1,0:T(8,128)S(1)} %dynamic-slice_bitcast_fusion.2, pred[512,1024]{1,0:T(8,128)(4,1)S(1)} %broadcast_compare_fusion.5), kind=kLoop, calls=%fused_computation.16.clone.1 | loop fusion | flops 37748736 | bytes 63488000 | tf_op jit(solution)/shard_map/while/body/eval_jaxpr/convert_element_type | solution.py:100
  454.4 9.7 %bitcast_add_fusion.4 = f32[1024,12,64]{0,2,1:T(8,128)} fusion(f32[1024,12,64]{0,2,1:T(8,128)} %get-tuple-element.502, bf16[12,512,1024]{2,1,0:T(8,128)(2,1)} %multiply_convert_fusion.2, pred[]{:T(512)S(6)} %compare.3, bf16[1024,12,64]{0,2,1:T(8,128)(2,1)} %get-tuple-element.522, s32[]{:T(128)S(6)} %select_n.64), kind=kOutput, calls=%fused_computation.23.clone.1 | convolution fusion | flops 807665664 | bytes 19660804 | tf_op jit(solution)/shard_map/while/body/eval_jaxpr/hqk,qhd->khd/dot_general | solution.py:107
  464.1 9.4 %bitcast_dynamic-update-slice_fusion.5 = bf16[2,512,12,64]{1,3,2,0:T(8,128)(2,1)} fusion(bf16[2,512,12,64]{1,3,2,0:T(8,128)(2,1)} %get-tuple-element.504, s32[]{:T(128)} %get-tuple-element.501, bf16[12,512,1024]{2,1,0:T(8,128)(2,1)} %multiply_convert_fusion.2, bf16[1024,12,64]{0,2,1:T(8,128)(2,1)S(1)} %get-tuple-element.524), kind=kOutput, calls=%fused_computation.24.clone.1 | convolution fusion | flops 805699584 | bytes 15729152 | tf_op jit(solution)/shard_map/while/body/eval_jaxpr/hqk,khd->qhd/dot_general | solution.py:102
  473.5 14.5 %bitcast_add_fusion.5 = f32[1024,12,64]{0,2,1:T(8,128)} fusion(f32[1024,12,64]{0,2,1:T(8,128)} %get-tuple-element.503, f32[12,512,1024]{2,1,0:T(8,128)} %fusion.123, f32[12,512]{1,0:T(8,128)S(1)} %dynamic-slice_bitcast_fusion.2, pred[512,1024]{1,0:T(8,128)(4,1)S(1)} %broadcast_compare_fusion.5, pred[]{:T(512)S(6)} %compare.3, ...), kind=kOutput, calls=%fused_computation.22.clone.1 | convolution fusion | flops 832045056 | bytes 32792580 | tf_op jit(solution)/shard_map/while/body/eval_jaxpr/hqk,qhd->khd/dot_general | solution.py:90
  488.2 3.2 copy.79
  492.1 2.7 copy-done.9
  496.2 9.2 convolution_bitcast_fusion
  505.4 8.0 copy.87
  513.5 1.8 copy-done.6
  515.3 10.5 %fusion.60 = f32[768,3072]{1,0:T(8,128)} fusion(bf16[1024,3072]{1,0:T(8,128)(2,1)} %get-tuple-element.322, f32[1024,768]{0,1:T(8,128)S(1)} %copy-done.6, f32[768]{0:T(1024)S(1)} %copy-done.39, f32[768]{0:T(1024)S(1)} %copy-done.28, f32[1024]{0:T(1024)S(1)} %copy-done.30, f32[1024]{0:T(1024)S(1)} %copy-done.24), kind=kOutput, calls=%fused_computation.118 | convolution fusion | flops 4835770368 | bytes 18888704 | tf_op jit(solution)/shard_map/rd,rf->df/dot_general | solution.py:214
  525.9 1.4 copy-done.12
  527.3 10.4 %fusion.68 = f32[3072,768]{1,0:T(8,128)} fusion(bf16[1024,3072]{1,0:T(8,128)(2,1)} %get-tuple-element.316, bf16[1024,768]{0,1:T(8,128)(2,1)S(1)} %copy-done.12), kind=kOutput, calls=%fused_computation.123 | convolution fusion | flops 4831838208 | bytes 17301504 | tf_op jit(solution)/shard_map/rf,rd->fd/dot_general | solution.py:206
  537.8 1.4 copy-done.8
  539.5 41.8 %all-reduce.18 = (f32[768]{0:T(1024)S(1)}, f32[768]{0:T(1024)S(1)}, f32[768]{0:T(1024)S(1)}, f32[768]{0:T(1024)S(1)}, f32[768]{0:T(1024)S(1)}, /*index=5*/f32[30...) all-reduce(f32[768]{0:T(1024)S(1)} %convert_reduce_fusion.4, ...), channel_id=3, replica_groups=mesh['fsdp'=32] {'fsdp'}, use_global_device_ids=true, to_apply=%region_19.20.clone | all-reduce | flops 9216 | bytes 73728
  586.0 9.0 fusion.52
  595.0 3.7 copy.82
  598.7 2.4 copy.81
  601.7 31.5 %reduce-scatter.13.cloned.1.call-done = f32[24,2304]{1,0:T(8,128)} async-done(((f32[768,2304]{1,0:T(8,128)}), f32[24,2304]{1,0:T(8,128)}) %reduce-scatter.13.cloned.1.call-update) | async-done | bytes 221200
  633.1 141.3 %reduce-scatter.9.cloned.1.call-done = f32[24,3072]{1,0:T(8,128)} async-done(((f32[768,3072]{1,0:T(8,128)}), f32[24,3072]{1,0:T(8,128)}) %reduce-scatter.9.cloned.1.call-update) | async-done | bytes 294928 | tf_op jit(solution)/shard_map/reduce_scatter | solution.py:258
  774.5 141.9 %reduce-scatter.11.cloned.1.call-done = f32[96,768]{1,0:T(8,128)} async-done(((f32[3072,768]{1,0:T(8,128)}), f32[96,768]{1,0:T(8,128)}) %reduce-scatter.11.cloned.1.call-update) | async-done | bytes 294928 | tf_op jit(solution)/shard_map/reduce_scatter | solution.py:260
  (188 shorter events, 30.8 us)
Async XLA Ops:
  7.2 60.8 %copy-start.13 = (bf16[1024,768]{1,0:T(8,128)(2,1)S(1)}, bf16[1024,768]{1,0:T(8,128)(2,1)}, u32[]{:S(2)}) copy-start(bf16[1024,768]{1,0:T(8,128)(2,1)} %param.35) | copy-start | bytes 4718596
  7.2 66.7 %all-gather.5.cloned.1.call-start = ((), (), s32[]{:S(2)}) async-start(), calls=%async_computation.4 | async-start | bytes 3649536 | tf_op jit(solution)/shard_map/all_gather | solution.py:152
  7.9 162.7 %all-gather.7.cloned.1.call-start = ((), (), s32[]{:S(2)}) async-start(), calls=%async_computation.5 | async-start | bytes 1216512 | tf_op jit(solution)/shard_map/all_gather | solution.py:155
  8.7 186.6 %all-gather.9.cloned.1.call-start = ((), (), s32[]{:S(2)}) async-start(), calls=%async_computation.6 | async-start | bytes 4866048 | tf_op jit(solution)/shard_map/all_gather | solution.py:178
  9.4 251.1 %all-gather.11.cloned.1.call-start = ((), (), s32[]{:S(2)}) async-start(), calls=%async_computation.7 | async-start | bytes 4866048 | tf_op jit(solution)/shard_map/all_gather | solution.py:180
  10.0 591.7 %reduce-scatter.7.cloned.1.call-start = ((), (), s32[]{:S(2)}) async-start(), calls=%async_computation.8 | async-start | bytes 2433024 | tf_op jit(solution)/shard_map/reduce_scatter | solution.py:254
  61.7 12.2 %copy-start.14 = (bf16[1024,768]{1,0:T(8,128)(2,1)S(1)}, bf16[1024,768]{1,0:T(8,128)(2,1)}, u32[]{:S(2)}) copy-start(bf16[1024,768]{1,0:T(8,128)(2,1)} %param.20) | copy-start | bytes 4718596
  88.6 24.5 %copy-start.16 = (bf16[2,512,12,64]{1,3,2,0:T(8,128)(2,1)S(1)}, bf16[2,512,12,64]{1,3,2,0:T(8,128)(2,1)}, u32[]{:S(2)}) copy-start(bf16[2,512,12,64]{1,3,2,0:T(8,128)(2,1)} %get-tuple-element.462) | copy-start | bytes 4718596 | tf_op jit(solution)/shard_map/while
  100.8 15.4 %copy-start = (f32[12,512,1024]{2,1,0:T(8,128)S(1)}, f32[12,512,1024]{2,1,0:T(8,128)}, u32[]{:S(2)}) copy-start(f32[12,512,1024]{2,1,0:T(8,128)} %get-tuple-element.434) | copy-start | bytes 75497472 | tf_op jit(solution)/shard_map/while
  125.2 1.1 copy-start.17
  128.0 24.6 %copy-start.16 = (bf16[2,512,12,64]{1,3,2,0:T(8,128)(2,1)S(1)}, bf16[2,512,12,64]{1,3,2,0:T(8,128)(2,1)}, u32[]{:S(2)}) copy-start(bf16[2,512,12,64]{1,3,2,0:T(8,128)(2,1)} %get-tuple-element.462) | copy-start | bytes 4718596 | tf_op jit(solution)/shard_map/while
  140.2 15.5 %copy-start = (f32[12,512,1024]{2,1,0:T(8,128)S(1)}, f32[12,512,1024]{2,1,0:T(8,128)}, u32[]{:S(2)}) copy-start(f32[12,512,1024]{2,1,0:T(8,128)} %get-tuple-element.434) | copy-start | bytes 75497472 | tf_op jit(solution)/shard_map/while
  164.7 1.1 copy-start.17
  165.9 4.8 copy-start.18
  165.9 4.8 copy-start.41
  174.0 1.7 copy-start.4
  174.1 21.2 %copy-start.27 = (f32[768]{0:T(1024)S(1)}, f32[768]{0:T(1024)}, u32[]{:S(2)}) copy-start(f32[768]{0:T(1024)} %convert_element_type.108) | copy-start | bytes 9220
  174.1 21.2 %copy-start.36 = (f32[3072]{0:T(1024)S(1)}, f32[3072]{0:T(1024)}, u32[]{:S(2)}) copy-start(f32[3072]{0:T(1024)} %convert_element_type.111) | copy-start | bytes 36868
  174.1 21.2 %copy-start.38 = (f32[768]{0:T(1024)S(1)}, f32[768]{0:T(1024)}, u32[]{:S(2)}) copy-start(f32[768]{0:T(1024)} %convert_element_type.109) | copy-start | bytes 9220
  174.1 127.6 %copy-start.23 = (f32[1024]{0:T(1024)}, f32[1024]{0:T(1024)S(1)}, u32[]{:S(2)}) copy-start(f32[1024]{0:T(1024)S(1)} %broadcast_multiply_fusion.5) | copy-start | bytes 12292
  176.1 125.6 %copy-start.29 = (f32[1024]{0:T(1024)}, f32[1024]{0:T(1024)S(1)}, u32[]{:S(2)}) copy-start(f32[1024]{0:T(1024)S(1)} %add_rsqrt_fusion.1) | copy-start | bytes 12292
  176.1 84.4 %copy-start.40 = (f32[768]{0:T(1024)S(1)}, f32[768]{0:T(1024)}, u32[]{:S(2)}) copy-start(f32[768]{0:T(1024)} %convert_element_type.113) | copy-start | bytes 9220
  269.9 1.4 copy-start.2
  269.9 1.4 copy-start.25
  269.9 1.4 copy-start.26
  270.4 3.1 copy-start.31
  273.4 3.7 copy-start.44
  273.4 18.4 %slice-start = ((s8[4718592]{0:T(1024)(128)(4,1)}), s8[4194304]{0:T(1024)(128)(4,1)S(1)}, s32[]{:S(2)}) async-start(s8[4718592]{0:T(1024)(128)(4,1)} %bitcast.111), calls=%async_computation.12 | async-start | bytes 8388608
  277.1 14.8 %copy-start.11 = (bf16[1024,768]{0,1:T(8,128)(2,1)}, bf16[1024,768]{0,1:T(8,128)(2,1)S(1)}, u32[]{:S(2)}) copy-start(bf16[1024,768]{0,1:T(8,128)(2,1)S(1)} %get-tuple-element.302) | copy-start | bytes 4718596
  277.1 14.8 %copy-start.5 = (f32[1024,768]{0,1:T(8,128)S(1)}, f32[1024,768]{0,1:T(8,128)}, u32[]{:S(2)}) copy-start(f32[1024,768]{0,1:T(8,128)} %copy-done.4) | copy-start | bytes 9437188
  277.1 14.8 %slice-start.1 = ((s8[4718592]{0:T(1024)(128)(4,1)}), s8[524288]{0:T(1024)(128)(4,1)S(1)}, s32[]{:S(2)}) async-start(s8[4718592]{0:T(1024)(128)(4,1)} %bitcast.111), calls=%async_computation.13 | async-start | bytes 1048576
  301.7 3.5 copy-start.19
  303.5 1.8 copy-start.10
  305.2 2.9 copy-start.45
  308.1 325.0 %reduce-scatter.13.cloned.1.call-start = ((), (), s32[]{:S(2)}) async-start(), calls=%async_computation.11 | async-start | bytes 7299072
  488.2 3.6 copy-start.1
  491.8 3.3 copy-start.7
  491.8 3.0 copy-start.9
  492.1 3.0 copy-start.20
  492.1 4.1 copy-start.15
  495.1 1.1 copy-start.22
  513.4 1.9 copy-start.6
  513.4 1.9 copy-start.24
  513.4 1.9 copy-start.28
  513.5 1.9 copy-start.30
  513.5 1.9 copy-start.39
  513.5 261.0 %reduce-scatter.9.cloned.1.call-start = ((), (), s32[]{:S(2)}) async-start(), calls=%async_computation.9 | async-start | bytes 9732096 | tf_op jit(solution)/shard_map/reduce_scatter | solution.py:258
  525.9 1.5 copy-start.12
  525.9 390.5 %reduce-scatter.11.cloned.1.call-start = ((), (), s32[]{:S(2)}) async-start(), calls=%async_computation.10 | async-start | bytes 9732096 | tf_op jit(solution)/shard_map/reduce_scatter | solution.py:260
  537.7 1.5 copy-start.8
  537.7 1.7 copy-start.32
  537.7 1.7 copy-start.33
  537.7 1.7 copy-start.34
  537.7 1.8 copy-start.35
  537.7 1.8 copy-start.37
  537.7 1.8 copy-start.42
  537.8 1.8 copy-start.43
  537.8 48.2 %copy-start.21 = (bf16[1024,12,64]{0,2,1:T(8,128)(2,1)S(1)}, bf16[1024,12,64]{0,2,1:T(8,128)(2,1)}, u32[]{:S(2)}) copy-start(bf16[1024,12,64]{0,2,1:T(8,128)(2,1)} %copy-done.20) | copy-start | bytes 4718596
  595.0 3.8 copy-start.3
Sparse Core Ops, SparseCore 0:
  10.9 62.9 all-gather.4
  76.8 52.9 all-gather.6
  132.7 62.4 all-gather.8
  198.0 62.4 all-gather.10
  308.2 97.9 reduce-scatter.6
  513.6 119.4 reduce-scatter.12
  639.6 134.7 reduce-scatter.8
  781.9 134.3 reduce-scatter.10
where the time goes:
time: 931 us; the launch traced here: 923 us
  waiting for transfers between devices  366 us (39%)
  matrix products  296 us (32%)
  other arithmetic  85.4 us (9%)
  blocking collectives  84.4 us (9%)
  local copies, waits for them, and re-layouts  68.6 us (7%)
  between operations  14.9 us (2%)
    reduce_scatter x1, waiting for transfers between devices, on_device(): lax.psum_scatter(grad_w_down, 'fsdp', scatter_dimension=0, tiled=True)  142 us
    reduce_scatter x1, waiting for transfers between devices, on_device(): lax.psum_scatter(grad_w_up, 'fsdp', scatter_dimension=0, tiled=True)  141 us
    unnamed x2, blocking collectives  84.4 us
    dot_general x4, matrix products, masked_scores(): jnp.einsum('qhd,khd->hqk', query_block, key_rows, preferred_element_type=...  47.3 us
    unnamed x124, local copies, waits for them, and re-layouts  46.1 us
    convert_element_type x2, other arithmetic, one_block(): grad_scores = (probs * (grad_probs - weighted)).astype(jnp.bfloat16)  42.7 us
    dot_general x1, matrix products, on_device(): jnp.dot(first_low, whole_up, preferred_element_type=jnp.float32)  39 us
    dot_general x2, matrix products, one_block(): jnp.einsum('qhd,khd->hqk', grad_block, value_rows, preferred_element_type...  36.3 us
  transfers between devices with their start and end apart: 8, of which 6 were waited for; matrix products, arithmetic and copies ran while one was open for 42% of the time, Pallas kernels for 0%

commit v1 on v0

v1 whole, which is shorter than its diff:
```python
import functools
import math

import jax
import jax.numpy as jnp
from jax import lax
from jax.experimental import pallas as pl
from jax.experimental.pallas import tpu as pltpu
from jax.sharding import PartitionSpec as P

DH = 64
PAIR = 2 * DH
BF = jnp.bfloat16
F32 = jnp.float32
NEG = -1e30
EPSILON = 1e-05
ROOT_HALF = 0.7071067811865476
INV_ROOT_TWO_PI = 0.3989422804014327
LAST_LAST = (((1,), (1,)), ((), ()))
VMEM_BYTES = 56 * 2**20


def norm_forward(values_in, gain, shift):
    centre = jnp.mean(values_in, axis=-1, keepdims=True)
    centered = values_in - centre
    spread = jnp.mean(centered * centered, axis=-1, keepdims=True)
    rstd_rows = lax.rsqrt(spread + EPSILON)
    normed = centered * rstd_rows
    return (normed * gain + shift, normed, rstd_rows)


def norm_backward(upstream, normed, rstd_rows, gain):
    scaled = upstream * gain
    plain_mean = jnp.mean(scaled, axis=-1, keepdims=True)
    cross_mean = jnp.mean(scaled * normed, axis=-1, keepdims=True)
    grad_in = rstd_rows * (scaled - plain_mean - normed * cross_mean)
    return (grad_in, jnp.sum(upstream * normed, axis=0), jnp.sum(upstream, axis=0))


def gelu_slope(inner):
    normal_cdf = 0.5 * (1.0 + lax.erf(inner * ROOT_HALF))
    return normal_cdf + inner * jnp.exp(-0.5 * inner * inner) * INV_ROOT_TWO_PI


def dot_last(a, b):
    return lax.dot_general(a, b, LAST_LAST, preferred_element_type=F32)


def dot(a, b):
    return jnp.dot(a, b, preferred_element_type=F32)


def segment_at(position, bounds_ref):
    segment = jnp.zeros(position.shape, jnp.int32)
    for index in range(bounds_ref.shape[0]):
        segment += (position >= bounds_ref[index]).astype(jnp.int32)
    return segment


def attention_forward_kernel(bounds_ref, q_ref, k_ref, v_ref, mixed_ref, logsum_ref, *, span, scale):
    rows = q_ref.shape[0]
    first_head = lax.broadcasted_iota(jnp.int32, (1, PAIR), 1) < DH
    key_segment = segment_at(lax.broadcasted_iota(jnp.int32, (1, rows), 1), bounds_ref)
    keys = k_ref[...]
    values = v_ref[...]
    for block in range(rows // span):
        here = pl.ds(block * span, span)
        queries = q_ref[here, :] * jnp.asarray(scale, BF)
        row = lax.broadcasted_iota(jnp.int32, (span, 1), 0) + block * span
        same = segment_at(row, bounds_ref) == key_segment
        mixed = []
        logsum = []
        for head in range(2):
            mine = first_head if head == 0 else jnp.logical_not(first_head)
            scores = dot_last(jnp.where(mine, queries, jnp.zeros_like(queries)), keys)
            scores = jnp.where(same, scores, NEG)
            highest = jnp.max(scores, axis=1, keepdims=True)
            exps = jnp.exp(scores - highest)
            total = jnp.sum(exps, axis=1, keepdims=True)
            mixed.append(dot(exps.astype(BF), values) * (1.0 / total))
            logsum.append(highest + jnp.log(total))
        mixed_ref[here, :] = jnp.where(first_head, mixed[0], mixed[1]).astype(BF)
        turned = jnp.transpose(jnp.where(first_head, logsum[0], logsum[1]))
        logsum_ref[0, 0:1, here] = turned[0:1]
        logsum_ref[0, 1:2, here] = turned[DH : DH + 1]


def pair_spec(rows, offset):
    return pl.BlockSpec((rows, PAIR), lambda pair, bounds: (0, offset + pair))


def attention_forward(bounds, stacked, span=512):
    rows, width = stacked.shape[0], stacked.shape[1] // 3
    pairs = width // PAIR
    return pl.pallas_call(
        functools.partial(attention_forward_kernel, span=span, scale=1.0 / math.sqrt(DH)),
        grid_spec=pltpu.PrefetchScalarGridSpec(
            num_scalar_prefetch=1,
            grid=(pairs,),
            in_specs=[pair_spec(rows, 0), pair_spec(rows, pairs), pair_spec(rows, 2 * pairs)],
            out_specs=[
                pair_spec(rows, 0),
                pl.BlockSpec((1, 8, rows), lambda pair, bounds: (pair, 0, 0)),
            ],
        ),
        out_shape=[
            jax.ShapeDtypeStruct((rows, width), BF),
            jax.ShapeDtypeStruct((pairs, 8, rows), F32),
        ],
        compiler_params=pltpu.CompilerParams(vmem_limit_bytes=VMEM_BYTES),
        cost_estimate=pl.CostEstimate(
            flops=4 * rows * rows * width * 4, bytes_accessed=8 * rows * width, transcendentals=0
        ),
        name="attention_forward",
    )(bounds, stacked, stacked, stacked)


def attention_backward_kernel(
    bounds_ref, q_ref, k_ref, v_ref, mixed_ref, grad_ref, logsum_ref, dq_ref, dk_ref, dv_ref, dk_sum, dv_sum, *, span, scale
):
    rows = q_ref.shape[0]
    first_head = lax.broadcasted_iota(jnp.int32, (1, PAIR), 1) < DH
    key_segment = segment_at(lax.broadcasted_iota(jnp.int32, (rows, 1), 0), bounds_ref)
    keys = k_ref[...]
    values = v_ref[...]
    keys_turned = jnp.transpose(keys)
    picks = (
        lax.broadcasted_iota(jnp.int32, (8, PAIR), 1) // DH
        == lax.broadcasted_iota(jnp.int32, (8, PAIR), 0)
    ).astype(F32)
    for block in range(rows // span):
        here = pl.ds(block * span, span)
        queries = q_ref[here, :]
        grads = grad_ref[here, :]
        weighted = lax.dot_general(
            picks,
            grads.astype(F32) * mixed_ref[here, :].astype(F32),
            LAST_LAST,
            preferred_element_type=F32,
            precision=lax.Precision.HIGHEST,
        )
        column = lax.broadcasted_iota(jnp.int32, (1, span), 1) + block * span
        same = key_segment == segment_at(column, bounds_ref)
        all_probs, all_scores, all_grads, all_queries, grad_queries = [], [], [], [], []
        for head in range(2):
            mine = first_head if head == 0 else jnp.logical_not(first_head)
            my_queries = jnp.where(mine, queries, jnp.zeros_like(queries)) * jnp.asarray(scale, BF)
            my_grads = jnp.where(mine, grads, jnp.zeros_like(grads))
            scores = dot_last(keys, my_queries) - logsum_ref[0, head : head + 1, here]
            probs = jnp.exp(jnp.where(same, scores, NEG))
            grad_probs = dot_last(values, my_grads)
            grad_scores = (probs * (grad_probs - weighted[head : head + 1])).astype(BF)
            all_probs.append(probs.astype(BF))
            all_scores.append(grad_scores)
            all_grads.append(my_grads)
            all_queries.append(my_queries)
            grad_queries.append(dot(keys_turned[DH * head : DH * (head + 1)], grad_scores))
        turned = jnp.concatenate(grad_queries, axis=0) * scale
        dq_ref[here, :] = jnp.transpose(turned).astype(BF)
        dv = dot(jnp.concatenate(all_probs, axis=1), jnp.concatenate(all_grads, axis=0))
        dk = dot(jnp.concatenate(all_scores, axis=1), jnp.concatenate(all_queries, axis=0))
        if block == 0:
            dv_sum[...] = dv
            dk_sum[...] = dk
        else:
            dv_sum[...] += dv
            dk_sum[...] += dk
    dk_ref[...] = dk_sum[...].astype(BF)
    dv_ref[...] = dv_sum[...].astype(BF)


def attention_backward(bounds, stacked, mixed, grad_mixed, logsum, span=256):
    rows, width = mixed.shape
    pairs = width // PAIR
    return pl.pallas_call(
        functools.partial(attention_backward_kernel, span=span, scale=1.0 / math.sqrt(DH)),
        grid_spec=pltpu.PrefetchScalarGridSpec(
            num_scalar_prefetch=1,
            grid=(pairs,),
            in_specs=[
                pair_spec(rows, 0),
                pair_spec(rows, pairs),
                pair_spec(rows, 2 * pairs),
                pair_spec(rows, 0),
                pair_spec(rows, 0),
                pl.BlockSpec((1, 8, rows), lambda pair, bounds: (pair, 0, 0)),
            ],
            out_specs=[pair_spec(rows, 0), pair_spec(rows, 0), pair_spec(rows, 0)],
            scratch_shapes=[pltpu.VMEM((rows, PAIR), F32), pltpu.VMEM((rows, PAIR), F32)],
        ),
        out_shape=[jax.ShapeDtypeStruct((rows, width), BF)] * 3,
        compiler_params=pltpu.CompilerParams(vmem_limit_bytes=VMEM_BYTES),
        cost_estimate=pl.CostEstimate(
            flops=10 * rows * rows * width * 4, bytes_accessed=16 * rows * width, transcendentals=0
        ),
        name="attention_backward",
    )(bounds, stacked, stacked, stacked, mixed, grad_mixed, logsum)


def on_device(
    hidden,
    lengths,
    w_qkv,
    bias_q,
    bias_v,
    w_out,
    bias_out,
    norm1_gain,
    norm1_bias,
    w_up,
    bias_up,
    w_down,
    bias_down,
    norm2_gain,
    norm2_bias,
    cotangent,
):
    count_rows, width = hidden.shape
    hidden_units = w_up.shape[1]
    n = lax.axis_size("fsdp")
    part = width // n
    inner_part = hidden_units // n
    wide = hidden_units // width
    bounds = jnp.cumsum(lengths)
    present = (jnp.arange(count_rows, dtype=jnp.int32) < bounds[-1]).astype(F32)[:, None]

    vectors = (bias_q, bias_v, bias_out, norm1_gain, norm1_bias, bias_up, bias_down, norm2_gain, norm2_bias)
    sizes = [vector.shape[0] for vector in vectors]
    starts = [sum(sizes[:i]) for i in range(len(sizes))]
    whole_qkv = lax.all_gather(w_qkv, "fsdp", axis=0, tiled=True)
    whole_vectors = lax.all_gather(jnp.concatenate(vectors)[None], "fsdp", axis=0, tiled=True)
    (
        whole_bias_q,
        whole_bias_v,
        whole_bias_out,
        whole_gain_one,
        whole_shift_one,
        whole_bias_up,
        whole_bias_down,
        whole_gain_two,
        whole_shift_two,
    ) = (
        whole_vectors[:, start : start + size].reshape(n * size).astype(F32)
        for start, size in zip(starts, sizes)
    )
    packed = jnp.concatenate(
        [w_out]
        + [w_up[:, width * i : width * (i + 1)] for i in range(wide)]
        + [w_down],
        axis=0,
    )
    gathered = lax.all_gather(packed, "fsdp", axis=0, tiled=True).reshape(n, -1, width)
    whole_out = gathered[:, :part].reshape(width, width)
    whole_up = (
        gathered[:, part : part * (1 + wide)]
        .reshape(n, wide, part, width)
        .transpose(0, 2, 1, 3)
        .reshape(width, hidden_units)
    )
    whole_down = gathered[:, part * (1 + wide) :].reshape(hidden_units, width)

    projected = jnp.dot(hidden, whole_qkv, preferred_element_type=F32)
    whole_bias = jnp.concatenate([whole_bias_q, jnp.zeros_like(whole_bias_q), whole_bias_v])
    stacked = (projected + whole_bias).astype(BF)
    mixed, logsum = attention_forward(bounds, stacked)
    branch = jnp.dot(mixed, whole_out, preferred_element_type=F32) + whole_bias_out
    first, normed_one, rstd_one = norm_forward(
        hidden.astype(F32) + branch, whole_gain_one, whole_shift_one
    )
    first_low = first.astype(BF)
    inner = jnp.dot(first_low, whole_up, preferred_element_type=F32) + whole_bias_up
    activated = jax.nn.gelu(inner, approximate=False).astype(BF)
    second = jnp.dot(activated, whole_down, preferred_element_type=F32) + whole_bias_down
    result, normed_two, rstd_two = norm_forward(first + second, whole_gain_two, whole_shift_two)
    output = result * present
    upstream = cotangent.astype(F32) * present
    grad_second, grad_gain_two, grad_shift_two = norm_backward(
        upstream, normed_two, rstd_two, whole_gain_two
    )
    grad_branch_two = grad_second.astype(BF)
    grad_w_down = jnp.einsum("rf,rd->fd", activated, grad_branch_two, preferred_element_type=F32)
    grad_bias_down = jnp.sum(grad_branch_two.astype(F32), axis=0)
    grad_activated = jnp.einsum(
        "rd,fd->rf", grad_branch_two, whole_down, preferred_element_type=F32
    )
    grad_inner = (grad_activated * gelu_slope(inner)).astype(BF)
    grad_w_up = jnp.einsum("rd,rf->df", first_low, grad_inner, preferred_element_type=F32)
    grad_bias_up = jnp.sum(grad_inner.astype(F32), axis=0)
    grad_first = grad_second + jnp.einsum(
        "rf,df->rd", grad_inner, whole_up, preferred_element_type=F32
    )
    grad_sum_one, grad_gain_one, grad_shift_one = norm_backward(
        grad_first, normed_one, rstd_one, whole_gain_one
    )
    grad_branch_one = grad_sum_one.astype(BF)
    grad_w_out = jnp.einsum("rd,re->de", mixed, grad_branch_one, preferred_element_type=F32)
    grad_bias_out = jnp.sum(grad_branch_one.astype(F32), axis=0)
    grad_mixed = jnp.einsum(
        "re,de->rd", grad_branch_one, whole_out, preferred_element_type=F32
    ).astype(BF)
    grads_packed = jnp.concatenate(
        [
            grad_w_out.astype(BF).reshape(n, part, width),
            grad_w_up.astype(BF)
            .reshape(n, part, wide, width)
            .transpose(0, 2, 1, 3)
            .reshape(n, wide * part, width),
            grad_w_down.astype(BF).reshape(n, inner_part, width),
        ],
        axis=1,
    )
    summed = lax.psum_scatter(
        grads_packed.reshape(-1, width), "fsdp", scatter_dimension=0, tiled=True
    ).astype(F32)
    my_out = summed[:part]
    my_up = (
        summed[part : part * (1 + wide)]
        .reshape(wide, part, width)
        .transpose(1, 0, 2)
        .reshape(part, hidden_units)
    )
    my_down = summed[part * (1 + wide) :]

    grad_stack = jnp.concatenate(
        attention_backward(bounds, stacked, mixed, grad_mixed, logsum), axis=1
    )
    grad_w_qkv = jnp.einsum("rd,re->de", hidden, grad_stack, preferred_element_type=F32)
    stack_sums = jnp.sum(grad_stack.astype(F32), axis=0)
    grad_hidden = grad_sum_one + jnp.einsum(
        "re,de->rd", grad_stack, whole_qkv, preferred_element_type=F32
    )
    vector_grads = jnp.concatenate(
        [
            grad.reshape(n, -1)
            for grad in (
                stack_sums[:width],
                stack_sums[2 * width :],
                grad_bias_out,
                grad_gain_one,
                grad_shift_one,
                grad_bias_up,
                grad_bias_down,
                grad_gain_two,
                grad_shift_two,
            )
        ],
        axis=1,
    )
    my_qkv = lax.psum_scatter(
        grad_w_qkv.astype(BF), "fsdp", scatter_dimension=0, tiled=True
    ).astype(F32)
    every_vector = lax.psum(vector_grads, "fsdp")
    my_vectors = lax.dynamic_index_in_dim(every_vector, lax.axis_index("fsdp"), 0, keepdims=False)
    (my_bias_q, my_bias_v, my_bias_out, my_gain_one, my_shift_one, my_bias_up, my_bias_down, my_gain_two, my_shift_two) = (
        my_vectors[start : start + size] for start, size in zip(starts, sizes)
    )
    return (
        output,
        grad_hidden,
        my_qkv,
        my_bias_q,
        my_bias_v,
        my_out,
        my_bias_out,
        my_gain_one,
        my_shift_one,
        my_up,
        my_bias_up,
        my_down,
        my_bias_down,
        my_gain_two,
        my_shift_two,
    )


def solution(mesh):
    rows = P("fsdp", None)
    flat = P("fsdp")
    weights = (rows, flat, flat, rows, flat, flat, flat, rows, flat, rows, flat, flat, flat)
    return jax.shard_map(
        on_device,
        mesh=mesh,
        in_specs=(rows, flat) + weights + (rows,),
        out_specs=(rows, rows) + weights,
        check_vma=False,
    )
```

time: 931 us -> 576 us (0.62)
  matrix products: 296 us -> 110 us
  waiting for transfers between devices: 366 us -> 209 us
  other arithmetic: 85.4 us -> 16.7 us
  Pallas kernels: 0 us -> 66.9 us
    dot_general x25 -> x11, matrix products: 286 us -> 105 us  [the longest x1 36.4 us: on_device(): jnp.dot(first_low, whole_up, preferred_element_type=F32) + whole_bias_up]
    reduce_scatter x3 -> x1, waiting for transfers between devices: 283 us -> 145 us  [on_device(): lax.psum_scatter(grads_packed.reshape(-1, width), 'fsdp', scatter_dimensi...]
    pallas_call x0 -> x2, Pallas kernels: none -> 66.9 us  [the longest x1 41.8 us: attention_backward(): pl.pallas_call(functools.partial(attention_backward_kernel, span=span, sc...]
    convert_element_type x13 -> x3, other arithmetic: 49.3 us -> 0.81 us  [the longest x1 0.65 us: on_device(): (jnp.arange(count_rows, dtype=jnp.int32) < bounds[-1]).astype(F32)[:, None]]
    unnamed x2 -> x1, blocking collectives: 84.4 us -> 42.6 us
    psum x0 -> x1, blocking collectives: none -> 39.9 us  [on_device(): every_vector = lax.psum(vector_grads, 'fsdp')]
    unnamed x9 -> x5, waiting for transfers between devices: 34.1 us -> 3.44 us
    reduce_sum x7 -> x3, other arithmetic: 30.7 us -> 8.44 us  [the longest x1 3.67 us: on_device(): grad_bias_down = jnp.sum(grad_branch_two.astype(F32), axis=0)]
  transfers between devices with their start and end apart: 8 -> 4, of which waited for: 6 -> 4; matrix products, arithmetic and copies ran while one was open for 42% -> 15% of each run, Pallas kernels for 0% -> 4%
where the time goes in v1:
time: 576 us; the launch traced here: 568 us
  waiting for transfers between devices  209 us (36%)
  matrix products  110 us (19%)
  blocking collectives  82.5 us (14%)
  local copies, waits for them, and re-layouts  67.8 us (12%)
  Pallas kernels  66.9 us (12%)
  other arithmetic  16.7 us (3%)
  between operations  14.5 us (3%)
    reduce_scatter x1, waiting for transfers between devices, on_device(): lax.psum_scatter(grads_packed.reshape(-1, width), 'fsdp', scatter_dimensi...  145 us
    all_gather x1, waiting for transfers between devices, on_device(): lax.all_gather(packed, 'fsdp', axis=0, tiled=True).reshape(n, -1, width)  55.8 us
    unnamed x1, blocking collectives  42.6 us
    pallas_call x1, Pallas kernels, attention_backward(): pl.pallas_call(functools.partial(attention_backward_kernel, span=span, sc...  41.8 us
    psum x1, blocking collectives, on_device(): every_vector = lax.psum(vector_grads, 'fsdp')  39.9 us
    dot_general x1, matrix products, on_device(): jnp.dot(first_low, whole_up, preferred_element_type=F32) + whole_bias_up  36.4 us
    unnamed x79, local copies, waits for them, and re-layouts  29.6 us
    pallas_call x1, Pallas kernels, attention_forward(): pl.pallas_call(functools.partial(attention_forward_kernel, span=span, sca...  25.2 us
  transfers between devices with their start and end apart: 4, of which 4 were waited for; matrix products, arithmetic and copies ran while one was open for 15% of the time, Pallas kernels for 4%

profile of v1, /device:TPU:0, one launch (start us, length us, event | category | flops | bytes accessed | tf_op | source)
XLA Modules:
  0.0 568.2 jit_solution(17284014369883074631)
XLA Ops:
  7.2 0.7 all-gather.4.cloned.1.call-update
  8.0 0.8 constant_dynamic-update-slice_fusion.1
  8.8 0.8 slice_dynamic-update-slice_fusion.3
  9.5 0.8 slice_dynamic-update-slice_fusion.2
  10.3 0.8 slice_dynamic-update-slice_fusion.1
  11.1 0.8 slice_dynamic-update-slice_fusion
  11.8 0.9 constant_dynamic-update-slice_fusion
  12.8 0.7 copy-done.13
  13.6 6.1 %concatenate.18 = bf16[288]{0:T(512)(128)(2,1)S(1)} concatenate(bf16[24]{0:T(256)(128)(2,1)} %param.19, bf16[24]{0:T(256)(128)(2,1)} %param.20, bf16[24]{0:T(256)(128)(2,1)} %param.22, bf16[24]{0:T(256)(128)(2,1)} %param.23, bf16[24]{0:T(256)(128)(2,1)} %param.24, bf16[96]{0:T(256)(128)(2,1)} %param.26, bf16[24]{0:T(256)(128)(2,1)} %param.28, bf16[24]{0:T(256)(128)(2,1)} %param.29, ...), dimensions={0} | concatenate | bytes 1152 | tf_op jit(solution)/shard_map/concatenate | solution.py:231
  19.7 0.2 dynamic-update-slice
  19.9 42.6 %all-reduce = bf16[9216]{0:T(1024)(128)(2,1)S(1)} all-reduce(bf16[9216]{0:T(1024)(128)(2,1)S(1)} %dynamic-update-slice), channel_id=2, replica_groups=mesh['fsdp'=32] {'fsdp'}, use_global_device_ids=true, to_apply=%add | all-reduce | flops 9216 | bytes 36864
  63.0 2.6 copy.61
  66.3 0.6 slice.153
  66.9 0.7 copy.64
  67.7 0.7 fusion.22
  68.4 5.7 all-gather.4.cloned.1.call-done
  74.1 8.5 %add_convert_fusion.q_ref.k_ref.v_ref = bf16[1024,2304]{1,0:T(8,128)(2,1)} fusion(bf16[1024,768]{1,0:T(8,128)(2,1)} %param.16, bf16[768,2304]{1,0:T(8,128)(2,1)} %all-gather.4.cloned.1.call-done, f32[2304]{0:T(1024)S(1)} %pad_maximum_fusion.1), kind=kOutput, calls=%fused_computation.29 | convolution fusion | flops 3628597248 | bytes 9839616 | tf_op jit(solution)/shard_map/dot_general | solution.py:262
  82.6 25.2 %attention_forward.1 = (bf16[1024,768]{1,0:T(8,128)(2,1)}, f32[6,8,1024]{2,1,0:T(8,128)}) custom-call(s32[2]{0:T(128)} %bitcast.83, bf16[1024,2304]{1,0:T(8,128)(2,1)} %add_convert_fusion.q_ref.k_ref.v_ref, bf16[1024,2304]{1,0:T(8,128)(2,1)} %add_convert_fusion.q_ref.k_ref.v_ref, bf16[1024,2304]{1,0:T(8,128)(2,1)} %add_convert_fusion.q_ref.k_ref.v_ref), custom_call_target="tpu_custom_call" | custom-call | flops 12884901888 | bytes 6291456 | tf_op jit(solution)/shard_map/attention_forward/pallas_call | solution.py:95
  107.7 55.8 %all-gather.6.cloned.1.call-done = bf16[6912,768]{1,0:T(8,128)(2,1)} async-done(((bf16[216,768]{1,0:T(8,128)(2,1)}), bf16[6912,768]{1,0:T(8,128)(2,1)}) %all-gather.6.cloned.1.call-update) | async-done | bytes 10616848 | tf_op jit(solution)/shard_map/all_gather | solution.py:252
  163.5 1.4 slice.179
  164.9 6.7 %fusion.29 = (bf16[32,96,768]{2,1,0:T(8,128)(2,1)}, bf16[32,96,768]{2,1,0:T(8,128)(2,1)S(1)}) fusion(bf16[32,216,768]{2,1,0:T(8,128)(2,1)} %bitcast.69), kind=kLoop, calls=%fused_computation.102 | loop fusion | bytes 18874368 | tf_op jit(solution)/shard_map/slice | solution.py:260
  171.6 3.1 fusion.32
  174.7 0.4 multiply_reduce_fusion.5
  175.1 2.3 copy.62
  177.5 1.1 copy.78
  178.5 36.4 %fusion.2 = (bf16[1024,3072]{1,0:T(8,128)(2,1)}, f32[1024,3072]{1,0:T(8,128)}) fusion(f32[3072]{0:T(1024)S(1)} %reshape.262, bf16[768,3072]{1,0:T(8,128)(2,1)S(1)} %bitcast.70, f32[1024,768]{0,1:T(8,128)S(1)} %get-tuple-element.121, f32[768]{0:T(1024)S(1)} %reshape.261, f32[768]{0:T(1024)S(1)} %reshape.260, f32[1024]{0:T(1024)S(1)} %add_rsqrt_fusion.1, ...), kind=kOutput, calls=%fused_computation.4 | convolution fusion | flops 5043388416 | bytes 26765312 | tf_op jit(solution)/shard_map/dot_general | solution.py:271
  215.0 9.0 %fusion.33 = (f32[1024]{0:T(1024)S(1)}, f32[1024,768]{0,1:T(8,128)S(1)}) fusion(f32[768]{0:T(1024)S(1)} %reshape.263, bf16[1024,3072]{1,0:T(8,128)(2,1)} %get-tuple-element.122, bf16[3072,768]{1,0:T(8,128)(2,1)} %bitcast.72, f32[768]{0:T(1024)S(1)} %reshape.261, f32[768]{0:T(1024)S(1)} %reshape.260, f32[1024]{0:T(1024)S(1)} %add_rsqrt_fusion.1, ...), kind=kOutput, calls=%fused_computation.106 | convolution fusion | flops 4837342208 | bytes 17323008 | tf_op jit(solution)/shard_map/dot_general | solution.py:273
  224.0 0.4 multiply_reduce_fusion.4
  224.4 1.5 multiply_reduce_fusion
  225.9 3.7 convert_reduce_fusion.2
  229.5 12.9 %convert_reduce_fusion = (f32[3072]{0:T(1024)}, bf16[1024,3072]{1,0:T(8,128)(2,1)S(1)}) fusion(f32[1024,3072]{1,0:T(8,128)} %get-tuple-element.123, f32[3072]{0:T(1024)S(1)} %reshape.262, bf16[1024,768]{0,1:T(8,128)(2,1)S(1)} %get-tuple-element.94, bf16[3072,768]{1,0:T(8,128)(2,1)S(1)} %bitcast.75), kind=kOutput, calls=%fused_computation.11 | convolution fusion | flops 4872729600 | bytes 25190400 | tf_op jit(solution)/shard_map/rd,fd->rf/dot_general | solution.py:283
  242.4 7.5 %multiply_reduce_fusion.1 = (f32[768]{0:T(1024)}, f32[1024]{0:T(1024)S(1)}, f32[1024]{0:T(1024)S(1)}, f32[768]{0:T(1024)}, f32[1024,768]{0,1:T(8,128)S(1)}) fusion(f32[1024,768]{0,1:T(8,128)S(1)} %get-tuple-element.121, f32[1024]{0:T(1024)S(1)} %add_rsqrt_fusion.1, f32[1024]{0:T(1024)S(1)} %broadcast_multiply_fusion.5, f32[768]{0:T(1024)S(1)} %reshape.260, ...), kind=kOutput, calls=%fused_computation.36 | convolution fusion | flops 4846776320 | bytes 22069248 | tf_op jit(solution)/shard_map/rf,df->rd/dot_general | solution.py:289
  250.0 1.7 convert_reduce_fusion.3
  251.7 2.6 convolution_convert_fusion.3.grad_ref
  254.3 41.8 %attention_backward.1 = (bf16[1024,768]{1,0:T(8,128)(2,1)}, bf16[1024,768]{1,0:T(8,128)(2,1)}, bf16[1024,768]{1,0:T(8,128)(2,1)}) custom-call(s32[2]{0:T(128)} %bitcast.84, bf16[1024,2304]{1,0:T(8,128)(2,1)} %add_convert_fusion.q_ref.k_ref.v_ref, bf16[1024,2304]{1,0:T(8,128)(2,1)} %add_convert_fusion.q_ref.k_ref.v_ref, ...), custom_call_target="tpu_custom_call" | custom-call | flops 32212254720 | bytes 12582912 | tf_op jit(solution)/shard_map/attention_backward/pallas_call | solution.py:175
  296.1 1.7 constant_dynamic-update-slice_fusion.4
  298.1 0.4 copy-done.11
  298.6 2.1 copy-done.3
  300.7 4.2 fusion.16
  304.9 4.1 copy.75
  309.1 1.8 copy-done.2
  310.9 10.0 %convolution_convert_fusion.1 = bf16[768,3072]{1,0:T(8,128)(2,1)} fusion(bf16[1024,3072]{1,0:T(8,128)(2,1)} %copy-done.26, f32[1024,768]{0,1:T(8,128)S(1)} %copy-done.2, f32[768]{0:T(1024)S(1)} %copy-done.20, f32[768]{0:T(1024)S(1)} %reshape.260, f32[1024]{0:T(1024)S(1)} %copy-done.17, f32[1024]{0:T(1024)S(1)} %broadcast_multiply_fusion.5), kind=kOutput, calls=%fused_computation.31 | convolution fusion | flops 4838129664 | bytes 14170112 | tf_op jit(solution)/shard_map/rd,rf->df/dot_general | solution.py:287
  320.9 9.8 %reshape.251 = bf16[32,24,4,768]{3,2,1,0:T(4,128)(2,1)} reshape(bf16[768,3072]{1,0:T(8,128)(2,1)} %convolution_convert_fusion.1) | data formatting | bytes 9437184 | tf_op jit(solution)/shard_map/reshape | solution.py:305
  330.7 3.5 copy.67
  334.2 0.5 copy-done.25
  334.7 1.5 convolution_convert_fusion.4
  336.2 0.5 copy-done.7
  336.7 0.7 slice-done.3
  337.4 5.5 convolution_convert_fusion
  342.9 5.0 pad_maximum_fusion
  348.0 3.0 convert_reduce_fusion.1
  351.9 9.0 %convolution_add_fusion.1 = f32[1024,768]{0,1:T(8,128)} fusion(f32[1024,768]{0,1:T(8,128)S(1)} %copy-done.5, bf16[1024,2304]{1,0:T(8,128)(2,1)} %copy-done.3, bf16[768,2304]{1,0:T(8,128)(2,1)} %all-gather.4.cloned.1.call-done), kind=kOutput, calls=%fused_computation.57 | convolution fusion | flops 3624665088 | bytes 14548992 | tf_op jit(solution)/shard_map/re,de->rd/dot_general | solution.py:329
  360.9 3.7 copy.70
  364.6 2.4 copy.69
  367.0 39.9 %psum.7 = f32[32,288]{1,0:T(8,128)S(1)} all-reduce(f32[32,288]{1,0:T(8,128)S(1)} %concatenate.22), channel_id=1, replica_groups=mesh['fsdp'=32] {'fsdp'}, use_global_device_ids=true, to_apply=%region_18.19 | all-reduce | flops 9216 | bytes 73728 | tf_op jit(solution)/shard_map/psum | solution.py:352
  406.9 0.6 dynamic-slice_bitcast_fusion.3
  407.5 0.6 dynamic-slice_bitcast_fusion
  408.1 2.7 reduce-scatter.7.cloned.1.call-done
  410.9 1.3 copy.76
  412.1 0.9 copy.71
  413.0 144.6 %reduce-scatter.5.cloned.1.call-done = bf16[216,768]{1,0:T(8,128)(2,1)} async-done(((bf16[6912,768]{1,0:T(8,128)(2,1)}), bf16[216,768]{1,0:T(8,128)(2,1)}) %reduce-scatter.5.cloned.1.call-update) | async-done | bytes 331792 | tf_op jit(solution)/shard_map/reduce_scatter | solution.py:312
  557.6 1.7 fusion.30
  559.4 0.7 copy.77
  560.1 1.4 slice.191
  (100 shorter events, 2.7 us)
Async XLA Ops:
  7.2 58.9 %copy-start.23 = (s32[2]{0:T(128)S(1)}, s32[2]{0:T(128)}, u32[]{:S(2)}) copy-start(s32[2]{0:T(128)} %param.17) | copy-start | bytes 28
  7.2 59.7 %copy-start.8 = (bf16[1024,768]{1,0:T(8,128)(2,1)S(1)}, bf16[1024,768]{1,0:T(8,128)(2,1)}, u32[]{:S(2)}) copy-start(bf16[1024,768]{1,0:T(8,128)(2,1)} %param.31) | copy-start | bytes 4718596
  7.2 66.9 %all-gather.4.cloned.1.call-start = ((), (), s32[]{:S(2)}) async-start(), calls=%async_computation.2 | async-start | bytes 3649536 | tf_op jit(solution)/shard_map/all_gather | solution.py:230
  7.9 155.6 %all-gather.6.cloned.1.call-start = ((), (), s32[]{:S(2)}) async-start(), calls=%async_computation.3 | async-start | bytes 10948608 | tf_op jit(solution)/shard_map/all_gather | solution.py:252
  12.8 0.7 copy-start.13
  13.5 397.3 %reduce-scatter.7.cloned.1.call-start = ((), (), s32[]{:S(2)}) async-start(), calls=%async_computation.5 | async-start | bytes 3649536
  65.8 149.2 %copy-start.19 = (f32[768]{0:T(1024)}, f32[768]{0:T(1024)S(1)}, u32[]{:S(2)}) copy-start(f32[768]{0:T(1024)S(1)} %reshape.261) | copy-start | bytes 9220
  66.3 16.2 %copy-start.24 = (s32[2,1]{0,1:T(1,128)}, s32[2,1]{0,1:T(1,128)S(1)}, u32[]{:S(2)}) copy-start(s32[2,1]{0,1:T(1,128)S(1)} %reduce-window.4) | copy-start | bytes 28
  164.8 6.8 %copy-start.10 = (bf16[1024,768]{0,1:T(8,128)(2,1)S(1)}, bf16[1024,768]{0,1:T(8,128)(2,1)}, u32[]{:S(2)}) copy-start(bf16[1024,768]{0,1:T(8,128)(2,1)} %copy.61) | copy-start | bytes 4718596
  174.7 75.3 %copy-start.1 = (f32[1024,768]{0,1:T(8,128)}, f32[1024,768]{0,1:T(8,128)S(1)}, u32[]{:S(2)}) copy-start(f32[1024,768]{0,1:T(8,128)S(1)} %get-tuple-element.121) | copy-start | bytes 9437188
  175.1 74.9 %copy-start.16 = (f32[1024]{0:T(1024)}, f32[1024]{0:T(1024)S(1)}, u32[]{:S(2)}) copy-start(f32[1024]{0:T(1024)S(1)} %add_rsqrt_fusion.1) | copy-start | bytes 12292
  224.4 5.2 slice-start
  225.8 3.7 slice-start.1
  229.5 12.9 %copy-start.6 = (bf16[1024,768]{0,1:T(8,128)(2,1)}, bf16[1024,768]{0,1:T(8,128)(2,1)S(1)}, u32[]{:S(2)}) copy-start(bf16[1024,768]{0,1:T(8,128)(2,1)S(1)} %get-tuple-element.94) | copy-start | bytes 4718596
  242.4 7.5 %copy-start.26 = (bf16[1024,3072]{1,0:T(8,128)(2,1)}, bf16[1024,3072]{1,0:T(8,128)(2,1)S(1)}, u32[]{:S(2)}) copy-start(bf16[1024,3072]{1,0:T(8,128)(2,1)S(1)} %get-tuple-element.128) | copy-start | bytes 18874372
  251.7 2.6 copy-start.4
  296.1 1.9 copy-start.12
  296.1 2.4 copy-start.11
  297.8 2.9 copy-start.9
  298.6 2.2 copy-start.3
  309.0 1.9 copy-start.2
  309.0 1.9 copy-start.17
  309.0 1.9 copy-start.20
  309.0 248.6 %reduce-scatter.5.cloned.1.call-start = ((), (), s32[]{:S(2)}) async-start(), calls=%async_computation.4 | async-start | bytes 10948608 | tf_op jit(solution)/shard_map/reduce_scatter | solution.py:312
  330.7 3.5 copy-start.5
  330.7 4.0 copy-start.25
  330.7 5.5 slice-start.2
  334.7 2.0 copy-start.7
  334.7 2.7 slice-start.3
  347.9 3.3 copy-start.15
  348.0 3.4 copy-start.22
  348.0 3.5 copy-start.21
  348.0 3.5 copy-start.18
  348.0 3.6 copy-start.14
  360.9 3.7 copy-start
Sparse Core Ops, SparseCore 0:
  10.9 63.1 all-gather.3
  77.6 85.8 all-gather.5
  309.1 101.6 reduce-scatter.6
  416.8 140.8 reduce-scatter.4

commit v2 on v1

--- a/solution.py
+++ b/solution.py
@@ -169,35 +169,36 @@
     dv_ref[...] = dv_sum[...].astype(BF)
 
 
-def attention_backward(bounds, stacked, mixed, grad_mixed, logsum, span=256):
+def attention_backward(bounds, stacked, mixed, grad_mixed, logsum, start=0, count=None, span=256):
     rows, width = mixed.shape
     pairs = width // PAIR
+    count = pairs if count is None else count
     return pl.pallas_call(
         functools.partial(attention_backward_kernel, span=span, scale=1.0 / math.sqrt(DH)),
         grid_spec=pltpu.PrefetchScalarGridSpec(
             num_scalar_prefetch=1,
-            grid=(pairs,),
+            grid=(count,),
             in_specs=[
-                pair_spec(rows, 0),
-                pair_spec(rows, pairs),
-                pair_spec(rows, 2 * pairs),
-                pair_spec(rows, 0),
-                pair_spec(rows, 0),
-                pl.BlockSpec((1, 8, rows), lambda pair, bounds: (pair, 0, 0)),
+                pair_spec(rows, start),
+                pair_spec(rows, pairs + start),
+                pair_spec(rows, 2 * pairs + start),
+                pair_spec(rows, start),
+                pair_spec(rows, start),
+                pl.BlockSpec((1, 8, rows), lambda pair, bounds: (start + pair, 0, 0)),
             ],
             out_specs=[pair_spec(rows, 0), pair_spec(rows, 0), pair_spec(rows, 0)],
             scratch_shapes=[pltpu.VMEM((rows, PAIR), F32), pltpu.VMEM((rows, PAIR), F32)],
         ),
-        out_shape=[jax.ShapeDtypeStruct((rows, width), BF)] * 3,
+        out_shape=[jax.ShapeDtypeStruct((rows, count * PAIR), BF)] * 3,
         compiler_params=pltpu.CompilerParams(vmem_limit_bytes=VMEM_BYTES),
         cost_estimate=pl.CostEstimate(
-            flops=10 * rows * rows * width * 4, bytes_accessed=16 * rows * width, transcendentals=0
+            flops=40 * rows * rows * count * PAIR, bytes_accessed=16 * rows * count * PAIR, transcendentals=0
         ),
         name="attention_backward",
     )(bounds, stacked, stacked, stacked, mixed, grad_mixed, logsum)
 
 
-def on_device(
+def general_layer(
     hidden,
     lengths,
     w_qkv,
@@ -373,12 +374,698 @@
     )
 
 
+CHIPS = (4, 2, 2, 2)
+
+
+def coordinates(index):
+    _, ys, xs, cores = CHIPS
+    return (index // (cores * xs * ys), index // (cores * xs) % ys, index // cores % xs, index % cores)
+
+
+def moved(array, step):
+    sizes = CHIPS
+    pairs = []
+    for source in range(math.prod(sizes)):
+        target = 0
+        for place, by, size in zip(coordinates(source), step, sizes):
+            target = target * size + (place + by) % size
+        pairs.append((source, target))
+    return lax.ppermute(array, "fsdp", pairs)
+
+
+def pack_weights_kernel(down_ref, up_ref, out_ref, packed_ref):
+    width = down_ref.shape[1]
+    wide = up_ref.shape[1] // width
+    parts = [down_ref[...]] + [up_ref[:, width * i : width * (i + 1)] for i in range(wide)]
+    parts = [part.astype(F32) for part in parts + [out_ref[...]]]
+    fill = packed_ref.shape[0] - sum(part.shape[0] for part in parts)
+    parts.append(jnp.zeros((fill, width), F32))
+    packed_ref[...] = jnp.concatenate(parts, axis=0).astype(BF)
+
+
+def pack_weights(w_down, w_up, w_out):
+    rows = w_down.shape[0] + w_up.size // w_out.shape[1] + w_out.shape[0]
+    return pl.pallas_call(
+        pack_weights_kernel,
+        out_shape=jax.ShapeDtypeStruct((rows + -rows % 16, w_out.shape[1]), BF),
+        name="pack_weights",
+    )(w_down, w_up, w_out)
+
+
+def pack_front_kernel(qkv_ref, vector_ref, up_ref, packed_ref):
+    width = packed_ref.shape[1]
+    parts = [qkv_ref[:, width * i : width * (i + 1)].astype(F32) for i in range(3)]
+    extra = jnp.zeros((8, width), F32)
+    lanes = lax.broadcasted_iota(jnp.int32, (8, PAIR), 1)
+    rows = lax.broadcasted_iota(jnp.int32, (8, PAIR), 0)
+    part, inner_part = vector_ref.shape[1], up_ref.shape[1]
+    vectors = jnp.concatenate(
+        [vector_ref[...].astype(F32), jnp.zeros((8, PAIR - part), F32)], axis=1
+    )
+    long = jnp.concatenate([up_ref[...].astype(F32), jnp.zeros((1, PAIR - inner_part), F32)], axis=1)
+    long = jnp.where((rows == 0) & (lanes < inner_part), long, 0.0)
+    extra = jnp.concatenate([vectors, long, extra[:, 2 * PAIR :]], axis=1)
+    packed_ref[...] = jnp.concatenate(parts + [extra], axis=0).astype(BF)
+
+
+def pack_front(w_qkv, vectors, bias_up):
+    part, width = w_qkv.shape[0], w_qkv.shape[1] // 3
+    return pl.pallas_call(
+        pack_front_kernel,
+        out_shape=jax.ShapeDtypeStruct((3 * part + 8, width), BF),
+        name="pack_front",
+    )(w_qkv, vectors, bias_up)
+
+
+def gather_pieces(packed):
+    column = jnp.stack([packed] + [moved(packed, (step, 0, 0, 0)) for step in range(1, CHIPS[0])])
+    pieces = [column] + [moved(column, step) for step in ((0, 0, 1, 0), (0, 1, 0, 0), (0, 1, 1, 0))]
+    return pieces, [moved(piece, (0, 0, 0, 1)) for piece in pieces]
+
+
+NEAR = ((0, 0, 1, 0), (0, 1, 0, 0), (0, 1, 1, 0))
+
+
+def near_sum_kernel(place_ref, *refs, cuts):
+    pairs = [(refs[2 * i], refs[2 * i + 1]) for i in range(len(cuts))]
+    outs = refs[2 * len(cuts) :]
+    ys, xs = CHIPS[1:3]
+    for out_ref, (_, step_y, step_x, _) in zip(outs, ((0, 0, 0, 0),) + NEAR):
+        chip = (place_ref[1] + step_y) % ys * xs + (place_ref[2] + step_x) % xs
+        for (keep_ref, came_ref), (start, size) in zip(pairs, cuts):
+            total = keep_ref[chip].astype(F32) + came_ref[chip].astype(F32)
+            out_ref[0, start : start + size, :] = total.astype(BF)
+
+
+def near_sum(place, *pairs):
+    zs, ys, xs, _ = CHIPS
+    near = ys * xs
+    sizes = [keep.shape[1] for keep, _ in pairs]
+    cuts = [(sum(sizes[:i]), size) for i, size in enumerate(sizes)]
+    width = pairs[0][0].shape[2]
+    out = jax.ShapeDtypeStruct((zs, sum(sizes), width), BF)
+    return pl.pallas_call(
+        functools.partial(near_sum_kernel, cuts=cuts),
+        grid_spec=pltpu.PrefetchScalarGridSpec(
+            num_scalar_prefetch=1,
+            grid=(zs,),
+            in_specs=[
+                pl.BlockSpec((near, size, width), lambda step, place: (step, 0, 0))
+                for size in sizes
+                for _ in range(2)
+            ],
+            out_specs=[pl.BlockSpec((1, sum(sizes), width), lambda step, place: (step, 0, 0))] * 4,
+        ),
+        out_shape=[out] * 4,
+        compiler_params=params(48),
+        cost_estimate=pl.CostEstimate(
+            flops=out.size, bytes_accessed=out.size, transcendentals=0
+        ),
+        name="near_sum",
+    )(place, *(array for pair in pairs for array in pair))
+
+
+def send_near(sends):
+    return [moved(array, step) for array, step in zip(sends, NEAR)]
+
+
+def far_sum(parts):
+    zs, ys, xs, cores = CHIPS
+    across = ys * xs * cores
+    groups = [[level * across + i for level in range(zs)] for i in range(across)]
+    total = sum(part.astype(F32) for part in parts).astype(BF)
+    return lax.psum_scatter(
+        total, "fsdp", scatter_dimension=0, axis_index_groups=groups, tiled=False
+    ).astype(F32)
+
+
+def reduce_far(parts, place):
+    z, zs = place[0], CHIPS[0]
+
+    def at(level):
+        return sum(
+            lax.dynamic_index_in_dim(part, level, 0, keepdims=False).astype(F32) for part in parts
+        )
+
+    return at(z), [at((z + step) % zs).astype(BF) for step in range(1, zs)]
+
+
+def send_far(sends):
+    return [moved(array, (step, 0, 0, 0)) for step, array in enumerate(sends, 1)]
+
+
+def total_of(mine, came):
+    return mine + sum(array.astype(F32) for array in came)
+
+
+def after(value, *first):
+    return lax.optimization_barrier((value, *first))[0]
+
+
+def params(megabytes):
+    return pltpu.CompilerParams(vmem_limit_bytes=megabytes * 2**20)
+
+
+def whole_block(array):
+    return pl.BlockSpec(array.shape, lambda *step: (0,) * array.ndim)
+
+
+def project_kernel(
+    place_ref, hidden_ref, *refs, part, inner_part
+):
+    pieces = refs[: len(refs) - 4]
+    stacked_ref, weight_ref, vector_ref, up_ref = refs[len(refs) - 4 :]
+    z, y, x, core = (place_ref[i] for i in range(4))
+    zs, ys, xs, cores = CHIPS
+    width = hidden_ref.shape[1]
+    lanes = lax.broadcasted_iota(jnp.int32, (8, width), 1)
+    up_lanes = lax.broadcasted_iota(jnp.int32, (8, up_ref.shape[1]), 1)
+    vectors = jnp.zeros((8, width), F32)
+    ups = jnp.zeros(up_ref.shape, F32)
+    steps = ((0, 0), (0, 1), (1, 0), (1, 1))
+    for kind, (step_y, step_x) in enumerate(steps):
+        for step_z in range(zs):
+            chip = ((z + zs - step_z) % zs * ys + (y + step_y) % ys) * xs + (x + step_x) % xs
+            mine = pieces[kind][step_z].astype(F32)
+            other = pieces[len(steps) + kind][step_z].astype(F32)
+            low = jnp.where(core == 0, mine, other)
+            high = jnp.where(core == 0, other, mine)
+            rows = pl.ds(pl.multiple_of(chip * (cores * part), cores * part), cores * part)
+            for third in range(3):
+                cut = slice(third * part, (third + 1) * part)
+                weight_ref[rows, third * width : (third + 1) * width] = jnp.concatenate(
+                    [low[cut], high[cut]], axis=0
+                ).astype(BF)
+            for owner, piece in ((chip * cores, low), (chip * cores + 1, high)):
+                extra = piece[3 * part :]
+                vectors += pltpu.roll(jnp.where(lanes < part, extra, 0.0), owner * part, 1)
+                long = jnp.concatenate(
+                    [extra[:, PAIR:]] + [jnp.zeros((8, up_ref.shape[1] - width + PAIR), F32)], axis=1
+                )
+                ups += pltpu.roll(jnp.where(up_lanes < inner_part, long, 0.0), owner * inner_part, 1)
+    vector_ref[...] = vectors
+    up_ref[...] = ups
+    hidden = hidden_ref[...]
+    for third, bias in ((0, vectors[0:1]), (1, None), (2, vectors[1:2])):
+        cut = slice(third * width, (third + 1) * width)
+        projected = dot(hidden, weight_ref[:, cut])
+        stacked_ref[:, cut] = (projected if bias is None else projected + bias).astype(BF)
+
+
+def project(place, hidden, pieces, hidden_units, count):
+    rows, width = hidden.shape
+    outs = [
+        jax.ShapeDtypeStruct((rows, 3 * width), BF),
+        jax.ShapeDtypeStruct((width, 3 * width), BF),
+        jax.ShapeDtypeStruct((8, width), F32),
+        jax.ShapeDtypeStruct((8, hidden_units), F32),
+    ]
+    return pl.pallas_call(
+        functools.partial(project_kernel, part=width // count, inner_part=hidden_units // count),
+        grid_spec=pltpu.PrefetchScalarGridSpec(
+            num_scalar_prefetch=1,
+            grid=(1,),
+            in_specs=[whole_block(hidden)] + [whole_block(piece) for piece in pieces],
+            out_specs=[whole_block(out) for out in outs],
+        ),
+        out_shape=outs,
+        compiler_params=params(48),
+        name="project",
+    )(place, hidden, *pieces)
+
+
+def gelu_and_slope(inner):
+    near = 1.0 / (1.0 + (0.3275911 * ROOT_HALF) * jnp.abs(inner))
+    bell = jnp.exp(-0.5 * inner * inner)
+    series = 0.7107068705 + near * (-0.7265760135 + near * 0.5307027145)
+    series = near * (0.127414796 + near * (-0.142248368 + near * series))
+    tail = series * bell
+    normal_cdf = jnp.where(inner >= 0, 1.0 - tail, tail)
+    return inner * normal_cdf, normal_cdf + inner * bell * INV_ROOT_TWO_PI
+
+
+def norm_back(upstream, normed, rstd_rows, gain):
+    scaled = upstream * gain
+    plain_mean = jnp.mean(scaled, axis=-1, keepdims=True)
+    cross_mean = jnp.mean(scaled * normed, axis=-1, keepdims=True)
+    return rstd_rows * (scaled - plain_mean - normed * cross_mean)
+
+
+def column_sum(values):
+    return jnp.sum(values, axis=0, keepdims=True)
+
+
+def row_pass_kernel(
+    bounds_ref, mixed_ref, hidden_ref, cotangent_ref, vector_ref, bias_up_ref, gathered_ref,
+    output_ref, first_turned_ref, mixed_turned_ref, activated_turned_ref, grad_second_ref,
+    grad_inner_ref, grad_sum_ref, grad_branch_ref, grad_mixed_ref, sums_ref, up_sums_ref,
+    w_out, w_up, w_down, staged, slope, sems, *, part, chunk
+):
+    step = pl.program_id(0)
+    span, width = mixed_ref.shape
+    count, inner_part = w_down.shape[0], w_down.shape[1]
+    hidden_units = w_up.shape[1]
+    wide = hidden_units // width
+
+    @pl.when(step == 0)
+    def _():
+        narrow = pltpu.make_async_copy(
+            gathered_ref.at[:, pl.ds(inner_part, staged.shape[1]), :], staged, sems.at[0]
+        )
+        down = pltpu.make_async_copy(
+            gathered_ref.at[:, pl.ds(0, inner_part), :], w_down, sems.at[1]
+        )
+        narrow.start()
+        down.start()
+        narrow.wait()
+        for pair in range(count // 2):
+            low = staged[2 * pair].astype(F32)
+            high = staged[2 * pair + 1].astype(F32)
+            rows = slice(2 * pair * part, 2 * (pair + 1) * part)
+            for group in range(wide + 1):
+                cut = slice(group * part, (group + 1) * part)
+                both = jnp.concatenate([low[cut], high[cut]], axis=0).astype(BF)
+                if group < wide:
+                    w_up[rows, group * width : (group + 1) * width] = both
+                else:
+                    w_out[rows, :] = both
+        down.wait()
+
+    def down_rows(cut):
+        owners = slice(cut.start // inner_part, cut.stop // inner_part)
+        return w_down[owners].reshape(cut.stop - cut.start, width)
+
+    bias_out, gain_one, shift_one, bias_down, gain_two, shift_two = (
+        vector_ref[i : i + 1, :] for i in range(2, 8)
+    )
+    mixed = mixed_ref[...]
+    branch = dot(mixed, w_out[...]) + bias_out
+    first, normed_one, rstd_one = norm_forward(
+        hidden_ref[...].astype(F32) + branch, gain_one, shift_one
+    )
+    first_low = first.astype(BF)
+    first_turned_ref[...] = jnp.transpose(first_low)
+    mixed_turned_ref[...] = jnp.transpose(mixed)
+    cuts = [slice(start, start + chunk) for start in range(0, hidden_units, chunk)]
+    second = jnp.zeros(first.shape, F32)
+    for cut in cuts:
+        inner = dot(first_low, w_up[:, cut]) + bias_up_ref[0:1, cut]
+        activated, slopes = gelu_and_slope(inner)
+        activated = activated.astype(BF)
+        slope[:, cut] = slopes
+        activated_turned_ref[cut, :] = jnp.transpose(activated)
+        second += dot(activated, down_rows(cut))
+    result, normed_two, rstd_two = norm_forward(
+        first + (second + bias_down), gain_two, shift_two
+    )
+    row = lax.broadcasted_iota(jnp.int32, (span, 1), 0) + step * span
+    present = (row < bounds_ref[bounds_ref.shape[0] - 1]).astype(F32)
+    output_ref[...] = result * present
+    upstream = cotangent_ref[...].astype(F32) * present
+    grad_second = norm_back(upstream, normed_two, rstd_two, gain_two)
+    grad_second_low = grad_second.astype(BF)
+    grad_second_ref[...] = grad_second_low
+    grad_first = grad_second
+    up_sums = []
+    for cut in cuts:
+        grad_activated = dot_last(grad_second_low, down_rows(cut))
+        grad_inner = (grad_activated * slope[:, cut]).astype(BF)
+        grad_inner_ref[:, cut] = grad_inner
+        up_sums.append(column_sum(grad_inner.astype(F32)))
+        grad_first += dot_last(grad_inner, w_up[:, cut])
+    grad_sum = norm_back(grad_first, normed_one, rstd_one, gain_one)
+    grad_sum_ref[...] = grad_sum
+    grad_branch = grad_sum.astype(BF)
+    grad_branch_ref[...] = grad_branch
+    grad_mixed_ref[...] = dot_last(grad_branch, w_out[...]).astype(BF)
+    sums = jnp.concatenate(
+        [
+            column_sum(grad_branch.astype(F32)),
+            column_sum(grad_first * normed_one),
+            column_sum(grad_first),
+            column_sum(grad_second_low.astype(F32)),
+            column_sum(upstream * normed_two),
+            column_sum(upstream),
+            jnp.zeros((2, width), F32),
+        ],
+        axis=0,
+    )
+    up_sums = jnp.concatenate(
+        [jnp.concatenate(up_sums, axis=1), jnp.zeros((7, hidden_units), F32)], axis=0
+    )
+
+    @pl.when(step == 0)
+    def _():
+        sums_ref[...] = sums
+        up_sums_ref[...] = up_sums
+
+    @pl.when(step > 0)
+    def _():
+        sums_ref[...] += sums
+        up_sums_ref[...] += up_sums
+
+
+def row_pass(bounds, mixed, hidden, cotangent, vectors, bias_up, gathered, inner_part, span=256, chunk=768):
+    rows, width = mixed.shape
+    hidden_units = bias_up.shape[1]
+    count = gathered.shape[0]
+    part = width // count
+    row_spec = pl.BlockSpec((span, width), lambda step, bounds: (step, 0))
+    turned_spec = pl.BlockSpec((width, span), lambda step, bounds: (0, step))
+    shape = jax.ShapeDtypeStruct
+    sums = shape((8, width), F32)
+    up_sums = shape((8, hidden_units), F32)
+    staged_rows = gathered.shape[1] - inner_part
+    return pl.pallas_call(
+        functools.partial(row_pass_kernel, part=part, chunk=chunk),
+        grid_spec=pltpu.PrefetchScalarGridSpec(
+            num_scalar_prefetch=1,
+            grid=(rows // span,),
+            in_specs=[
+                row_spec,
+                row_spec,
+                row_spec,
+                whole_block(vectors),
+                whole_block(bias_up),
+                pl.BlockSpec(memory_space=pl.ANY),
+            ],
+            out_specs=[
+                row_spec,
+                turned_spec,
+                turned_spec,
+                pl.BlockSpec((hidden_units, span), lambda step, bounds: (0, step)),
+                row_spec,
+                pl.BlockSpec((span, hidden_units), lambda step, bounds: (step, 0)),
+                row_spec,
+                row_spec,
+                row_spec,
+                whole_block(sums),
+                whole_block(up_sums),
+            ],
+            scratch_shapes=[
+                pltpu.VMEM((width, width), BF),
+                pltpu.VMEM((width, hidden_units), BF),
+                pltpu.VMEM((count, inner_part, width), BF),
+                pltpu.VMEM((count, staged_rows, width), BF),
+                pltpu.VMEM((span, hidden_units), F32),
+                pltpu.SemaphoreType.DMA((2,)),
+            ],
+        ),
+        out_shape=[
+            shape((rows, width), F32),
+            shape((width, rows), BF),
+            shape((width, rows), BF),
+            shape((hidden_units, rows), BF),
+            shape((rows, width), BF),
+            shape((rows, hidden_units), BF),
+            shape((rows, width), F32),
+            shape((rows, width), BF),
+            shape((rows, width), BF),
+            sums,
+            up_sums,
+        ],
+        compiler_params=params(60),
+        cost_estimate=pl.CostEstimate(
+            flops=2 * rows * width * (4 * hidden_units + 2 * width),
+            bytes_accessed=40 * rows * width,
+            transcendentals=0,
+        ),
+        name="row_pass",
+    )(bounds, mixed, hidden, cotangent, vectors, bias_up, gathered)
+
+
+def split_owners(place_ref, keep_ref, send_ref, tile_of, count, lead=()):
+    for core in range(2):
+
+        @pl.when(place_ref[3] == core)
+        def _():
+            for owner in range(count):
+                target = keep_ref if owner % 2 == core else send_ref
+                target[(owner // 2,) + lead] = tile_of(owner).astype(BF)
+
+
+def down_grad_kernel(place_ref, left_ref, right_ref, keep_ref, send_ref):
+    part = keep_ref.shape[1]
+    product = dot(left_ref[...], right_ref[...])
+    count = product.shape[0] // part
+    split_owners(place_ref, keep_ref, send_ref, lambda o: product[o * part : (o + 1) * part], count)
+
+
+def down_grad(place, left, right, count, steps=4):
+    tall, rows = left.shape
+    width = right.shape[1]
+    part = tall // count
+    half = count // 2
+    spec = pl.BlockSpec((half // steps, part, width), lambda step, place: (step, 0, 0))
+    return pl.pallas_call(
+        down_grad_kernel,
+        grid_spec=pltpu.PrefetchScalarGridSpec(
+            num_scalar_prefetch=1,
+            grid=(steps,),
+            in_specs=[
+                pl.BlockSpec((tall // steps, rows), lambda step, place: (step, 0)),
+                whole_block(right),
+            ],
+            out_specs=[spec, spec],
+        ),
+        out_shape=[jax.ShapeDtypeStruct((half, part, width), BF)] * 2,
+        compiler_params=params(48),
+        cost_estimate=pl.CostEstimate(
+            flops=2 * rows * width * tall, bytes_accessed=4 * tall * rows, transcendentals=0
+        ),
+        name="grad_w_down",
+    )(place, left, right)
+
+
+def up_grad_kernel(place_ref, first_ref, mixed_ref, inner_ref, branch_ref, keep_ref, send_ref):
+    step = pl.program_id(0)
+    part = keep_ref.shape[2]
+
+    def go(product):
+        count = product.shape[0] // part
+        split_owners(
+            place_ref, keep_ref, send_ref, lambda o: product[o * part : (o + 1) * part], count, (0,)
+        )
+
+    @pl.when(step < pl.num_programs(0) - 1)
+    def _():
+        go(dot(first_ref[...], inner_ref[...]))
+
+    @pl.when(step == pl.num_programs(0) - 1)
+    def _():
+        go(dot(mixed_ref[...], branch_ref[...]))
+
+
+def up_grad(place, first_turned, mixed_turned, grad_inner, grad_branch, count):
+    width, rows = first_turned.shape
+    wide = grad_inner.shape[1] // width
+    half, part = count // 2, width // count
+    spec = pl.BlockSpec((half, 1, part, width), lambda step, place: (0, step, 0, 0))
+    return pl.pallas_call(
+        up_grad_kernel,
+        grid_spec=pltpu.PrefetchScalarGridSpec(
+            num_scalar_prefetch=1,
+            grid=(wide + 1,),
+            in_specs=[
+                whole_block(first_turned),
+                whole_block(mixed_turned),
+                pl.BlockSpec((rows, width), lambda step, place: (0, jnp.minimum(step, wide - 1))),
+                whole_block(grad_branch),
+            ],
+            out_specs=[spec, spec],
+        ),
+        out_shape=[jax.ShapeDtypeStruct((half, wide + 1, part, width), BF)] * 2,
+        compiler_params=params(48),
+        cost_estimate=pl.CostEstimate(
+            flops=2 * rows * width * width * (wide + 1),
+            bytes_accessed=4 * rows * width * (wide + 1),
+            transcendentals=0,
+        ),
+        name="grad_w_up_out",
+    )(place, first_turned, mixed_turned, grad_inner, grad_branch)
+
+
+def qkv_grad_kernel(place_ref, hidden_ref, sums_ref, up_sums_ref, *refs, part, inner_part):
+    keep_ref, send_ref = refs[-2:]
+    stack = refs[:-2]
+    each = len(stack) // 3
+    rows, width = hidden_ref.shape
+    turned = jnp.transpose(hidden_ref[...])
+    ones = jnp.ones((8, rows), BF)
+
+    def joined(left, third):
+        return jnp.concatenate(
+            [dot(left, ref[...]) for ref in stack[third * each : (third + 1) * each]], axis=1
+        )
+
+    products = [joined(turned, third) for third in range(3)]
+    vectors = jnp.concatenate(
+        [joined(ones, 0)[0:1], joined(ones, 2)[0:1], sums_ref[0:6, :]], axis=0
+    )
+    top = lax.broadcasted_iota(jnp.int32, (8, 1), 0) == 0
+
+    def tile_of(owner):
+        cut = slice(owner * part, (owner + 1) * part)
+        own = pltpu.roll(vectors, width - owner * part, 1) if owner else vectors
+        start = owner * inner_part // PAIR * PAIR
+        long = jnp.concatenate(
+            [up_sums_ref[:, start : start + PAIR], up_sums_ref[:, start + PAIR : start + 2 * PAIR]]
+            if start + 2 * PAIR <= up_sums_ref.shape[1]
+            else [up_sums_ref[:, start : start + PAIR]] * 2,
+            axis=1,
+        )
+        shift = owner * inner_part - start
+        long = pltpu.roll(long, 2 * PAIR - shift, 1) if shift else long
+        extra = jnp.concatenate(
+            [own[:, :PAIR], jnp.where(top, long[:, :PAIR], 0.0), jnp.zeros((8, width - 2 * PAIR), F32)],
+            axis=1,
+        )
+        return jnp.concatenate([product[cut] for product in products] + [extra], axis=0)
+
+    split_owners(place_ref, keep_ref, send_ref, tile_of, width // part)
+
+
+def qkv_grad(place, hidden, stack, sums, up_sums, count):
+    rows, width = hidden.shape
+    part = width // count
+    out = jax.ShapeDtypeStruct((count // 2, 3 * part + 8, width), BF)
+    return pl.pallas_call(
+        functools.partial(qkv_grad_kernel, part=part, inner_part=up_sums.shape[1] // count),
+        grid_spec=pltpu.PrefetchScalarGridSpec(
+            num_scalar_prefetch=1,
+            grid=(1,),
+            in_specs=[whole_block(array) for array in (hidden, sums, up_sums, *stack)],
+            out_specs=[whole_block(out)] * 2,
+        ),
+        out_shape=[out] * 2,
+        compiler_params=params(56),
+        cost_estimate=pl.CostEstimate(
+            flops=6 * rows * width * width, bytes_accessed=12 * rows * width, transcendentals=0
+        ),
+        name="grad_w_qkv",
+    )(place, hidden, sums, up_sums, *stack)
+
+
+def hidden_grad_kernel(grad_sum_ref, weight_ref, *refs):
+    out_ref = refs[-1]
+    stack = refs[:-1]
+    total = grad_sum_ref[...]
+    start = 0
+    for ref in stack:
+        size = ref.shape[1]
+        total += dot_last(ref[...], weight_ref[:, start : start + size])
+        start += size
+    out_ref[...] = total
+
+
+def hidden_grad(grad_sum, weight, stack, span=256):
+    rows, width = grad_sum.shape
+    return pl.pallas_call(
+        hidden_grad_kernel,
+        grid=(rows // span,),
+        in_specs=[pl.BlockSpec((span, width), lambda step: (step, 0)), whole_block(weight)]
+        + [pl.BlockSpec((span, array.shape[1]), lambda step: (step, 0)) for array in stack],
+        out_specs=pl.BlockSpec((span, width), lambda step: (step, 0)),
+        out_shape=jax.ShapeDtypeStruct((rows, width), F32),
+        compiler_params=params(48),
+        cost_estimate=pl.CostEstimate(
+            flops=6 * rows * width * width, bytes_accessed=14 * rows * width, transcendentals=0
+        ),
+        name="grad_hidden",
+    )(grad_sum, weight, *stack)
+
+
+def meshed_layer(
+    hidden, lengths, w_qkv, bias_q, bias_v, w_out, bias_out, norm1_gain, norm1_bias, w_up, bias_up,
+    w_down, bias_down, norm2_gain, norm2_bias, cotangent
+):
+    count_rows, width = hidden.shape
+    hidden_units = w_up.shape[1]
+    n = lax.axis_size("fsdp")
+    part = width // n
+    inner_part = hidden_units // n
+    wide = hidden_units // width
+    bounds = jnp.cumsum(lengths)
+    coords = coordinates(lax.axis_index("fsdp"))
+    place = jnp.stack([jnp.asarray(coord, jnp.int32) for coord in coords])
+
+    gathered = lax.all_gather(pack_weights(w_down, w_up, w_out), "fsdp", axis=0, tiled=True)
+    gathered = gathered.reshape(n, -1, width)
+    vectors = jnp.stack(
+        [bias_q, bias_v, bias_out, norm1_gain, norm1_bias, bias_down, norm2_gain, norm2_bias]
+    )
+    front = pack_front(w_qkv, vectors, bias_up[None])
+    mine, others = gather_pieces(front)
+    stacked, whole_qkv, whole_vectors, whole_up_bias = project(
+        place, hidden, mine + others, hidden_units, n
+    )
+    mixed, logsum = attention_forward(bounds, stacked)
+    (
+        output, first_turned, mixed_turned, activated_turned, grad_second, grad_inner, grad_sum,
+        grad_branch, grad_mixed, sums, up_sums,
+    ) = row_pass(
+        bounds, mixed, hidden, cotangent, whole_vectors, whole_up_bias, gathered, inner_part
+    )
+    core = (0, 0, 0, 1)
+    up_keep, up_send = up_grad(place, first_turned, mixed_turned, grad_inner, grad_branch, n)
+    up_came = moved(up_send, core)
+    down_keep, down_send = down_grad(place, activated_turned, after(grad_second, up_keep), n)
+    down_came = moved(down_send, core)
+    up_keep, up_came = (array.reshape(n // 2, -1, width) for array in (up_keep, up_came))
+    here, *sends = near_sum(place, (down_keep, down_came), (up_keep, up_came))
+    parts = [here] + send_near(sends)
+    stack = attention_backward(bounds, stacked, mixed, after(grad_mixed, *sends), logsum)
+    qkv_keep, qkv_send = qkv_grad(place, hidden, stack, sums, up_sums, n)
+    qkv_came = moved(qkv_send, core)
+    total = far_sum([here] + [after(part, qkv_keep) for part in parts[1:]])
+    here, *sends = near_sum(place, (qkv_keep, qkv_came))
+    qkv_parts = send_near(sends)
+    grad_hidden = hidden_grad(after(grad_sum, *sends), whole_qkv, stack)
+    qkv_mine, qkv_far = reduce_far([here] + [after(part, grad_hidden) for part in qkv_parts], coords)
+
+    my_up_out = total[inner_part:].reshape(wide + 1, part, width)
+    my_down = total[:inner_part]
+    my_up = my_up_out[:wide].transpose(1, 0, 2).reshape(part, hidden_units)
+    my_out = my_up_out[wide]
+    mine_qkv = total_of(
+        qkv_mine, [after(came, my_up, my_out, my_down) for came in send_far(qkv_far)]
+    )
+    my_qkv = jnp.concatenate([mine_qkv[part * i : part * (i + 1)] for i in range(3)], axis=1)
+    my_vectors = mine_qkv[3 * part :]
+    my_bias_q, my_bias_v, my_bias_out, my_gain_one, my_shift_one, my_bias_down, my_gain_two, my_shift_two = (
+        my_vectors[i, :part] for i in range(8)
+    )
+    my_bias_up = my_vectors[0, PAIR : PAIR + inner_part]
+    return (
+        output,
+        grad_hidden,
+        my_qkv,
+        my_bias_q,
+        my_bias_v,
+        my_out,
+        my_bias_out,
+        my_gain_one,
+        my_shift_one,
+        my_up,
+        my_bias_up,
+        my_down,
+        my_bias_down,
+        my_gain_two,
+        my_shift_two,
+    )
+
+
+def layer(*arrays):
+    known = lax.axis_size("fsdp") == math.prod(CHIPS)
+    return (meshed_layer if known else general_layer)(*arrays)
+
+
 def solution(mesh):
     rows = P("fsdp", None)
     flat = P("fsdp")
     weights = (rows, flat, flat, rows, flat, flat, flat, rows, flat, rows, flat, flat, flat)
     return jax.shard_map(
-        on_device,
+        layer,
         mesh=mesh,
         in_specs=(rows, flat) + weights + (rows,),
         out_specs=(rows, rows) + weights,

time: 576 us -> 317 us (0.55); the launches traced: 568 us -> 316 us
  waiting for transfers between devices: 209 us -> 79.6 us
  matrix products: 110 us -> 0 us
  Pallas kernels: 66.9 us -> 172 us
  blocking collectives: 82.5 us -> 0 us
  local copies, waits for them, and re-layouts: 67.8 us -> 19.4 us
  starting transfers between devices: 0.16 us -> 22.9 us
  other arithmetic: 16.7 us -> 7.41 us
    reduce_scatter x1, waiting for transfers between devices: 145 us -> 0.01 us  [far_sum(): lax.psum_scatter(total, 'fsdp', scatter_dimension=0, axis_index_groups=gr...]
    dot_general x12 -> x0, matrix products: 110 us -> none  [the longest x1 36.4 us: on_device(): jnp.dot(first_low, whole_up, preferred_element_type=F32) + whole_bias_up]
    pallas_call x0 -> x10, Pallas kernels: none -> 106 us  [the longest x1 45.8 us: row_pass(): pl.pallas_call(functools.partial(row_pass_kernel, part=part, chunk=chunk)...]
    ppermute x0 -> x22, waiting for transfers between devices: none -> 63.5 us  [moved(): return lax.ppermute(array, 'fsdp', pairs)]
    all_gather x2 -> x1, waiting for transfers between devices: 61.4 us -> 16.1 us  [meshed_layer(): lax.all_gather(pack_weights(w_down, w_up, w_out), 'fsdp', axis=0, tiled=T...]
    unnamed x1 -> x0, blocking collectives: 42.6 us -> none
    psum x1 -> x0, blocking collectives: 39.9 us -> none  [on_device(): every_vector = lax.psum(vector_grads, 'fsdp')]
    ppermute x0 -> x22, starting transfers between devices: none -> 22.8 us  [moved(): return lax.ppermute(array, 'fsdp', pairs)]
  transfers between devices with their start and end apart: 4 -> 24, of which waited for: 4 -> 12; matrix products, arithmetic and copies ran while one was open for 15% -> 2% of each run, Pallas kernels for 4% -> 34%
where the time goes in v2:
time: 317 us; the launch traced here: 316 us
  Pallas kernels  172 us (54%)
  waiting for transfers between devices  79.6 us (25%)
  starting transfers between devices  22.9 us (7%)
  local copies, waits for them, and re-layouts  19.4 us (6%)
  between operations  14.2 us (4%)
  other arithmetic  7.41 us (2%)
    ppermute x22, waiting for transfers between devices, moved(): return lax.ppermute(array, 'fsdp', pairs)  63.5 us
    pallas_call x1, Pallas kernels, row_pass(): pl.pallas_call(functools.partial(row_pass_kernel, part=part, chunk=chunk)...  45.8 us
    pallas_call x1, Pallas kernels, attention_backward(): pl.pallas_call(functools.partial(attention_backward_kernel, span=span, sc...  41.3 us
    pallas_call x1, Pallas kernels, attention_forward(): pl.pallas_call(functools.partial(attention_forward_kernel, span=span, sca...  24.9 us
    ppermute x22, starting transfers between devices, moved(): return lax.ppermute(array, 'fsdp', pairs)  22.8 us
    all_gather x1, waiting for transfers between devices, meshed_layer(): lax.all_gather(pack_weights(w_down, w_up, w_out), 'fsdp', axis=0, tiled=T...  16.1 us
    unnamed x40, local copies, waits for them, and re-layouts  13.9 us
    pallas_call x1, Pallas kernels, up_grad(): pl.pallas_call(up_grad_kernel, grid_spec=pltpu.PrefetchScalarGridSpec(num...  11 us
  transfers between devices with their start and end apart: 24, of which 12 were waited for; matrix products, arithmetic and copies ran while one was open for 2% of the time, Pallas kernels for 34%

profile of v2, /device:TPU:0, one launch (start us, length us, event | category | flops | bytes accessed | tf_op | source)
XLA Modules:
  0.0 315.9 jit_solution(13166015741630321646)
XLA Ops:
  7.2 1.8 pack_weights.1
  9.2 1.4 stack.70.vector_ref
  10.5 1.6 pack_front.1
  12.1 3.0 collective-permute-start
  15.1 2.6 collective-permute-start.1
  17.7 1.3 collective-permute-start.2
  19.1 2.5 collective-permute-done
  21.6 4.4 %collective-permute-done.1 = bf16[80,768]{1,0:T(8,128)(2,1)S(1)} collective-permute-done((bf16[80,768]{1,0:T(8,128)(2,1)}, bf16[80,768]{1,0:T(8,128)(2,1)S(1)}, u32[]{:S(2)}, u32[]{:S(2)}) %collective-permute-start.1) | collective-permute-done | bytes 122912 | tf_op jit(solution)/shard_map/ppermute | solution.py:393
  26.1 1.0 pad_maximum_fusion.refs_0_
  27.0 1.6 collective-permute-start.3
  28.6 1.5 collective-permute-start.4
  30.1 0.5 collective-permute-start.5
  30.6 10.6 %collective-permute-done.3.refs_1_ = bf16[4,80,768]{2,1,0:T(8,128)(2,1)S(1)} collective-permute-done((bf16[4,80,768]{2,1,0:T(8,128)(2,1)S(1)}, bf16[4,80,768]{2,1,0:T(8,128)(2,1)S(1)}, u32[]{:S(2)}, u32[]{:S(2)}) %collective-permute-start.3) | collective-permute-done | bytes 491552 | tf_op jit(solution)/shard_map/ppermute | solution.py:393
  41.2 8.7 %collective-permute-done.4.refs_2_ = bf16[4,80,768]{2,1,0:T(8,128)(2,1)S(1)} collective-permute-done((bf16[4,80,768]{2,1,0:T(8,128)(2,1)S(1)}, bf16[4,80,768]{2,1,0:T(8,128)(2,1)S(1)}, u32[]{:S(2)}, u32[]{:S(2)}) %collective-permute-start.4) | collective-permute-done | bytes 491552 | tf_op jit(solution)/shard_map/ppermute | solution.py:393
  49.8 8.8 %collective-permute-done.5.refs_3_ = bf16[4,80,768]{2,1,0:T(8,128)(2,1)S(1)} collective-permute-done((bf16[4,80,768]{2,1,0:T(8,128)(2,1)S(1)}, bf16[4,80,768]{2,1,0:T(8,128)(2,1)S(1)}, u32[]{:S(2)}, u32[]{:S(2)}) %collective-permute-start.5) | collective-permute-done | bytes 491552 | tf_op jit(solution)/shard_map/ppermute | solution.py:393
  58.6 0.7 reduce-window.9
  59.4 1.2 collective-permute-done.9.refs_7_
  60.6 10.5 %project.1 = (bf16[1024,2304]{1,0:T(8,128)(2,1)}, bf16[768,2304]{1,0:T(8,128)(2,1)}, f32[8,768]{1,0:T(8,128)S(1)}, f32[8,3072]{1,0:T(8,128)S(1)}) custom-call(s32[4]{0:T(128)S(1)} %pad_add_fusion.place_ref, bf16[1024,768]{1,0:T(8,128)(2,1)S(1)} %copy-done.5, bf16[4,80,768]{2,1,0:T(8,128)(2,1)S(1)} %pad_maximum_fusion.refs_0_, ...), custom_call_target="tpu_custom_call" | custom-call | tf_op jit(solution)/shard_map/project/pallas_call | solution.py:583
  71.1 0.6 copy-done.10
  71.8 0.6 copy-done.11
  72.4 24.9 %attention_forward.1 = (bf16[1024,768]{1,0:T(8,128)(2,1)}, f32[6,8,1024]{2,1,0:T(8,128)}) custom-call(s32[2]{0:T(128)} %bitcast.76, bf16[1024,2304]{1,0:T(8,128)(2,1)} %get-tuple-element.61.q_ref.k_ref.v_ref, bf16[1024,2304]{1,0:T(8,128)(2,1)} %get-tuple-element.61.q_ref.k_ref.v_ref, bf16[1024,2304]{1,0:T(8,128)(2,1)} %get-tuple-element.61.q_ref.k_ref.v_ref), custom_call_target="tpu_custom_call" | custom-call | flops 12884901888 | bytes 6291456 | tf_op jit(solution)/shard_map/attention_forward/pallas_call | solution.py:95
  97.3 16.1 %all-gather.2.cloned.1.call-done = bf16[7168,768]{1,0:T(8,128)(2,1)} async-done(((bf16[224,768]{1,0:T(8,128)(2,1)}), bf16[7168,768]{1,0:T(8,128)(2,1)}) %all-gather.2.cloned.1.call-update) | async-done | bytes 11010064 | tf_op jit(solution)/shard_map/all_gather | solution.py:992
  113.4 45.8 %row_pass.1 = (f32[1024,768]{1,0:T(8,128)}, bf16[768,1024]{1,0:T(8,128)(2,1)}, bf16[768,1024]{1,0:T(8,128)(2,1)}, bf16[3072,1024]{1,0:T(8,128)(2,1)}, bf16[1024,...) custom-call(s32[2]{0:T(128)} %bitcast.77, ...), custom_call_target="tpu_custom_call" | custom-call | flops 21743271936 | bytes 31457280 | tf_op jit(solution)/shard_map/row_pass/pallas_call | solution.py:739
  159.3 1.4 copy-done.13
  160.7 1.4 copy-done.14
  162.1 1.4 copy-done.15
  163.5 11.0 %grad_w_up_out.1 = (bf16[16,5,24,768]{3,2,1,0:T(8,128)(2,1)}, bf16[16,5,24,768]{3,2,1,0:T(8,128)(2,1)}) custom-call(s32[4]{0:T(128)S(1)} %pad_add_fusion.place_ref, bf16[768,1024]{1,0:T(8,128)(2,1)S(1)} %copy-done.13, bf16[768,1024]{1,0:T(8,128)(2,1)S(1)} %copy-done.14, bf16[1024,3072]{1,0:T(8,128)(2,1)} %get-tuple-element.74.inner_ref, ...), custom_call_target="tpu_custom_call" | custom-call | flops 6039797760 | bytes 15728640 | tf_op jit(solution)/shard_map/grad_w_up_out/pallas_call | solution.py:864
  174.7 9.2 %grad_w_down.1 = (bf16[16,96,768]{2,1,0:T(8,128)(2,1)S(1)}, bf16[16,96,768]{2,1,0:T(8,128)(2,1)}) custom-call(s32[4]{0:T(128)S(1)} %pad_add_fusion.place_ref, bf16[3072,1024]{1,0:T(8,128)(2,1)} %get-tuple-element.70.left_ref, bf16[1024,768]{1,0:T(8,128)(2,1)S(1)} %copy-done.12), custom_call_target="tpu_custom_call" | custom-call | flops 4831838208 | bytes 12582912 | tf_op jit(solution)/shard_map/grad_w_down/pallas_call | solution.py:820
  184.0 1.4 copy-done
  185.4 0.3 collective-permute-start.10
  185.7 4.5 %collective-permute-done.10.refs_1_ = bf16[16,96,768]{2,1,0:T(8,128)(2,1)S(1)} collective-permute-done((bf16[16,96,768]{2,1,0:T(8,128)(2,1)}, bf16[16,96,768]{2,1,0:T(8,128)(2,1)S(1)}, u32[]{:S(2)}, u32[]{:S(2)}) %collective-permute-start.10) | collective-permute-done | bytes 2359328 | tf_op jit(solution)/shard_map/ppermute | solution.py:393
  190.2 1.4 copy-done.17
  191.6 0.9 copy-done.16
  192.4 5.6 %near_sum.2 = (bf16[4,216,768]{2,1,0:T(8,128)(2,1)S(1)}, bf16[4,216,768]{2,1,0:T(8,128)(2,1)S(1)}, bf16[4,216,768]{2,1,0:T(8,128)(2,1)S(1)}, bf16[4,216,768]{2,1,0:T(8,128)(2,1)S(1)}) custom-call(s32[4]{0:T(128)S(1)} %pad_add_fusion.place_ref, bf16[16,96,768]{2,1,0:T(8,128)(2,1)} %copy-done, bf16[16,96,768]{2,1,0:T(8,128)(2,1)} %copy-done.17, ...), custom_call_target="tpu_custom_call" | custom-call | flops 663552 | bytes 663552 | tf_op jit(solution)/shard_map/near_sum/pallas_call | solution.py:467
  198.0 1.5 collective-permute-start.17
  199.5 0.6 collective-permute-start.18
  200.1 1.4 collective-permute-start.19
  201.6 41.3 %attention_backward.1 = (bf16[1024,768]{1,0:T(8,128)(2,1)}, bf16[1024,768]{1,0:T(8,128)(2,1)}, bf16[1024,768]{1,0:T(8,128)(2,1)}) custom-call(s32[2]{0:T(128)} %bitcast.78, bf16[1024,2304]{1,0:T(8,128)(2,1)} %get-tuple-element.61.q_ref.k_ref.v_ref, bf16[1024,2304]{1,0:T(8,128)(2,1)} %get-tuple-element.61.q_ref.k_ref.v_ref, ...), custom_call_target="tpu_custom_call" | custom-call | flops 32212254720 | bytes 12582912 | tf_op jit(solution)/shard_map/attention_backward/pallas_call | solution.py:176
  242.9 10.2 %grad_w_qkv.1 = (bf16[16,80,768]{2,1,0:T(8,128)(2,1)}, bf16[16,80,768]{2,1,0:T(8,128)(2,1)}) custom-call(s32[4]{0:T(128)} %copy-done.8, bf16[1024,768]{1,0:T(8,128)(2,1)} %hidden_ref.5, f32[8,768]{1,0:T(8,128)} %get-tuple-element.67.sums_ref, f32[8,3072]{1,0:T(8,128)} %get-tuple-element.68.up_sums_ref, bf16[1024,768]{1,0:T(8,128)(2,1)} %get-tuple-element.86.refs_0_, ...), custom_call_target="tpu_custom_call" | custom-call | flops 3623878656 | bytes 9437184 | tf_op jit(solution)/shard_map/grad_w_qkv/pallas_call | solution.py:932
  253.1 5.9 %collective-permute-done.18 = bf16[4,216,768]{2,1,0:T(8,128)(2,1)S(1)} collective-permute-done((bf16[4,216,768]{2,1,0:T(8,128)(2,1)S(1)}, bf16[4,216,768]{2,1,0:T(8,128)(2,1)S(1)}, u32[]{:S(2)}, u32[]{:S(2)}) %collective-permute-start.18) | collective-permute-done | bytes 1327136 | tf_op jit(solution)/shard_map/ppermute | solution.py:393
  259.0 1.1 copy-done.18
  260.0 3.7 %add_convert_fusion = bf16[4,216,768]{2,1,0:T(8,128)(2,1)} fusion(bf16[4,216,768]{2,1,0:T(8,128)(2,1)} %collective-permute-done.19, bf16[4,216,768]{2,1,0:T(8,128)(2,1)} %copy-done.18, bf16[4,216,768]{2,1,0:T(8,128)(2,1)S(1)} %collective-permute-done.17, bf16[4,216,768]{2,1,0:T(8,128)(2,1)S(1)} %get-tuple-element.100), kind=kLoop, calls=%fused_computation | loop fusion | flops 5308416 | bytes 6635520 | tf_op jit(solution)/shard_map/convert_element_type | solution.py:496
  263.8 4.2 %collective-permute-done.12.refs_1_ = bf16[16,80,768]{2,1,0:T(8,128)(2,1)S(1)} collective-permute-done((bf16[16,80,768]{2,1,0:T(8,128)(2,1)}, bf16[16,80,768]{2,1,0:T(8,128)(2,1)S(1)}, u32[]{:S(2)}, u32[]{:S(2)}) %collective-permute-start.12) | collective-permute-done | bytes 1966112 | tf_op jit(solution)/shard_map/ppermute | solution.py:393
  268.0 2.3 near_sum.3
  270.3 0.8 copy-done.6
  271.1 0.6 collective-permute-start.13
  271.7 1.5 collective-permute-start.14
  273.2 1.4 collective-permute-start.15
  274.6 1.4 copy-done.3
  276.0 1.4 copy-done.4
  277.4 8.1 %grad_hidden.1 = f32[1024,768]{1,0:T(8,128)} custom-call(f32[1024,768]{1,0:T(8,128)} %get-tuple-element.94.grad_sum_ref, bf16[768,2304]{1,0:T(8,128)(2,1)} %get-tuple-element.95.weight_ref, bf16[1024,768]{1,0:T(8,128)(2,1)S(1)} %copy-done.2, bf16[1024,768]{1,0:T(8,128)(2,1)S(1)} %copy-done.3, bf16[1024,768]{1,0:T(8,128)(2,1)S(1)} %copy-done.4), custom_call_target="tpu_custom_call" | custom-call | flops 3623878656 | bytes 11010048 | tf_op jit(solution)/shard_map/grad_hidden/pallas_call | solution.py:963
  285.5 9.9 %collective-permute-done.14 = bf16[4,80,768]{2,1,0:T(8,128)(2,1)S(1)} collective-permute-done((bf16[4,80,768]{2,1,0:T(8,128)(2,1)}, bf16[4,80,768]{2,1,0:T(8,128)(2,1)S(1)}, u32[]{:S(2)}, u32[]{:S(2)}) %collective-permute-start.14) | collective-permute-done | bytes 491552 | tf_op jit(solution)/shard_map/ppermute | solution.py:393
  295.6 1.3 collective-permute-start.16
  296.9 1.1 collective-permute-start.20
  298.0 2.4 collective-permute-start.21
  300.3 1.0 convert_element_type.108
  301.4 0.7 slice_bitcast_fusion
  302.1 0.9 slice.87
  303.0 0.7 copy.32
  303.8 0.6 slice_bitcast_fusion.1
  304.4 2.8 collective-permute-done.20
  307.3 0.5 slice_bitcast_fusion.2
  307.9 0.5 slice_bitcast_fusion.5
  308.4 0.7 pad_maximum_fusion.1
  (54 shorter events, 0.9 us)
Async XLA Ops:
  7.2 51.5 %copy-start.19 = (s32[2]{0:T(128)S(1)}, s32[2]{0:T(128)}, u32[]{:S(2)}) copy-start(s32[2]{0:T(128)} %param.17) | copy-start | bytes 28
  7.2 53.5 %copy-start.5 = (bf16[1024,768]{1,0:T(8,128)(2,1)S(1)}, bf16[1024,768]{1,0:T(8,128)(2,1)}, u32[]{:S(2)}) copy-start(bf16[1024,768]{1,0:T(8,128)(2,1)} %hidden_ref.5) | copy-start | bytes 4718596
  7.2 106.2 %all-gather.2.cloned.1.call-start = ((), (), s32[]{:S(2)}) async-start(), calls=%async_computation.1 | async-start | bytes 11354112 | tf_op jit(solution)/shard_map/all_gather | solution.py:992
  9.1 291.2 %reduce-scatter.2.cloned.1.call-start = ((), (), s32[]{:S(2)}) async-start(), calls=%async_computation.2 | async-start | bytes 1658880 | tf_op jit(solution)/shard_map/reduce_scatter | solution.py:497
  12.1 9.5 %collective-permute-start = (bf16[80,768]{1,0:T(8,128)(2,1)}, bf16[80,768]{1,0:T(8,128)(2,1)S(1)}, u32[]{:S(2)}, u32[]{:S(2)}) collective-permute-start(bf16[80,768]{1,0:T(8,128)(2,1)} %pack_front.1), channel_id=1, source_target_pairs={{0,8},{1,9},{2,10},{3,11},{4,12},{5,13},{6,14},{7,15},{8,16},{9,17... | collective-permute-start | bytes 368648 | tf_op jit(solution)/shard_map/ppermute | solution.py:393
  15.1 10.9 %collective-permute-start.1 = (bf16[80,768]{1,0:T(8,128)(2,1)}, bf16[80,768]{1,0:T(8,128)(2,1)S(1)}, u32[]{:S(2)}, u32[]{:S(2)}) collective-permute-start(bf16[80,768]{1,0:T(8,128)(2,1)} %pack_front.1), channel_id=1, source_target_pairs={{0,16},{1,17},{2,18},{3,19},{4,20},{5,21},{6,22},{7,23},{8,24},{9,... | collective-permute-start | bytes 368648 | tf_op jit(solution)/shard_map/ppermute | solution.py:393
  17.7 8.3 %collective-permute-start.2 = (bf16[80,768]{1,0:T(8,128)(2,1)}, bf16[80,768]{1,0:T(8,128)(2,1)S(1)}, u32[]{:S(2)}, u32[]{:S(2)}) collective-permute-start(bf16[80,768]{1,0:T(8,128)(2,1)} %pack_front.1), channel_id=1, source_target_pairs={{0,24},{1,25},{2,26},{3,27},{4,28},{5,29},{6,30},{7,31},{8,0},{9,1... | collective-permute-start | bytes 368648 | tf_op jit(solution)/shard_map/ppermute | solution.py:393
  27.0 14.2 %collective-permute-start.3 = (bf16[4,80,768]{2,1,0:T(8,128)(2,1)S(1)}, bf16[4,80,768]{2,1,0:T(8,128)(2,1)S(1)}, u32[]{:S(2)}, u32[]{:S(2)}) collective-permute-start(bf16[4,80,768]{2,1,0:T(8,128)(2,1)S(1)} %pad_maximum_fusion.refs_0_), channel_id=1, source_target_pairs={{0,2},{1,3},{2,0},{3,1},{4,6},{5,7},{6,4},{7,5},{8,10},{9,11},{10,... | collective-permute-start | bytes 1474568 | tf_op jit(solution)/shard_map/ppermute | solution.py:393
  28.6 21.3 %collective-permute-start.4 = (bf16[4,80,768]{2,1,0:T(8,128)(2,1)S(1)}, bf16[4,80,768]{2,1,0:T(8,128)(2,1)S(1)}, u32[]{:S(2)}, u32[]{:S(2)}) collective-permute-start(bf16[4,80,768]{2,1,0:T(8,128)(2,1)S(1)} %pad_maximum_fusion.refs_0_), channel_id=1, source_target_pairs={{0,4},{1,5},{2,6},{3,7},{4,0},{5,1},{6,2},{7,3},{8,12},{9,13},{10,... | collective-permute-start | bytes 1474568 | tf_op jit(solution)/shard_map/ppermute | solution.py:393
  30.1 28.5 %collective-permute-start.5 = (bf16[4,80,768]{2,1,0:T(8,128)(2,1)S(1)}, bf16[4,80,768]{2,1,0:T(8,128)(2,1)S(1)}, u32[]{:S(2)}, u32[]{:S(2)}) collective-permute-start(bf16[4,80,768]{2,1,0:T(8,128)(2,1)S(1)} %pad_maximum_fusion.refs_0_), channel_id=1, source_target_pairs={{0,6},{1,7},{2,4},{3,5},{4,2},{5,3},{6,0},{7,1},{8,14},{9,15},{10,... | collective-permute-start | bytes 1474568 | tf_op jit(solution)/shard_map/ppermute | solution.py:393
  30.6 28.8 %collective-permute-start.6 = (bf16[4,80,768]{2,1,0:T(8,128)(2,1)S(1)}, bf16[4,80,768]{2,1,0:T(8,128)(2,1)}, u32[]{:S(2)}, u32[]{:S(2)}) collective-permute-start(bf16[4,80,768]{2,1,0:T(8,128)(2,1)S(1)} %pad_maximum_fusion.refs_0_), channel_id=1, source_target_pairs={{0,1},{1,0},{2,3},{3,2},{4,5},{5,4},{6,7},{7,6},{8,9},{9,8},{10,11... | collective-permute-start | bytes 1474568 | tf_op jit(solution)/shard_map/ppermute | solution.py:393
  41.2 18.2 %collective-permute-start.7 = (bf16[4,80,768]{2,1,0:T(8,128)(2,1)S(1)}, bf16[4,80,768]{2,1,0:T(8,128)(2,1)}, u32[]{:S(2)}, u32[]{:S(2)}) collective-permute-start(bf16[4,80,768]{2,1,0:T(8,128)(2,1)S(1)} %collective-permute-done.3.refs_1_), channel_id=1, source_target_pairs={{0,1},{1,0},{2,3},{3,2},{4,5},{5,4},{6,7},{7,6},{8,9},{9,8},{10,11... | collective-permute-start | bytes 1474568 | tf_op jit(solution)/shard_map/ppermute | solution.py:393
  49.8 9.6 %collective-permute-start.8 = (bf16[4,80,768]{2,1,0:T(8,128)(2,1)S(1)}, bf16[4,80,768]{2,1,0:T(8,128)(2,1)}, u32[]{:S(2)}, u32[]{:S(2)}) collective-permute-start(bf16[4,80,768]{2,1,0:T(8,128)(2,1)S(1)} %collective-permute-done.4.refs_2_), channel_id=1, source_target_pairs={{0,1},{1,0},{2,3},{3,2},{4,5},{5,4},{6,7},{7,6},{8,9},{9,8},{10,11... | collective-permute-start | bytes 1474568 | tf_op jit(solution)/shard_map/ppermute | solution.py:393
  58.6 2.0 collective-permute-start.9
  59.4 130.7 %copy-start.8 = (s32[4]{0:T(128)}, s32[4]{0:T(128)S(1)}, u32[]{:S(2)}) copy-start(s32[4]{0:T(128)S(1)} %pad_add_fusion.place_ref) | copy-start | bytes 52
  71.1 0.6 copy-start.10
  71.8 0.6 copy-start.11
  159.3 1.4 copy-start.13
  160.7 1.4 copy-start.14
  162.1 1.4 copy-start.15
  163.5 11.2 %copy-start.12 = (bf16[1024,768]{1,0:T(8,128)(2,1)S(1)}, bf16[1024,768]{1,0:T(8,128)(2,1)}, u32[]{:S(2)}) copy-start(bf16[1024,768]{1,0:T(8,128)(2,1)} %get-tuple-element.77.right_ref) | copy-start | bytes 4718596
  174.5 15.6 %collective-permute-start.11 = (bf16[16,5,24,768]{3,2,1,0:T(8,128)(2,1)}, bf16[16,5,24,768]{3,2,1,0:T(8,128)(2,1)S(1)}, u32[]{:S(2)}, u32[]{:S(2)}) collective-permute-start(bf16[16,5,24,768]{3,2,1,0:T(8,128)(2,1)} %get-tuple-element.80), channel_id=1, source_target_pairs={{0,1},{1,0},{2,3},{3,2},{4,5},{5,4},{6,7},{7,6},{8,9},{9,8},{10,11... | collective-permute-start | bytes 8847368 | tf_op jit(solution)/shard_map/ppermute | solution.py:393
  184.0 1.4 copy-start
  185.4 4.7 %collective-permute-start.10 = (bf16[16,96,768]{2,1,0:T(8,128)(2,1)}, bf16[16,96,768]{2,1,0:T(8,128)(2,1)S(1)}, u32[]{:S(2)}, u32[]{:S(2)}) collective-permute-start(bf16[16,96,768]{2,1,0:T(8,128)(2,1)} %get-tuple-element.79), channel_id=1, source_target_pairs={{0,1},{1,0},{2,3},{3,2},{4,5},{5,4},{6,7},{7,6},{8,9},{9,8},{10,11... | collective-permute-start | bytes 7077896 | tf_op jit(solution)/shard_map/ppermute | solution.py:393
  190.1 1.4 copy-start.17
  190.1 2.3 copy-start.16
  198.0 55.0 %collective-permute-start.17 = (bf16[4,216,768]{2,1,0:T(8,128)(2,1)S(1)}, bf16[4,216,768]{2,1,0:T(8,128)(2,1)S(1)}, u32[]{:S(2)}, u32[]{:S(2)}) collective-permute-start(bf16[4,216,768]{2,1,0:T(8,128)(2,1)S(1)} %get-tuple-element.81), channel_id=1, source_target_pairs={{0,2},{1,3},{2,0},{3,1},{4,6},{5,7},{6,4},{7,5},{8,10},{9,11},{10,... | collective-permute-start | bytes 3981320 | tf_op jit(solution)/shard_map/ppermute | solution.py:393
  199.5 59.5 %collective-permute-start.18 = (bf16[4,216,768]{2,1,0:T(8,128)(2,1)S(1)}, bf16[4,216,768]{2,1,0:T(8,128)(2,1)S(1)}, u32[]{:S(2)}, u32[]{:S(2)}) collective-permute-start(bf16[4,216,768]{2,1,0:T(8,128)(2,1)S(1)} %get-tuple-element.82), channel_id=1, source_target_pairs={{0,4},{1,5},{2,6},{3,7},{4,0},{5,1},{6,2},{7,3},{8,12},{9,13},{10,... | collective-permute-start | bytes 3981320 | tf_op jit(solution)/shard_map/ppermute | solution.py:393
  200.1 58.9 %collective-permute-start.19 = (bf16[4,216,768]{2,1,0:T(8,128)(2,1)S(1)}, bf16[4,216,768]{2,1,0:T(8,128)(2,1)}, u32[]{:S(2)}, u32[]{:S(2)}) collective-permute-start(bf16[4,216,768]{2,1,0:T(8,128)(2,1)S(1)} %get-tuple-element.83), channel_id=1, source_target_pairs={{0,6},{1,7},{2,4},{3,5},{4,2},{5,3},{6,0},{7,1},{8,14},{9,15},{10,... | collective-permute-start | bytes 3981320 | tf_op jit(solution)/shard_map/ppermute | solution.py:393
  259.0 1.1 copy-start.18
  260.0 8.0 %copy-start.1 = (bf16[16,80,768]{2,1,0:T(8,128)(2,1)S(1)}, bf16[16,80,768]{2,1,0:T(8,128)(2,1)}, u32[]{:S(2)}) copy-start(bf16[16,80,768]{2,1,0:T(8,128)(2,1)} %get-tuple-element.89.refs_0_) | copy-start | bytes 5898244
  260.0 8.0 %copy-start.9 = (s32[4]{0:T(128)S(1)}, s32[4]{0:T(128)}, u32[]{:S(2)}) copy-start(s32[4]{0:T(128)} %copy-done.8) | copy-start | bytes 52
  263.7 10.9 %copy-start.2 = (bf16[1024,768]{1,0:T(8,128)(2,1)S(1)}, bf16[1024,768]{1,0:T(8,128)(2,1)}, u32[]{:S(2)}) copy-start(bf16[1024,768]{1,0:T(8,128)(2,1)} %get-tuple-element.86.refs_0_) | copy-start | bytes 4718596
  263.7 4.2 %collective-permute-start.12 = (bf16[16,80,768]{2,1,0:T(8,128)(2,1)}, bf16[16,80,768]{2,1,0:T(8,128)(2,1)S(1)}, u32[]{:S(2)}, u32[]{:S(2)}) collective-permute-start(bf16[16,80,768]{2,1,0:T(8,128)(2,1)} %get-tuple-element.90), channel_id=1, source_target_pairs={{0,1},{1,0},{2,3},{3,2},{4,5},{5,4},{6,7},{7,6},{8,9},{9,8},{10,11... | collective-permute-start | bytes 5898248 | tf_op jit(solution)/shard_map/ppermute | solution.py:393
  270.3 0.8 copy-start.6
  271.1 14.4 %collective-permute-start.13 = (bf16[4,80,768]{2,1,0:T(8,128)(2,1)}, bf16[4,80,768]{2,1,0:T(8,128)(2,1)S(1)}, u32[]{:S(2)}, u32[]{:S(2)}) collective-permute-start(bf16[4,80,768]{2,1,0:T(8,128)(2,1)} %get-tuple-element.91), channel_id=1, source_target_pairs={{0,2},{1,3},{2,0},{3,1},{4,6},{5,7},{6,4},{7,5},{8,10},{9,11},{10,... | collective-permute-start | bytes 1474568 | tf_op jit(solution)/shard_map/ppermute | solution.py:393
  271.7 23.7 %collective-permute-start.14 = (bf16[4,80,768]{2,1,0:T(8,128)(2,1)}, bf16[4,80,768]{2,1,0:T(8,128)(2,1)S(1)}, u32[]{:S(2)}, u32[]{:S(2)}) collective-permute-start(bf16[4,80,768]{2,1,0:T(8,128)(2,1)} %get-tuple-element.92), channel_id=1, source_target_pairs={{0,4},{1,5},{2,6},{3,7},{4,0},{5,1},{6,2},{7,3},{8,12},{9,13},{10,... | collective-permute-start | bytes 1474568 | tf_op jit(solution)/shard_map/ppermute | solution.py:393
  273.2 22.3 %collective-permute-start.15 = (bf16[4,80,768]{2,1,0:T(8,128)(2,1)}, bf16[4,80,768]{2,1,0:T(8,128)(2,1)S(1)}, u32[]{:S(2)}, u32[]{:S(2)}) collective-permute-start(bf16[4,80,768]{2,1,0:T(8,128)(2,1)} %get-tuple-element.93), channel_id=1, source_target_pairs={{0,6},{1,7},{2,4},{3,5},{4,2},{5,3},{6,0},{7,1},{8,14},{9,15},{10,... | collective-permute-start | bytes 1474568 | tf_op jit(solution)/shard_map/ppermute | solution.py:393
  274.6 1.4 copy-start.3
  276.0 1.4 copy-start.4
  277.4 18.0 %copy-start.7 = (bf16[4,80,768]{2,1,0:T(8,128)(2,1)S(1)}, bf16[4,80,768]{2,1,0:T(8,128)(2,1)}, u32[]{:S(2)}) copy-start(bf16[4,80,768]{2,1,0:T(8,128)(2,1)} %copy-done.6) | copy-start | bytes 1474564
  295.6 8.8 %collective-permute-start.16 = (bf16[80,768]{1,0:T(8,128)(2,1)S(1)}, bf16[80,768]{1,0:T(8,128)(2,1)S(1)}, u32[]{:S(2)}, u32[]{:S(2)}) collective-permute-start(bf16[80,768]{1,0:T(8,128)(2,1)S(1)} %get-tuple-element.107), channel_id=1, source_target_pairs={{0,8},{1,9},{2,10},{3,11},{4,12},{5,13},{6,14},{7,15},{8,16},{9,17... | collective-permute-start | bytes 368648 | tf_op jit(solution)/shard_map/ppermute | solution.py:393
  296.9 10.3 %collective-permute-start.20 = (bf16[80,768]{1,0:T(8,128)(2,1)S(1)}, bf16[80,768]{1,0:T(8,128)(2,1)S(1)}, u32[]{:S(2)}, u32[]{:S(2)}) collective-permute-start(bf16[80,768]{1,0:T(8,128)(2,1)S(1)} %get-tuple-element.109), channel_id=1, source_target_pairs={{0,16},{1,17},{2,18},{3,19},{4,20},{5,21},{6,22},{7,23},{8,24},{9,... | collective-permute-start | bytes 368648 | tf_op jit(solution)/shard_map/ppermute | solution.py:393
  298.0 9.2 %collective-permute-start.21 = (bf16[80,768]{1,0:T(8,128)(2,1)S(1)}, bf16[80,768]{1,0:T(8,128)(2,1)S(1)}, u32[]{:S(2)}, u32[]{:S(2)}) collective-permute-start(bf16[80,768]{1,0:T(8,128)(2,1)S(1)} %get-tuple-element.108), channel_id=1, source_target_pairs={{0,24},{1,25},{2,26},{3,27},{4,28},{5,29},{6,30},{7,31},{8,0},{9,1... | collective-permute-start | bytes 368648 | tf_op jit(solution)/shard_map/ppermute | solution.py:393
Sparse Core Ops, SparseCore 0:
  11.5 101.8 all-gather.1
  263.8 30.0 reduce-scatter.1

commit v3 on v2

--- a/solution.py
+++ b/solution.py
@@ -17,7 +17,7 @@
 ROOT_HALF = 0.7071067811865476
 INV_ROOT_TWO_PI = 0.3989422804014327
 LAST_LAST = (((1,), (1,)), ((), ()))
-VMEM_BYTES = 56 * 2**20
+VMEM_BYTES = 60 * 2**20
 
 
 def norm_forward(values_in, gain, shift):
@@ -57,145 +57,118 @@
     return segment
 
 
-def attention_forward_kernel(bounds_ref, q_ref, k_ref, v_ref, mixed_ref, logsum_ref, *, span, scale):
+def attention_forward_kernel(bounds_ref, q_ref, k_ref, v_ref, mixed_ref, probs_ref, *, scale):
     rows = q_ref.shape[0]
     first_head = lax.broadcasted_iota(jnp.int32, (1, PAIR), 1) < DH
-    key_segment = segment_at(lax.broadcasted_iota(jnp.int32, (1, rows), 1), bounds_ref)
     keys = k_ref[...]
-    values = v_ref[...]
-    for block in range(rows // span):
-        here = pl.ds(block * span, span)
-        queries = q_ref[here, :] * jnp.asarray(scale, BF)
-        row = lax.broadcasted_iota(jnp.int32, (span, 1), 0) + block * span
-        same = segment_at(row, bounds_ref) == key_segment
-        mixed = []
-        logsum = []
-        for head in range(2):
-            mine = first_head if head == 0 else jnp.logical_not(first_head)
-            scores = dot_last(jnp.where(mine, queries, jnp.zeros_like(queries)), keys)
-            scores = jnp.where(same, scores, NEG)
-            highest = jnp.max(scores, axis=1, keepdims=True)
-            exps = jnp.exp(scores - highest)
-            total = jnp.sum(exps, axis=1, keepdims=True)
-            mixed.append(dot(exps.astype(BF), values) * (1.0 / total))
-            logsum.append(highest + jnp.log(total))
-        mixed_ref[here, :] = jnp.where(first_head, mixed[0], mixed[1]).astype(BF)
-        turned = jnp.transpose(jnp.where(first_head, logsum[0], logsum[1]))
-        logsum_ref[0, 0:1, here] = turned[0:1]
-        logsum_ref[0, 1:2, here] = turned[DH : DH + 1]
+    values_turned = jnp.transpose(v_ref[...])
+    queries = q_ref[...] * jnp.asarray(scale, BF)
+    same = segment_at(lax.broadcasted_iota(jnp.int32, (rows, 1), 0), bounds_ref) == segment_at(
+        lax.broadcasted_iota(jnp.int32, (1, rows), 1), bounds_ref
+    )
+    mixed = []
+    for head in range(2):
+        mine = first_head if head == 0 else jnp.logical_not(first_head)
+        scores = dot_last(keys, jnp.where(mine, queries, jnp.zeros_like(queries)))
+        scores = jnp.where(same, scores, NEG)
+        highest = jnp.max(scores, axis=0, keepdims=True)
+        exps = jnp.exp(scores - highest)
+        total = jnp.sum(exps, axis=0, keepdims=True)
+        probs = (exps * (1.0 / total)).astype(BF)
+        probs_ref[head] = probs
+        mixed.append(dot(values_turned[DH * head : DH * (head + 1)], probs))
+    mixed_ref[...] = jnp.transpose(jnp.concatenate(mixed, axis=0)).astype(BF)
 
 
 def pair_spec(rows, offset):
-    return pl.BlockSpec((rows, PAIR), lambda pair, bounds: (0, offset + pair))
-
-
-def attention_forward(bounds, stacked, span=512):
+    return pl.BlockSpec((rows, PAIR), lambda pair, *_: (0, offset + pair))
+
+
+def attention_forward(bounds, stacked):
     rows, width = stacked.shape[0], stacked.shape[1] // 3
     pairs = width // PAIR
     return pl.pallas_call(
-        functools.partial(attention_forward_kernel, span=span, scale=1.0 / math.sqrt(DH)),
+        functools.partial(attention_forward_kernel, scale=1.0 / math.sqrt(DH)),
         grid_spec=pltpu.PrefetchScalarGridSpec(
             num_scalar_prefetch=1,
             grid=(pairs,),
             in_specs=[pair_spec(rows, 0), pair_spec(rows, pairs), pair_spec(rows, 2 * pairs)],
             out_specs=[
                 pair_spec(rows, 0),
-                pl.BlockSpec((1, 8, rows), lambda pair, bounds: (pair, 0, 0)),
+                pl.BlockSpec((2, rows, rows), lambda pair, bounds: (pair, 0, 0)),
             ],
         ),
         out_shape=[
             jax.ShapeDtypeStruct((rows, width), BF),
-            jax.ShapeDtypeStruct((pairs, 8, rows), F32),
+            jax.ShapeDtypeStruct((2 * pairs, rows, rows), BF),
         ],
         compiler_params=pltpu.CompilerParams(vmem_limit_bytes=VMEM_BYTES),
         cost_estimate=pl.CostEstimate(
-            flops=4 * rows * rows * width * 4, bytes_accessed=8 * rows * width, transcendentals=0
+            flops=rows * width, bytes_accessed=rows * width, transcendentals=0
         ),
         name="attention_forward",
     )(bounds, stacked, stacked, stacked)
 
 
 def attention_backward_kernel(
-    bounds_ref, q_ref, k_ref, v_ref, mixed_ref, grad_ref, logsum_ref, dq_ref, dk_ref, dv_ref, dk_sum, dv_sum, *, span, scale
+    q_ref, k_ref, v_ref, mixed_ref, grad_ref, probs_ref, dq_ref, dk_ref, dv_ref, *, scale
 ):
-    rows = q_ref.shape[0]
     first_head = lax.broadcasted_iota(jnp.int32, (1, PAIR), 1) < DH
-    key_segment = segment_at(lax.broadcasted_iota(jnp.int32, (rows, 1), 0), bounds_ref)
-    keys = k_ref[...]
     values = v_ref[...]
-    keys_turned = jnp.transpose(keys)
+    keys_turned = jnp.transpose(k_ref[...])
     picks = (
         lax.broadcasted_iota(jnp.int32, (8, PAIR), 1) // DH
         == lax.broadcasted_iota(jnp.int32, (8, PAIR), 0)
     ).astype(F32)
-    for block in range(rows // span):
-        here = pl.ds(block * span, span)
-        queries = q_ref[here, :]
-        grads = grad_ref[here, :]
-        weighted = lax.dot_general(
-            picks,
-            grads.astype(F32) * mixed_ref[here, :].astype(F32),
-            LAST_LAST,
-            preferred_element_type=F32,
-            precision=lax.Precision.HIGHEST,
-        )
-        column = lax.broadcasted_iota(jnp.int32, (1, span), 1) + block * span
-        same = key_segment == segment_at(column, bounds_ref)
-        all_probs, all_scores, all_grads, all_queries, grad_queries = [], [], [], [], []
-        for head in range(2):
-            mine = first_head if head == 0 else jnp.logical_not(first_head)
-            my_queries = jnp.where(mine, queries, jnp.zeros_like(queries)) * jnp.asarray(scale, BF)
-            my_grads = jnp.where(mine, grads, jnp.zeros_like(grads))
-            scores = dot_last(keys, my_queries) - logsum_ref[0, head : head + 1, here]
-            probs = jnp.exp(jnp.where(same, scores, NEG))
-            grad_probs = dot_last(values, my_grads)
-            grad_scores = (probs * (grad_probs - weighted[head : head + 1])).astype(BF)
-            all_probs.append(probs.astype(BF))
-            all_scores.append(grad_scores)
-            all_grads.append(my_grads)
-            all_queries.append(my_queries)
-            grad_queries.append(dot(keys_turned[DH * head : DH * (head + 1)], grad_scores))
-        turned = jnp.concatenate(grad_queries, axis=0) * scale
-        dq_ref[here, :] = jnp.transpose(turned).astype(BF)
-        dv = dot(jnp.concatenate(all_probs, axis=1), jnp.concatenate(all_grads, axis=0))
-        dk = dot(jnp.concatenate(all_scores, axis=1), jnp.concatenate(all_queries, axis=0))
-        if block == 0:
-            dv_sum[...] = dv
-            dk_sum[...] = dk
-        else:
-            dv_sum[...] += dv
-            dk_sum[...] += dk
-    dk_ref[...] = dk_sum[...].astype(BF)
-    dv_ref[...] = dv_sum[...].astype(BF)
-
-
-def attention_backward(bounds, stacked, mixed, grad_mixed, logsum, start=0, count=None, span=256):
+    queries = q_ref[...] * jnp.asarray(scale, BF)
+    grads = grad_ref[...]
+    weighted = lax.dot_general(
+        picks,
+        grads.astype(F32) * mixed_ref[...].astype(F32),
+        LAST_LAST,
+        preferred_element_type=F32,
+        precision=lax.Precision.HIGHEST,
+    )
+    all_scores, all_grads, all_queries, grad_queries = [], [], [], []
+    for head in range(2):
+        mine = first_head if head == 0 else jnp.logical_not(first_head)
+        my_grads = jnp.where(mine, grads, jnp.zeros_like(grads))
+        grad_probs = dot_last(values, my_grads) - weighted[head : head + 1]
+        grad_scores = (probs_ref[head].astype(F32) * grad_probs).astype(BF)
+        all_scores.append(grad_scores)
+        all_grads.append(my_grads)
+        all_queries.append(jnp.where(mine, queries, jnp.zeros_like(queries)))
+        grad_queries.append(dot(keys_turned[DH * head : DH * (head + 1)], grad_scores))
+    turned = jnp.concatenate(grad_queries, axis=0) * scale
+    dq_ref[...] = jnp.transpose(turned).astype(BF)
+    all_probs = jnp.concatenate([probs_ref[0], probs_ref[1]], axis=1)
+    dv_ref[...] = dot(all_probs, jnp.concatenate(all_grads, axis=0)).astype(BF)
+    all_scores = jnp.concatenate(all_scores, axis=1)
+    dk_ref[...] = dot(all_scores, jnp.concatenate(all_queries, axis=0)).astype(BF)
+
+
+def attention_backward(stacked, mixed, grad_mixed, probs):
     rows, width = mixed.shape
     pairs = width // PAIR
-    count = pairs if count is None else count
-    return pl.pallas_call(
-        functools.partial(attention_backward_kernel, span=span, scale=1.0 / math.sqrt(DH)),
-        grid_spec=pltpu.PrefetchScalarGridSpec(
-            num_scalar_prefetch=1,
-            grid=(count,),
-            in_specs=[
-                pair_spec(rows, start),
-                pair_spec(rows, pairs + start),
-                pair_spec(rows, 2 * pairs + start),
-                pair_spec(rows, start),
-                pair_spec(rows, start),
-                pl.BlockSpec((1, 8, rows), lambda pair, bounds: (start + pair, 0, 0)),
-            ],
-            out_specs=[pair_spec(rows, 0), pair_spec(rows, 0), pair_spec(rows, 0)],
-            scratch_shapes=[pltpu.VMEM((rows, PAIR), F32), pltpu.VMEM((rows, PAIR), F32)],
-        ),
-        out_shape=[jax.ShapeDtypeStruct((rows, count * PAIR), BF)] * 3,
+    return pl.pallas_call(
+        functools.partial(attention_backward_kernel, scale=1.0 / math.sqrt(DH)),
+        grid=(pairs,),
+        in_specs=[
+            pair_spec(rows, 0),
+            pair_spec(rows, pairs),
+            pair_spec(rows, 2 * pairs),
+            pair_spec(rows, 0),
+            pair_spec(rows, 0),
+            pl.BlockSpec((2, rows, rows), lambda pair: (pair, 0, 0)),
+        ],
+        out_specs=[pair_spec(rows, 0), pair_spec(rows, 0), pair_spec(rows, 0)],
+        out_shape=[jax.ShapeDtypeStruct((rows, width), BF)] * 3,
         compiler_params=pltpu.CompilerParams(vmem_limit_bytes=VMEM_BYTES),
         cost_estimate=pl.CostEstimate(
-            flops=40 * rows * rows * count * PAIR, bytes_accessed=16 * rows * count * PAIR, transcendentals=0
+            flops=rows * width, bytes_accessed=rows * width, transcendentals=0
         ),
         name="attention_backward",
-    )(bounds, stacked, stacked, stacked, mixed, grad_mixed, logsum)
+    )(stacked, stacked, stacked, mixed, grad_mixed, probs)
 
 
 def general_layer(
@@ -263,7 +236,7 @@
     projected = jnp.dot(hidden, whole_qkv, preferred_element_type=F32)
     whole_bias = jnp.concatenate([whole_bias_q, jnp.zeros_like(whole_bias_q), whole_bias_v])
     stacked = (projected + whole_bias).astype(BF)
-    mixed, logsum = attention_forward(bounds, stacked)
+    mixed, probs = attention_forward(bounds, stacked)
     branch = jnp.dot(mixed, whole_out, preferred_element_type=F32) + whole_bias_out
     first, normed_one, rstd_one = norm_forward(
         hidden.astype(F32) + branch, whole_gain_one, whole_shift_one
@@ -323,7 +296,7 @@
     my_down = summed[part * (1 + wide) :]
 
     grad_stack = jnp.concatenate(
-        attention_backward(bounds, stacked, mixed, grad_mixed, logsum), axis=1
+        attention_backward(stacked, mixed, grad_mixed, probs), axis=1
     )
     grad_w_qkv = jnp.einsum("rd,re->de", hidden, grad_stack, preferred_element_type=F32)
     stack_sums = jnp.sum(grad_stack.astype(F32), axis=0)
@@ -477,7 +450,7 @@
             out_specs=[pl.BlockSpec((1, sum(sizes), width), lambda step, place: (step, 0, 0))] * 4,
         ),
         out_shape=[out] * 4,
-        compiler_params=params(48),
+        compiler_params=params(24),
         cost_estimate=pl.CostEstimate(
             flops=out.size, bytes_accessed=out.size, transcendentals=0
         ),
@@ -485,15 +458,120 @@
     )(place, *(array for pair in pairs for array in pair))
 
 
+def first_sum_kernel(place_ref, *refs, cuts):
+    keep_ref, by_x_ref, by_y_ref = refs[2 * len(cuts) :]
+    _, ys, xs, _ = CHIPS
+    y, x = place_ref[1], place_ref[2]
+    low = pl.program_id(0) < CHIPS[0] // 2
+
+    def total(pair, chip):
+        return (refs[2 * pair][chip].astype(F32) + refs[2 * pair + 1][chip].astype(F32)).astype(BF)
+
+    for other in range(2):
+        mine = jnp.where(low, other * xs + x, y * xs + other)
+        theirs = jnp.where(low, other * xs + (x + 1) % xs, (y + 1) % ys * xs + other)
+        for pair, (start, size) in enumerate(cuts):
+            rows = slice(start, start + size)
+            keep_ref[0, other, rows, :] = total(pair, mine)
+
+            @pl.when(low)
+            def _():
+                by_x_ref[0, other, rows, :] = total(pair, theirs)
+
+            @pl.when(jnp.logical_not(low))
+            def _():
+                by_y_ref[0, other, rows, :] = total(pair, theirs)
+
+
+def halves(block):
+    half = CHIPS[0] // 2
+    rest = (0,) * (len(block) - 1)
+    low = pl.BlockSpec(block, lambda step, place: (jnp.minimum(step, half - 1),) + rest)
+    high = pl.BlockSpec(block, lambda step, place: (jnp.maximum(step - half, 0),) + rest)
+    return low, high
+
+
+def first_sum(place, *pairs):
+    zs, ys, xs, _ = CHIPS
+    sizes = [keep.shape[1] for keep, _ in pairs]
+    cuts = [(sum(sizes[:i]), size) for i, size in enumerate(sizes)]
+    width = pairs[0][0].shape[2]
+    block = (1, 2, sum(sizes), width)
+    keep = jax.ShapeDtypeStruct((zs,) + block[1:], BF)
+    send = jax.ShapeDtypeStruct((zs // 2,) + block[1:], BF)
+    return pl.pallas_call(
+        functools.partial(first_sum_kernel, cuts=cuts),
+        grid_spec=pltpu.PrefetchScalarGridSpec(
+            num_scalar_prefetch=1,
+            grid=(zs,),
+            in_specs=[
+                pl.BlockSpec((ys * xs, size, width), lambda step, place: (step, 0, 0))
+                for size in sizes
+                for _ in range(2)
+            ],
+            out_specs=[pl.BlockSpec(block, lambda step, place: (step, 0, 0, 0)), *halves(block)],
+        ),
+        out_shape=[keep, send, send],
+        compiler_params=params(24),
+        cost_estimate=pl.CostEstimate(flops=keep.size, bytes_accessed=keep.size, transcendentals=0),
+        name="first_sum",
+    )(place, *(array for pair in pairs for array in pair))
+
+
+def second_sum_kernel(place_ref, keep_ref, from_x_ref, from_y_ref, own_ref, by_y_ref, by_x_ref):
+    low = pl.program_id(0) < CHIPS[0] // 2
+
+    def go(came_ref, own, send_ref):
+        def total(index):
+            return (keep_ref[0, index].astype(F32) + came_ref[0, index].astype(F32)).astype(BF)
+
+        own_ref[0] = total(own)
+        send_ref[0] = total(1 - own)
+
+    @pl.when(low)
+    def _():
+        go(from_x_ref, place_ref[1], by_y_ref)
+
+    @pl.when(jnp.logical_not(low))
+    def _():
+        go(from_y_ref, place_ref[2], by_x_ref)
+
+
+def second_sum(place, keep, from_x, from_y):
+    zs = CHIPS[0]
+    block = (1,) + keep.shape[2:]
+    own = jax.ShapeDtypeStruct((zs,) + block[1:], BF)
+    send = jax.ShapeDtypeStruct((zs // 2,) + block[1:], BF)
+    return pl.pallas_call(
+        second_sum_kernel,
+        grid_spec=pltpu.PrefetchScalarGridSpec(
+            num_scalar_prefetch=1,
+            grid=(zs,),
+            in_specs=[
+                pl.BlockSpec((1,) + keep.shape[1:], lambda step, place: (step, 0, 0, 0)),
+                *halves((1,) + keep.shape[1:]),
+            ],
+            out_specs=[pl.BlockSpec(block, lambda step, place: (step, 0, 0)), *halves(block)],
+        ),
+        out_shape=[own, send, send],
+        compiler_params=params(24),
+        cost_estimate=pl.CostEstimate(flops=own.size, bytes_accessed=own.size, transcendentals=0),
+        name="second_sum",
+    )(place, keep, from_x, from_y)
+
+
 def send_near(sends):
     return [moved(array, step) for array, step in zip(sends, NEAR)]
 
 
-def far_sum(parts):
+def far_add(own, low, high):
+    return (own.astype(F32) + jnp.concatenate([low, high]).astype(F32)).astype(BF)
+
+
+def far_scatter(total):
     zs, ys, xs, cores = CHIPS
     across = ys * xs * cores
     groups = [[level * across + i for level in range(zs)] for i in range(across)]
-    total = sum(part.astype(F32) for part in parts).astype(BF)
     return lax.psum_scatter(
         total, "fsdp", scatter_dimension=0, axis_index_groups=groups, tiled=False
     ).astype(F32)
@@ -533,8 +611,8 @@
 def project_kernel(
     place_ref, hidden_ref, *refs, part, inner_part
 ):
-    pieces = refs[: len(refs) - 4]
-    stacked_ref, weight_ref, vector_ref, up_ref = refs[len(refs) - 4 :]
+    pieces = refs[: len(refs) - 5]
+    stacked_ref, weight_ref, vector_ref, up_ref, turned_ref = refs[len(refs) - 5 :]
     z, y, x, core = (place_ref[i] for i in range(4))
     zs, ys, xs, cores = CHIPS
     width = hidden_ref.shape[1]
@@ -566,6 +644,7 @@
     vector_ref[...] = vectors
     up_ref[...] = ups
     hidden = hidden_ref[...]
+    turned_ref[...] = jnp.transpose(hidden)
     for third, bias in ((0, vectors[0:1]), (1, None), (2, vectors[1:2])):
         cut = slice(third * width, (third + 1) * width)
         projected = dot(hidden, weight_ref[:, cut])
@@ -579,6 +658,7 @@
         jax.ShapeDtypeStruct((width, 3 * width), BF),
         jax.ShapeDtypeStruct((8, width), F32),
         jax.ShapeDtypeStruct((8, hidden_units), F32),
+        jax.ShapeDtypeStruct((width, rows), BF),
     ]
     return pl.pallas_call(
         functools.partial(project_kernel, part=width // count, inner_part=hidden_units // count),
@@ -617,8 +697,7 @@
 
 def row_pass_kernel(
     bounds_ref, mixed_ref, hidden_ref, cotangent_ref, vector_ref, bias_up_ref, gathered_ref,
-    output_ref, first_turned_ref, mixed_turned_ref, activated_turned_ref, grad_second_ref,
-    grad_inner_ref, grad_sum_ref, grad_branch_ref, grad_mixed_ref, sums_ref, up_sums_ref,
+    output_ref, left_ref, right_ref, grad_sum_ref, grad_mixed_ref, sums_ref, up_sums_ref,
     w_out, w_up, w_down, staged, slope, sems, *, part, chunk
 ):
     step = pl.program_id(0)
@@ -627,18 +706,26 @@
     hidden_units = w_up.shape[1]
     wide = hidden_units // width
 
+    batch = count // 4
+    copies = [
+        pltpu.make_async_copy(
+            gathered_ref.at[pl.ds(start, batch), pl.ds(inner_part, staged.shape[1])],
+            staged.at[pl.ds(start, batch)],
+            sems.at[1 + start // batch],
+        )
+        for start in range(0, count, batch)
+    ]
+    down_copy = pltpu.make_async_copy(
+        gathered_ref.at[:, pl.ds(0, inner_part)], w_down, sems.at[0]
+    )
+
     @pl.when(step == 0)
     def _():
-        narrow = pltpu.make_async_copy(
-            gathered_ref.at[:, pl.ds(inner_part, staged.shape[1]), :], staged, sems.at[0]
-        )
-        down = pltpu.make_async_copy(
-            gathered_ref.at[:, pl.ds(0, inner_part), :], w_down, sems.at[1]
-        )
-        narrow.start()
-        down.start()
-        narrow.wait()
+        for copy in copies + [down_copy]:
+            copy.start()
         for pair in range(count // 2):
+            if 2 * pair % batch == 0:
+                copies[2 * pair // batch].wait()
             low = staged[2 * pair].astype(F32)
             high = staged[2 * pair + 1].astype(F32)
             rows = slice(2 * pair * part, 2 * (pair + 1) * part)
@@ -649,7 +736,6 @@
                     w_up[rows, group * width : (group + 1) * width] = both
                 else:
                     w_out[rows, :] = both
-        down.wait()
 
     def down_rows(cut):
         owners = slice(cut.start // inner_part, cut.stop // inner_part)
@@ -664,8 +750,8 @@
         hidden_ref[...].astype(F32) + branch, gain_one, shift_one
     )
     first_low = first.astype(BF)
-    first_turned_ref[...] = jnp.transpose(first_low)
-    mixed_turned_ref[...] = jnp.transpose(mixed)
+    left_ref[hidden_units : hidden_units + width, :] = jnp.transpose(first_low)
+    left_ref[hidden_units + width :, :] = jnp.transpose(mixed)
     cuts = [slice(start, start + chunk) for start in range(0, hidden_units, chunk)]
     second = jnp.zeros(first.shape, F32)
     for cut in cuts:
@@ -673,7 +759,13 @@
         activated, slopes = gelu_and_slope(inner)
         activated = activated.astype(BF)
         slope[:, cut] = slopes
-        activated_turned_ref[cut, :] = jnp.transpose(activated)
+        left_ref[cut, :] = jnp.transpose(activated)
+        if cut.start == 0:
+
+            @pl.when(step == 0)
+            def _():
+                down_copy.wait()
+
         second += dot(activated, down_rows(cut))
     result, normed_two, rstd_two = norm_forward(
         first + (second + bias_down), gain_two, shift_two
@@ -684,19 +776,19 @@
     upstream = cotangent_ref[...].astype(F32) * present
     grad_second = norm_back(upstream, normed_two, rstd_two, gain_two)
     grad_second_low = grad_second.astype(BF)
-    grad_second_ref[...] = grad_second_low
+    right_ref[:, :width] = grad_second_low
     grad_first = grad_second
     up_sums = []
     for cut in cuts:
         grad_activated = dot_last(grad_second_low, down_rows(cut))
         grad_inner = (grad_activated * slope[:, cut]).astype(BF)
-        grad_inner_ref[:, cut] = grad_inner
+        right_ref[:, width + cut.start : width + cut.stop] = grad_inner
         up_sums.append(column_sum(grad_inner.astype(F32)))
         grad_first += dot_last(grad_inner, w_up[:, cut])
     grad_sum = norm_back(grad_first, normed_one, rstd_one, gain_one)
     grad_sum_ref[...] = grad_sum
     grad_branch = grad_sum.astype(BF)
-    grad_branch_ref[...] = grad_branch
+    right_ref[:, width + hidden_units :] = grad_branch
     grad_mixed_ref[...] = dot_last(grad_branch, w_out[...]).astype(BF)
     sums = jnp.concatenate(
         [
@@ -731,7 +823,7 @@
     count = gathered.shape[0]
     part = width // count
     row_spec = pl.BlockSpec((span, width), lambda step, bounds: (step, 0))
-    turned_spec = pl.BlockSpec((width, span), lambda step, bounds: (0, step))
+    stacked = hidden_units + 2 * width
     shape = jax.ShapeDtypeStruct
     sums = shape((8, width), F32)
     up_sums = shape((8, hidden_units), F32)
@@ -751,12 +843,8 @@
             ],
             out_specs=[
                 row_spec,
-                turned_spec,
-                turned_spec,
-                pl.BlockSpec((hidden_units, span), lambda step, bounds: (0, step)),
-                row_spec,
-                pl.BlockSpec((span, hidden_units), lambda step, bounds: (step, 0)),
-                row_spec,
+                pl.BlockSpec((stacked, span), lambda step, bounds: (0, step)),
+                pl.BlockSpec((span, stacked), lambda step, bounds: (step, 0)),
                 row_spec,
                 row_spec,
                 whole_block(sums),
@@ -768,18 +856,14 @@
                 pltpu.VMEM((count, inner_part, width), BF),
                 pltpu.VMEM((count, staged_rows, width), BF),
                 pltpu.VMEM((span, hidden_units), F32),
-                pltpu.SemaphoreType.DMA((2,)),
+                pltpu.SemaphoreType.DMA((5,)),
             ],
         ),
         out_shape=[
             shape((rows, width), F32),
-            shape((width, rows), BF),
-            shape((width, rows), BF),
-            shape((hidden_units, rows), BF),
-            shape((rows, width), BF),
-            shape((rows, hidden_units), BF),
+            shape((stacked, rows), BF),
+            shape((rows, stacked), BF),
             shape((rows, width), F32),
-            shape((rows, width), BF),
             shape((rows, width), BF),
             sums,
             up_sums,
@@ -795,13 +879,11 @@
 
 
 def split_owners(place_ref, keep_ref, send_ref, tile_of, count, lead=()):
-    for core in range(2):
-
-        @pl.when(place_ref[3] == core)
-        def _():
-            for owner in range(count):
-                target = keep_ref if owner % 2 == core else send_ref
-                target[(owner // 2,) + lead] = tile_of(owner).astype(BF)
+    first = place_ref[3] == 0
+    for chip in range(count // 2):
+        even, odd = tile_of(2 * chip), tile_of(2 * chip + 1)
+        keep_ref[(chip,) + lead] = jnp.where(first, even, odd).astype(BF)
+        send_ref[(chip,) + lead] = jnp.where(first, odd, even).astype(BF)
 
 
 def down_grad_kernel(place_ref, left_ref, right_ref, keep_ref, send_ref):
@@ -811,10 +893,10 @@
     split_owners(place_ref, keep_ref, send_ref, lambda o: product[o * part : (o + 1) * part], count)
 
 
-def down_grad(place, left, right, count, steps=4):
-    tall, rows = left.shape
-    width = right.shape[1]
-    part = tall // count
+def down_grad(place, left, right, width, count):
+    rows = left.shape[1]
+    steps = left.shape[0] // width - 2
+    part = steps * width // count
     half = count // 2
     spec = pl.BlockSpec((half // steps, part, width), lambda step, place: (step, 0, 0))
     return pl.pallas_call(
@@ -823,42 +905,32 @@
             num_scalar_prefetch=1,
             grid=(steps,),
             in_specs=[
-                pl.BlockSpec((tall // steps, rows), lambda step, place: (step, 0)),
-                whole_block(right),
+                pl.BlockSpec((width, rows), lambda step, place: (step, 0)),
+                pl.BlockSpec((rows, width), lambda step, place: (0, 0)),
             ],
             out_specs=[spec, spec],
         ),
         out_shape=[jax.ShapeDtypeStruct((half, part, width), BF)] * 2,
         compiler_params=params(48),
         cost_estimate=pl.CostEstimate(
-            flops=2 * rows * width * tall, bytes_accessed=4 * tall * rows, transcendentals=0
+            flops=rows * width, bytes_accessed=rows * width, transcendentals=0
         ),
         name="grad_w_down",
     )(place, left, right)
 
 
-def up_grad_kernel(place_ref, first_ref, mixed_ref, inner_ref, branch_ref, keep_ref, send_ref):
-    step = pl.program_id(0)
+def up_grad_kernel(place_ref, left_ref, right_ref, keep_ref, send_ref):
     part = keep_ref.shape[2]
-
-    def go(product):
-        count = product.shape[0] // part
-        split_owners(
-            place_ref, keep_ref, send_ref, lambda o: product[o * part : (o + 1) * part], count, (0,)
-        )
-
-    @pl.when(step < pl.num_programs(0) - 1)
-    def _():
-        go(dot(first_ref[...], inner_ref[...]))
-
-    @pl.when(step == pl.num_programs(0) - 1)
-    def _():
-        go(dot(mixed_ref[...], branch_ref[...]))
-
-
-def up_grad(place, first_turned, mixed_turned, grad_inner, grad_branch, count):
-    width, rows = first_turned.shape
-    wide = grad_inner.shape[1] // width
+    product = dot(left_ref[...], right_ref[...])
+    count = product.shape[0] // part
+    split_owners(
+        place_ref, keep_ref, send_ref, lambda o: product[o * part : (o + 1) * part], count, (0,)
+    )
+
+
+def up_grad(place, left, right, width, count):
+    rows = left.shape[1]
+    wide = left.shape[0] // width - 2
     half, part = count // 2, width // count
     spec = pl.BlockSpec((half, 1, part, width), lambda step, place: (0, step, 0, 0))
     return pl.pallas_call(
@@ -867,30 +939,26 @@
             num_scalar_prefetch=1,
             grid=(wide + 1,),
             in_specs=[
-                whole_block(first_turned),
-                whole_block(mixed_turned),
-                pl.BlockSpec((rows, width), lambda step, place: (0, jnp.minimum(step, wide - 1))),
-                whole_block(grad_branch),
+                pl.BlockSpec((width, rows), lambda step, place: (wide + step // wide, 0)),
+                pl.BlockSpec((rows, width), lambda step, place: (0, 1 + step)),
             ],
             out_specs=[spec, spec],
         ),
         out_shape=[jax.ShapeDtypeStruct((half, wide + 1, part, width), BF)] * 2,
         compiler_params=params(48),
         cost_estimate=pl.CostEstimate(
-            flops=2 * rows * width * width * (wide + 1),
-            bytes_accessed=4 * rows * width * (wide + 1),
-            transcendentals=0,
+            flops=rows * width, bytes_accessed=rows * width, transcendentals=0
         ),
         name="grad_w_up_out",
-    )(place, first_turned, mixed_turned, grad_inner, grad_branch)
-
-
-def qkv_grad_kernel(place_ref, hidden_ref, sums_ref, up_sums_ref, *refs, part, inner_part):
-    keep_ref, send_ref = refs[-2:]
-    stack = refs[:-2]
+    )(place, left, right)
+
+
+def qkv_grad_kernel(place_ref, turned_ref, sums_ref, up_sums_ref, *refs, part, inner_part):
+    long_refs, short_refs = refs[-4:-2], refs[-2:]
+    stack = refs[:-4]
     each = len(stack) // 3
-    rows, width = hidden_ref.shape
-    turned = jnp.transpose(hidden_ref[...])
+    width, rows = turned_ref.shape
+    turned = turned_ref[...]
     ones = jnp.ones((8, rows), BF)
 
     def joined(left, third):
@@ -920,30 +988,38 @@
             [own[:, :PAIR], jnp.where(top, long[:, :PAIR], 0.0), jnp.zeros((8, width - 2 * PAIR), F32)],
             axis=1,
         )
-        return jnp.concatenate([product[cut] for product in products] + [extra], axis=0)
-
-    split_owners(place_ref, keep_ref, send_ref, tile_of, width // part)
-
-
-def qkv_grad(place, hidden, stack, sums, up_sums, count):
-    rows, width = hidden.shape
+        return jnp.concatenate([products[2][cut], extra], axis=0)
+
+    def long_tile_of(owner):
+        cut = slice(owner * part, (owner + 1) * part)
+        return jnp.concatenate([product[cut] for product in products[:2]], axis=0)
+
+    split_owners(place_ref, *long_refs, long_tile_of, width // part)
+    split_owners(place_ref, *short_refs, tile_of, width // part)
+
+
+def qkv_grad(place, turned, stack, sums, up_sums, count):
+    width, rows = turned.shape
     part = width // count
-    out = jax.ShapeDtypeStruct((count // 2, 3 * part + 8, width), BF)
+    outs = [
+        jax.ShapeDtypeStruct((count // 2, tall, width), BF)
+        for tall in (2 * part, 2 * part, part + 8, part + 8)
+    ]
     return pl.pallas_call(
         functools.partial(qkv_grad_kernel, part=part, inner_part=up_sums.shape[1] // count),
         grid_spec=pltpu.PrefetchScalarGridSpec(
             num_scalar_prefetch=1,
             grid=(1,),
-            in_specs=[whole_block(array) for array in (hidden, sums, up_sums, *stack)],
-            out_specs=[whole_block(out)] * 2,
-        ),
-        out_shape=[out] * 2,
-        compiler_params=params(56),
+            in_specs=[whole_block(array) for array in (turned, sums, up_sums, *stack)],
+            out_specs=[whole_block(out) for out in outs],
+        ),
+        out_shape=outs,
+        compiler_params=params(48),
         cost_estimate=pl.CostEstimate(
-            flops=6 * rows * width * width, bytes_accessed=12 * rows * width, transcendentals=0
+            flops=rows * width, bytes_accessed=rows * width, transcendentals=0
         ),
         name="grad_w_qkv",
-    )(place, hidden, sums, up_sums, *stack)
+    )(place, turned, sums, up_sums, *stack)
 
 
 def hidden_grad_kernel(grad_sum_ref, weight_ref, *refs):
@@ -969,7 +1045,7 @@
         out_shape=jax.ShapeDtypeStruct((rows, width), F32),
         compiler_params=params(48),
         cost_estimate=pl.CostEstimate(
-            flops=6 * rows * width * width, bytes_accessed=14 * rows * width, transcendentals=0
+            flops=rows * width, bytes_accessed=rows * width, transcendentals=0
         ),
         name="grad_hidden",
     )(grad_sum, weight, *stack)
@@ -996,33 +1072,34 @@
     )
     front = pack_front(w_qkv, vectors, bias_up[None])
     mine, others = gather_pieces(front)
-    stacked, whole_qkv, whole_vectors, whole_up_bias = project(
+    stacked, whole_qkv, whole_vectors, whole_up_bias, hidden_turned = project(
         place, hidden, mine + others, hidden_units, n
     )
-    mixed, logsum = attention_forward(bounds, stacked)
-    (
-        output, first_turned, mixed_turned, activated_turned, grad_second, grad_inner, grad_sum,
-        grad_branch, grad_mixed, sums, up_sums,
-    ) = row_pass(
+    mixed, probs = attention_forward(bounds, stacked)
+    output, left, right, grad_sum, grad_mixed, sums, up_sums = row_pass(
         bounds, mixed, hidden, cotangent, whole_vectors, whole_up_bias, gathered, inner_part
     )
     core = (0, 0, 0, 1)
-    up_keep, up_send = up_grad(place, first_turned, mixed_turned, grad_inner, grad_branch, n)
+    up_keep, up_send = up_grad(place, left, right, width, n)
     up_came = moved(up_send, core)
-    down_keep, down_send = down_grad(place, activated_turned, after(grad_second, up_keep), n)
+    down_keep, down_send = down_grad(place, after(left, up_keep), right, width, n)
     down_came = moved(down_send, core)
     up_keep, up_came = (array.reshape(n // 2, -1, width) for array in (up_keep, up_came))
-    here, *sends = near_sum(place, (down_keep, down_came), (up_keep, up_came))
-    parts = [here] + send_near(sends)
-    stack = attention_backward(bounds, stacked, mixed, after(grad_mixed, *sends), logsum)
-    qkv_keep, qkv_send = qkv_grad(place, hidden, stack, sums, up_sums, n)
-    qkv_came = moved(qkv_send, core)
-    total = far_sum([here] + [after(part, qkv_keep) for part in parts[1:]])
-    here, *sends = near_sum(place, (qkv_keep, qkv_came))
+    keep, by_x, by_y = first_sum(place, (down_keep, down_came), (up_keep, up_came))
+    from_x, from_y = moved(by_x, NEAR[0]), moved(by_y, NEAR[1])
+    stack = attention_backward(stacked, mixed, after(grad_mixed, by_x, by_y), probs)
+    own, by_y, by_x = second_sum(place, keep, after(from_x, *stack), after(from_y, *stack))
+    low, high = moved(by_y, NEAR[1]), moved(by_x, NEAR[0])
+    long_keep, long_send, short_keep, short_send = qkv_grad(
+        place, after(hidden_turned, by_x, by_y), stack, sums, up_sums, n
+    )
+    long_came, short_came = moved(long_send, core), moved(short_send, core)
+    here, *sends = near_sum(place, (long_keep, long_came), (short_keep, short_came))
+    total = far_add(own, after(low, *sends), after(high, *sends))
+    grad_hidden = hidden_grad(after(grad_sum, total), whole_qkv, stack)
+    total = far_scatter(total)
     qkv_parts = send_near(sends)
-    grad_hidden = hidden_grad(after(grad_sum, *sends), whole_qkv, stack)
-    qkv_mine, qkv_far = reduce_far([here] + [after(part, grad_hidden) for part in qkv_parts], coords)
-
+    qkv_mine, qkv_far = reduce_far([here] + qkv_parts, coords)
     my_up_out = total[inner_part:].reshape(wide + 1, part, width)
     my_down = total[:inner_part]
     my_up = my_up_out[:wide].transpose(1, 0, 2).reshape(part, hidden_units)

time: 317 us -> 298 us (0.940)
  Pallas kernels: 172 us -> 159 us
  local copies, waits for them, and re-layouts: 19.4 us -> 11.8 us
    pallas_call x2 -> x1, Pallas kernels: 7.87 us -> 1.09 us  [near_sum(): pl.pallas_call(functools.partial(near_sum_kernel, cuts=cuts), grid_spec=p...]
    unnamed x40 -> x32, local copies, waits for them, and re-layouts: 13.9 us -> 7.21 us
    pallas_call x2 -> x4, Pallas kernels: 66.3 us -> 64.6 us  [the longest x1 31.4 us: attention_backward(): pl.pallas_call(functools.partial(attention_backward_kernel, scale=1.0 / m...]
    ppermute x22 -> x24, waiting for transfers between devices: 63.5 us -> 65.2 us  [moved(): return lax.ppermute(array, 'fsdp', pairs)]
    ppermute x22 -> x24, starting transfers between devices: 22.8 us -> 24 us  [moved(): return lax.ppermute(array, 'fsdp', pairs)]
  transfers between devices with their start and end apart: 24 -> 26, of which waited for: 12 -> 15; matrix products, arithmetic and copies ran while one was open for 2% -> 3% of each run, Pallas kernels for 34% -> 29%
where the time goes in v3:
time: 298 us; the launch traced here: 297 us
  Pallas kernels  159 us (53%)
  waiting for transfers between devices  80.3 us (27%)
  starting transfers between devices  24.1 us (8%)
  between operations  14.3 us (5%)
  local copies, waits for them, and re-layouts  11.8 us (4%)
  other arithmetic  7.69 us (3%)
    ppermute x24, waiting for transfers between devices, moved(): return lax.ppermute(array, 'fsdp', pairs)  65.2 us
    pallas_call x1, Pallas kernels, row_pass(): pl.pallas_call(functools.partial(row_pass_kernel, part=part, chunk=chunk)...  46.4 us
    pallas_call x1, Pallas kernels, attention_backward(): pl.pallas_call(functools.partial(attention_backward_kernel, scale=1.0 / m...  31.4 us
    pallas_call x1, Pallas kernels, attention_forward(): pl.pallas_call(functools.partial(attention_forward_kernel, scale=1.0 / ma...  27.2 us
    ppermute x24, starting transfers between devices, moved(): return lax.ppermute(array, 'fsdp', pairs)  24 us
    all_gather x1, waiting for transfers between devices, meshed_layer(): lax.all_gather(pack_weights(w_down, w_up, w_out), 'fsdp', axis=0, tiled=T...  13.4 us
    pallas_call x1, Pallas kernels, up_grad(): pl.pallas_call(up_grad_kernel, grid_spec=pltpu.PrefetchScalarGridSpec(num...  10.3 us
    pallas_call x1, Pallas kernels, project(): pl.pallas_call(functools.partial(project_kernel, part=width // count, inn...  9.9 us
  transfers between devices with their start and end apart: 26, of which 15 were waited for; matrix products, arithmetic and copies ran while one was open for 3% of the time, Pallas kernels for 29%

profile of v3, /device:TPU:0, one launch (start us, length us, event | category | flops | bytes accessed | tf_op | source)
XLA Modules:
  0.0 297.0 jit_solution(7232822225588343491)
XLA Ops:
  7.2 1.7 pack_weights.1
  9.0 1.4 stack.70.vector_ref
  10.4 1.6 pack_front.1
  12.0 3.0 %collective-permute-start = (bf16[80,768]{1,0:T(8,128)(2,1)}, bf16[80,768]{1,0:T(8,128)(2,1)S(1)}, u32[]{:S(2)}, u32[]{:S(2)}) collective-permute-start(bf16[80,768]{1,0:T(8,128)(2,1)} %pack_front.1), channel_id=1, source_target_pairs={{0,8},{1,9},{2,10},{3,11},{4,12},{5,13},{6,14},{7,15},{8,16},{9,17... | collective-permute-start | bytes 368648 | tf_op jit(solution)/shard_map/ppermute | solution.py:366
  15.0 2.6 collective-permute-start.1
  17.6 1.3 collective-permute-start.2
  19.0 2.5 collective-permute-done
  21.5 4.4 %collective-permute-done.1 = bf16[80,768]{1,0:T(8,128)(2,1)S(1)} collective-permute-done((bf16[80,768]{1,0:T(8,128)(2,1)}, bf16[80,768]{1,0:T(8,128)(2,1)S(1)}, u32[]{:S(2)}, u32[]{:S(2)}) %collective-permute-start.1) | collective-permute-done | bytes 122912 | tf_op jit(solution)/shard_map/ppermute | solution.py:366
  25.9 1.0 pad_maximum_fusion.refs_0_
  26.9 1.6 collective-permute-start.3
  28.5 1.5 collective-permute-start.4
  30.5 10.6 %collective-permute-done.3.refs_1_ = bf16[4,80,768]{2,1,0:T(8,128)(2,1)S(1)} collective-permute-done((bf16[4,80,768]{2,1,0:T(8,128)(2,1)S(1)}, bf16[4,80,768]{2,1,0:T(8,128)(2,1)S(1)}, u32[]{:S(2)}, u32[]{:S(2)}) %collective-permute-start.3) | collective-permute-done | bytes 491552 | tf_op jit(solution)/shard_map/ppermute | solution.py:366
  41.1 8.8 %collective-permute-done.4.refs_2_ = bf16[4,80,768]{2,1,0:T(8,128)(2,1)S(1)} collective-permute-done((bf16[4,80,768]{2,1,0:T(8,128)(2,1)S(1)}, bf16[4,80,768]{2,1,0:T(8,128)(2,1)S(1)}, u32[]{:S(2)}, u32[]{:S(2)}) %collective-permute-start.4) | collective-permute-done | bytes 491552 | tf_op jit(solution)/shard_map/ppermute | solution.py:366
  49.9 8.5 %collective-permute-done.5.refs_3_ = bf16[4,80,768]{2,1,0:T(8,128)(2,1)S(1)} collective-permute-done((bf16[4,80,768]{2,1,0:T(8,128)(2,1)S(1)}, bf16[4,80,768]{2,1,0:T(8,128)(2,1)S(1)}, u32[]{:S(2)}, u32[]{:S(2)}) %collective-permute-start.5) | collective-permute-done | bytes 491552 | tf_op jit(solution)/shard_map/ppermute | solution.py:366
  58.4 0.7 reduce-window.9
  59.1 1.2 collective-permute-done.9.refs_7_
  60.4 9.9 %project.1 = (bf16[1024,2304]{1,0:T(8,128)(2,1)}, bf16[768,2304]{1,0:T(8,128)(2,1)}, f32[8,768]{1,0:T(8,128)S(1)}, f32[8,3072]{1,0:T(8,128)S(1)}, bf16[768,1024]{1,0:T(8,128)(2,1)S(1)}) custom-call(s32[4]{0:T(128)S(1)} %pad_add_fusion.place_ref, bf16[1024,768]{1,0:T(8,128)(2,1)} %hidden_ref.3, bf16[4,80,768]{2,1,0:T(8,128)(2,1)S(1)} %pad_maximum_fusion.refs_0_, ...), custom_call_target="tpu_custom_call" | custom-call | tf_op jit(solution)/shard_map/project/pallas_call | solution.py:663
  70.3 1.2 copy-done.3
  71.4 0.6 copy-done.12
  72.1 0.6 copy-done.13
  72.7 27.2 %attention_forward.1 = (bf16[1024,768]{1,0:T(8,128)(2,1)}, bf16[12,1024,1024]{2,1,0:T(8,128)(2,1)}) custom-call(s32[2]{0:T(128)} %bitcast.66, bf16[1024,2304]{1,0:T(8,128)(2,1)} %get-tuple-element.61.q_ref.k_ref.v_ref, bf16[1024,2304]{1,0:T(8,128)(2,1)} %get-tuple-element.61.q_ref.k_ref.v_ref, bf16[1024,2304]{1,0:T(8,128)(2,1)} %get-tuple-element.61.q_ref.k_ref.v_ref), custom_call_target="tpu_custom_call" | custom-call | flops 786432 | bytes 786432 | tf_op jit(solution)/shard_map/attention_forward/pallas_call | solution.py:90
  99.9 13.4 %all-gather.2.cloned.1.call-done = bf16[7168,768]{1,0:T(8,128)(2,1)} async-done(((bf16[224,768]{1,0:T(8,128)(2,1)}), bf16[7168,768]{1,0:T(8,128)(2,1)}) %all-gather.2.cloned.1.call-update) | async-done | bytes 11010064 | tf_op jit(solution)/shard_map/all_gather | solution.py:1068
  113.3 46.4 %row_pass.1 = (f32[1024,768]{1,0:T(8,128)}, bf16[4608,1024]{1,0:T(8,128)(2,1)}, bf16[1024,4608]{1,0:T(8,128)(2,1)}, f32[1024,768]{1,0:T(8,128)}, bf16[1024,768]{...) custom-call(s32[2]{0:T(128)} %bitcast.67, bf16[1024,768]{1,0:T(8,128)(2,1)} %get-tuple-element.62.mixed_ref, ...), custom_call_target="tpu_custom_call" | custom-call | flops 21743271936 | bytes 31457280 | tf_op jit(solution)/shard_map/row_pass/pallas_call | solution.py:831
  159.7 10.3 %grad_w_up_out.1 = (bf16[16,5,24,768]{3,2,1,0:T(8,128)(2,1)S(1)}, bf16[16,5,24,768]{3,2,1,0:T(8,128)(2,1)S(1)}) custom-call(s32[4]{0:T(128)S(1)} %pad_add_fusion.place_ref, bf16[4608,1024]{1,0:T(8,128)(2,1)} %get-tuple-element.70.left_ref, bf16[1024,4608]{1,0:T(8,128)(2,1)} %get-tuple-element.68.right_ref), custom_call_target="tpu_custom_call" | custom-call | flops 786432 | bytes 786432 | tf_op jit(solution)/shard_map/grad_w_up_out/pallas_call | solution.py:936
  170.4 8.0 %grad_w_down.1 = (bf16[16,96,768]{2,1,0:T(8,128)(2,1)S(1)}, bf16[16,96,768]{2,1,0:T(8,128)(2,1)S(1)}) custom-call(s32[4]{0:T(128)S(1)} %pad_add_fusion.place_ref, bf16[4608,1024]{1,0:T(8,128)(2,1)} %get-tuple-element.70.left_ref, bf16[1024,4608]{1,0:T(8,128)(2,1)} %get-tuple-element.68.right_ref), custom_call_target="tpu_custom_call" | custom-call | flops 786432 | bytes 786432 | tf_op jit(solution)/shard_map/grad_w_down/pallas_call | solution.py:902
  178.7 4.3 %collective-permute-done.10.refs_1_ = bf16[16,96,768]{2,1,0:T(8,128)(2,1)S(1)} collective-permute-done((bf16[16,96,768]{2,1,0:T(8,128)(2,1)S(1)}, bf16[16,96,768]{2,1,0:T(8,128)(2,1)S(1)}, u32[]{:S(2)}, u32[]{:S(2)}) %collective-permute-start.10) | collective-permute-done | bytes 2359328 | tf_op jit(solution)/shard_map/ppermute | solution.py:366
  183.0 3.6 %first_sum.1 = (bf16[4,2,216,768]{3,2,1,0:T(8,128)(2,1)S(1)}, bf16[2,2,216,768]{3,2,1,0:T(8,128)(2,1)}, bf16[2,2,216,768]{3,2,1,0:T(8,128)(2,1)}) custom-call(s32[4]{0:T(128)S(1)} %pad_add_fusion.place_ref, bf16[16,96,768]{2,1,0:T(8,128)(2,1)S(1)} %get-tuple-element.71.refs_0_, bf16[16,96,768]{2,1,0:T(8,128)(2,1)S(1)} %collective-permute-done.10.refs_1_, ...), custom_call_target="tpu_custom_call" | custom-call | flops 1327104 | bytes 1327104 | tf_op jit(solution)/shard_map/first_sum/pallas_call | solution.py:502
  186.6 1.5 collective-permute-start.13
  188.1 0.6 collective-permute-start.12
  188.6 31.4 %attention_backward.1 = (bf16[1024,768]{1,0:T(8,128)(2,1)}, bf16[1024,768]{1,0:T(8,128)(2,1)}, bf16[1024,768]{1,0:T(8,128)(2,1)}) custom-call(bf16[1024,2304]{1,0:T(8,128)(2,1)} %get-tuple-element.61.q_ref.k_ref.v_ref, bf16[1024,2304]{1,0:T(8,128)(2,1)} %get-tuple-element.61.q_ref.k_ref.v_ref, bf16[1024,2304]{1,0:T(8,128)(2,1)} %get-tuple-element.61.q_ref.k_ref.v_ref, ...), custom_call_target="tpu_custom_call" | custom-call | flops 786432 | bytes 786432 | tf_op jit(solution)/shard_map/attention_backward/pallas_call | solution.py:153
  220.1 2.4 second_sum.1
  222.5 7.2 %grad_w_qkv.1 = (bf16[16,48,768]{2,1,0:T(8,128)(2,1)S(1)}, bf16[16,48,768]{2,1,0:T(8,128)(2,1)S(1)}, bf16[16,32,768]{2,1,0:T(8,128)(2,1)S(1)}, bf16[16,32,768]{2,1,0:T(8,128)(2,1)S(1)}) custom-call(s32[4]{0:T(128)S(1)} %pad_add_fusion.place_ref, bf16[768,1024]{1,0:T(8,128)(2,1)S(1)} %copy-done.4, f32[8,768]{1,0:T(8,128)S(1)} %copy-done.8, ...), custom_call_target="tpu_custom_call" | custom-call | flops 786432 | bytes 786432 | tf_op jit(solution)/shard_map/grad_w_qkv/pallas_call | solution.py:1008
  230.3 1.4 collective-permute-start.14
  231.7 0.6 collective-permute-start.17
  232.3 1.4 collective-permute-done.16.refs_3_
  233.7 1.1 near_sum.1
  234.8 0.8 copy-done.5
  235.6 0.8 copy-done.9
  236.4 0.8 copy-done.10
  237.2 0.8 copy-done.11
  238.0 9.2 %collective-permute-done.14 = bf16[2,216,768]{2,1,0:T(8,128)(2,1)S(1)} collective-permute-done((bf16[2,216,768]{2,1,0:T(8,128)(2,1)S(1)}, bf16[2,216,768]{2,1,0:T(8,128)(2,1)S(1)}, u32[]{:S(2)}, u32[]{:S(2)}) %collective-permute-start.14) | collective-permute-done | bytes 663584 | tf_op jit(solution)/shard_map/ppermute | solution.py:366
  247.2 1.1 collective-permute-done.17
  248.3 1.5 add_convert_fusion
  249.8 0.7 collective-permute-start.18
  250.5 1.5 collective-permute-start.19
  251.9 1.4 collective-permute-start.20
  253.3 1.6 copy-done.2
  254.9 8.0 %grad_hidden.1 = f32[1024,768]{1,0:T(8,128)} custom-call(f32[1024,768]{1,0:T(8,128)} %get-tuple-element.101.grad_sum_ref, bf16[768,2304]{1,0:T(8,128)(2,1)} %get-tuple-element.102.weight_ref, bf16[1024,768]{1,0:T(8,128)(2,1)S(1)} %copy-done, bf16[1024,768]{1,0:T(8,128)(2,1)S(1)} %copy-done.1, bf16[1024,768]{1,0:T(8,128)(2,1)S(1)} %copy-done.2), custom_call_target="tpu_custom_call" | custom-call | flops 786432 | bytes 786432 | tf_op jit(solution)/shard_map/grad_hidden/pallas_call | solution.py:1039
  263.0 1.3 collective-permute-done.18
  264.3 8.8 %collective-permute-done.19 = bf16[4,80,768]{2,1,0:T(8,128)(2,1)} collective-permute-done((bf16[4,80,768]{2,1,0:T(8,128)(2,1)}, bf16[4,80,768]{2,1,0:T(8,128)(2,1)}, u32[]{:S(2)}, u32[]{:S(2)}) %collective-permute-start.19) | collective-permute-done | bytes 491552 | tf_op jit(solution)/shard_map/ppermute | solution.py:366
  273.1 1.5 fusion
  274.6 1.2 collective-permute-start.21
  275.9 1.1 collective-permute-start.22
  276.9 2.4 collective-permute-start.23
  279.3 1.7 reduce-scatter.2.cloned.1.call-done
  281.0 1.1 convert_element_type.100
  282.1 0.7 slice_bitcast_fusion
  282.9 0.7 copy.32
  283.6 0.6 slice_bitcast_fusion.1
  284.3 2.9 collective-permute-done.22
  287.2 1.2 bitcast_add_fusion
  288.4 0.5 slice_bitcast_fusion.2
  288.9 0.5 slice_bitcast_fusion.5
  289.5 0.7 pad_maximum_fusion.1
  (51 shorter events, 2.0 us)
Async XLA Ops:
  7.2 51.2 %copy-start.15 = (s32[2]{0:T(128)S(1)}, s32[2]{0:T(128)}, u32[]{:S(2)}) copy-start(s32[2]{0:T(128)} %param.17) | copy-start | bytes 28
  7.2 106.1 %all-gather.2.cloned.1.call-start = ((), (), s32[]{:S(2)}) async-start(), calls=%async_computation.1 | async-start | bytes 11354112 | tf_op jit(solution)/shard_map/all_gather | solution.py:1068
  9.0 272.0 %reduce-scatter.2.cloned.1.call-start = ((), (), s32[]{:S(2)}) async-start(), calls=%async_computation.2 | async-start | bytes 1658880 | tf_op jit(solution)/shard_map/reduce_scatter | solution.py:575
  12.0 9.5 %collective-permute-start = (bf16[80,768]{1,0:T(8,128)(2,1)}, bf16[80,768]{1,0:T(8,128)(2,1)S(1)}, u32[]{:S(2)}, u32[]{:S(2)}) collective-permute-start(bf16[80,768]{1,0:T(8,128)(2,1)} %pack_front.1), channel_id=1, source_target_pairs={{0,8},{1,9},{2,10},{3,11},{4,12},{5,13},{6,14},{7,15},{8,16},{9,17... | collective-permute-start | bytes 368648 | tf_op jit(solution)/shard_map/ppermute | solution.py:366
  15.0 10.9 %collective-permute-start.1 = (bf16[80,768]{1,0:T(8,128)(2,1)}, bf16[80,768]{1,0:T(8,128)(2,1)S(1)}, u32[]{:S(2)}, u32[]{:S(2)}) collective-permute-start(bf16[80,768]{1,0:T(8,128)(2,1)} %pack_front.1), channel_id=1, source_target_pairs={{0,16},{1,17},{2,18},{3,19},{4,20},{5,21},{6,22},{7,23},{8,24},{9,... | collective-permute-start | bytes 368648 | tf_op jit(solution)/shard_map/ppermute | solution.py:366
  17.6 8.3 %collective-permute-start.2 = (bf16[80,768]{1,0:T(8,128)(2,1)}, bf16[80,768]{1,0:T(8,128)(2,1)S(1)}, u32[]{:S(2)}, u32[]{:S(2)}) collective-permute-start(bf16[80,768]{1,0:T(8,128)(2,1)} %pack_front.1), channel_id=1, source_target_pairs={{0,24},{1,25},{2,26},{3,27},{4,28},{5,29},{6,30},{7,31},{8,0},{9,1... | collective-permute-start | bytes 368648 | tf_op jit(solution)/shard_map/ppermute | solution.py:366
  26.9 14.2 %collective-permute-start.3 = (bf16[4,80,768]{2,1,0:T(8,128)(2,1)S(1)}, bf16[4,80,768]{2,1,0:T(8,128)(2,1)S(1)}, u32[]{:S(2)}, u32[]{:S(2)}) collective-permute-start(bf16[4,80,768]{2,1,0:T(8,128)(2,1)S(1)} %pad_maximum_fusion.refs_0_), channel_id=1, source_target_pairs={{0,2},{1,3},{2,0},{3,1},{4,6},{5,7},{6,4},{7,5},{8,10},{9,11},{10,... | collective-permute-start | bytes 1474568 | tf_op jit(solution)/shard_map/ppermute | solution.py:366
  28.5 21.4 %collective-permute-start.4 = (bf16[4,80,768]{2,1,0:T(8,128)(2,1)S(1)}, bf16[4,80,768]{2,1,0:T(8,128)(2,1)S(1)}, u32[]{:S(2)}, u32[]{:S(2)}) collective-permute-start(bf16[4,80,768]{2,1,0:T(8,128)(2,1)S(1)} %pad_maximum_fusion.refs_0_), channel_id=1, source_target_pairs={{0,4},{1,5},{2,6},{3,7},{4,0},{5,1},{6,2},{7,3},{8,12},{9,13},{10,... | collective-permute-start | bytes 1474568 | tf_op jit(solution)/shard_map/ppermute | solution.py:366
  30.0 28.4 %collective-permute-start.5 = (bf16[4,80,768]{2,1,0:T(8,128)(2,1)S(1)}, bf16[4,80,768]{2,1,0:T(8,128)(2,1)S(1)}, u32[]{:S(2)}, u32[]{:S(2)}) collective-permute-start(bf16[4,80,768]{2,1,0:T(8,128)(2,1)S(1)} %pad_maximum_fusion.refs_0_), channel_id=1, source_target_pairs={{0,6},{1,7},{2,4},{3,5},{4,2},{5,3},{6,0},{7,1},{8,14},{9,15},{10,... | collective-permute-start | bytes 1474568 | tf_op jit(solution)/shard_map/ppermute | solution.py:366
  30.5 28.7 %collective-permute-start.6 = (bf16[4,80,768]{2,1,0:T(8,128)(2,1)S(1)}, bf16[4,80,768]{2,1,0:T(8,128)(2,1)S(1)}, u32[]{:S(2)}, u32[]{:S(2)}) collective-permute-start(bf16[4,80,768]{2,1,0:T(8,128)(2,1)S(1)} %pad_maximum_fusion.refs_0_), channel_id=1, source_target_pairs={{0,1},{1,0},{2,3},{3,2},{4,5},{5,4},{6,7},{7,6},{8,9},{9,8},{10,11... | collective-permute-start | bytes 1474568 | tf_op jit(solution)/shard_map/ppermute | solution.py:366
  41.1 18.1 %collective-permute-start.7 = (bf16[4,80,768]{2,1,0:T(8,128)(2,1)S(1)}, bf16[4,80,768]{2,1,0:T(8,128)(2,1)S(1)}, u32[]{:S(2)}, u32[]{:S(2)}) collective-permute-start(bf16[4,80,768]{2,1,0:T(8,128)(2,1)S(1)} %collective-permute-done.3.refs_1_), channel_id=1, source_target_pairs={{0,1},{1,0},{2,3},{3,2},{4,5},{5,4},{6,7},{7,6},{8,9},{9,8},{10,11... | collective-permute-start | bytes 1474568 | tf_op jit(solution)/shard_map/ppermute | solution.py:366
  49.9 9.2 %collective-permute-start.8 = (bf16[4,80,768]{2,1,0:T(8,128)(2,1)S(1)}, bf16[4,80,768]{2,1,0:T(8,128)(2,1)S(1)}, u32[]{:S(2)}, u32[]{:S(2)}) collective-permute-start(bf16[4,80,768]{2,1,0:T(8,128)(2,1)S(1)} %collective-permute-done.4.refs_2_), channel_id=1, source_target_pairs={{0,1},{1,0},{2,3},{3,2},{4,5},{5,4},{6,7},{7,6},{8,9},{9,8},{10,11... | collective-permute-start | bytes 1474568 | tf_op jit(solution)/shard_map/ppermute | solution.py:366
  58.4 2.0 collective-permute-start.9
  70.2 1.2 copy-start.3
  71.4 0.6 copy-start.12
  72.1 0.6 copy-start.13
  170.0 13.0 %collective-permute-start.11 = (bf16[16,5,24,768]{3,2,1,0:T(8,128)(2,1)S(1)}, bf16[16,5,24,768]{3,2,1,0:T(8,128)(2,1)S(1)}, u32[]{:S(2)}, u32[]{:S(2)}) collective-permute-start(bf16[16,5,24,768]{3,2,1,0:T(8,128)(2,1)S(1)} %get-tuple-element.73), channel_id=1, source_target_pairs={{0,1},{1,0},{2,3},{3,2},{4,5},{5,4},{6,7},{7,6},{8,9},{9,8},{10,11... | collective-permute-start | bytes 8847368 | tf_op jit(solution)/shard_map/ppermute | solution.py:366
  178.4 4.6 %collective-permute-start.10 = (bf16[16,96,768]{2,1,0:T(8,128)(2,1)S(1)}, bf16[16,96,768]{2,1,0:T(8,128)(2,1)S(1)}, u32[]{:S(2)}, u32[]{:S(2)}) collective-permute-start(bf16[16,96,768]{2,1,0:T(8,128)(2,1)S(1)} %get-tuple-element.72), channel_id=1, source_target_pairs={{0,1},{1,0},{2,3},{3,2},{4,5},{5,4},{6,7},{7,6},{8,9},{9,8},{10,11... | collective-permute-start | bytes 7077896 | tf_op jit(solution)/shard_map/ppermute | solution.py:366
  186.6 33.4 %collective-permute-start.13 = (bf16[2,2,216,768]{3,2,1,0:T(8,128)(2,1)}, bf16[2,2,216,768]{3,2,1,0:T(8,128)(2,1)S(1)}, u32[]{:S(2)}, u32[]{:S(2)}) collective-permute-start(bf16[2,2,216,768]{3,2,1,0:T(8,128)(2,1)} %get-tuple-element.77), channel_id=1, source_target_pairs={{0,4},{1,5},{2,6},{3,7},{4,0},{5,1},{6,2},{7,3},{8,12},{9,13},{10,... | collective-permute-start | bytes 3981320 | tf_op jit(solution)/shard_map/ppermute | solution.py:366
  188.1 32.0 %collective-permute-start.12 = (bf16[2,2,216,768]{3,2,1,0:T(8,128)(2,1)}, bf16[2,2,216,768]{3,2,1,0:T(8,128)(2,1)}, u32[]{:S(2)}, u32[]{:S(2)}) collective-permute-start(bf16[2,2,216,768]{3,2,1,0:T(8,128)(2,1)} %get-tuple-element.75), channel_id=1, source_target_pairs={{0,2},{1,3},{2,0},{3,1},{4,6},{5,7},{6,4},{7,5},{8,10},{9,11},{10,... | collective-permute-start | bytes 3981320 | tf_op jit(solution)/shard_map/ppermute | solution.py:366
  220.0 2.4 copy-start.4
  220.0 2.4 copy-start.7
  220.1 2.4 copy-start.8
  229.7 4.0 %collective-permute-start.15 = (bf16[16,48,768]{2,1,0:T(8,128)(2,1)S(1)}, bf16[16,48,768]{2,1,0:T(8,128)(2,1)S(1)}, u32[]{:S(2)}, u32[]{:S(2)}) collective-permute-start(bf16[16,48,768]{2,1,0:T(8,128)(2,1)S(1)} %get-tuple-element.93), channel_id=1, source_target_pairs={{0,1},{1,0},{2,3},{3,2},{4,5},{5,4},{6,7},{7,6},{8,9},{9,8},{10,11... | collective-permute-start | bytes 3538952 | tf_op jit(solution)/shard_map/ppermute | solution.py:366
  229.8 4.0 %collective-permute-start.16 = (bf16[16,32,768]{2,1,0:T(8,128)(2,1)S(1)}, bf16[16,32,768]{2,1,0:T(8,128)(2,1)S(1)}, u32[]{:S(2)}, u32[]{:S(2)}) collective-permute-start(bf16[16,32,768]{2,1,0:T(8,128)(2,1)S(1)} %get-tuple-element.95), channel_id=1, source_target_pairs={{0,1},{1,0},{2,3},{3,2},{4,5},{5,4},{6,7},{7,6},{8,9},{9,8},{10,11... | collective-permute-start | bytes 2359304 | tf_op jit(solution)/shard_map/ppermute | solution.py:366
  230.3 16.9 %collective-permute-start.14 = (bf16[2,216,768]{2,1,0:T(8,128)(2,1)S(1)}, bf16[2,216,768]{2,1,0:T(8,128)(2,1)S(1)}, u32[]{:S(2)}, u32[]{:S(2)}) collective-permute-start(bf16[2,216,768]{2,1,0:T(8,128)(2,1)S(1)} %get-tuple-element.86), channel_id=1, source_target_pairs={{0,4},{1,5},{2,6},{3,7},{4,0},{5,1},{6,2},{7,3},{8,12},{9,13},{10,... | collective-permute-start | bytes 1990664 | tf_op jit(solution)/shard_map/ppermute | solution.py:366
  231.7 16.6 %collective-permute-start.17 = (bf16[2,216,768]{2,1,0:T(8,128)(2,1)S(1)}, bf16[2,216,768]{2,1,0:T(8,128)(2,1)S(1)}, u32[]{:S(2)}, u32[]{:S(2)}) collective-permute-start(bf16[2,216,768]{2,1,0:T(8,128)(2,1)S(1)} %get-tuple-element.88), channel_id=1, source_target_pairs={{0,2},{1,3},{2,0},{3,1},{4,6},{5,7},{6,4},{7,5},{8,10},{9,11},{10,... | collective-permute-start | bytes 1990664 | tf_op jit(solution)/shard_map/ppermute | solution.py:366
  234.8 0.8 copy-start.5
  235.6 0.8 copy-start.9
  236.4 0.8 copy-start.10
  237.2 0.8 copy-start.11
  248.3 5.1 %copy-start = (bf16[1024,768]{1,0:T(8,128)(2,1)S(1)}, bf16[1024,768]{1,0:T(8,128)(2,1)}, u32[]{:S(2)}) copy-start(bf16[1024,768]{1,0:T(8,128)(2,1)} %get-tuple-element.80.refs_0_) | copy-start | bytes 4718596
  248.3 5.1 %copy-start.1 = (bf16[1024,768]{1,0:T(8,128)(2,1)S(1)}, bf16[1024,768]{1,0:T(8,128)(2,1)}, u32[]{:S(2)}) copy-start(bf16[1024,768]{1,0:T(8,128)(2,1)} %get-tuple-element.81.refs_1_) | copy-start | bytes 4718596
  249.8 14.5 %collective-permute-start.18 = (bf16[4,80,768]{2,1,0:T(8,128)(2,1)}, bf16[4,80,768]{2,1,0:T(8,128)(2,1)}, u32[]{:S(2)}, u32[]{:S(2)}) collective-permute-start(bf16[4,80,768]{2,1,0:T(8,128)(2,1)} %copy-done.11), channel_id=1, source_target_pairs={{0,2},{1,3},{2,0},{3,1},{4,6},{5,7},{6,4},{7,5},{8,10},{9,11},{10,... | collective-permute-start | bytes 1474568 | tf_op jit(solution)/shard_map/ppermute | solution.py:366
  250.5 22.7 %collective-permute-start.19 = (bf16[4,80,768]{2,1,0:T(8,128)(2,1)}, bf16[4,80,768]{2,1,0:T(8,128)(2,1)}, u32[]{:S(2)}, u32[]{:S(2)}) collective-permute-start(bf16[4,80,768]{2,1,0:T(8,128)(2,1)} %copy-done.10), channel_id=1, source_target_pairs={{0,4},{1,5},{2,6},{3,7},{4,0},{5,1},{6,2},{7,3},{8,12},{9,13},{10,... | collective-permute-start | bytes 1474568 | tf_op jit(solution)/shard_map/ppermute | solution.py:366
  251.9 21.2 %collective-permute-start.20 = (bf16[4,80,768]{2,1,0:T(8,128)(2,1)}, bf16[4,80,768]{2,1,0:T(8,128)(2,1)}, u32[]{:S(2)}, u32[]{:S(2)}) collective-permute-start(bf16[4,80,768]{2,1,0:T(8,128)(2,1)} %copy-done.9), channel_id=1, source_target_pairs={{0,6},{1,7},{2,4},{3,5},{4,2},{5,3},{6,0},{7,1},{8,14},{9,15},{10,... | collective-permute-start | bytes 1474568 | tf_op jit(solution)/shard_map/ppermute | solution.py:366
  253.3 1.6 copy-start.2
  254.9 18.2 %copy-start.6 = (bf16[4,80,768]{2,1,0:T(8,128)(2,1)S(1)}, bf16[4,80,768]{2,1,0:T(8,128)(2,1)}, u32[]{:S(2)}) copy-start(bf16[4,80,768]{2,1,0:T(8,128)(2,1)} %copy-done.5) | copy-start | bytes 1474564
  274.6 9.6 %collective-permute-start.21 = (bf16[80,768]{1,0:T(8,128)(2,1)S(1)}, bf16[80,768]{1,0:T(8,128)(2,1)S(1)}, u32[]{:S(2)}, u32[]{:S(2)}) collective-permute-start(bf16[80,768]{1,0:T(8,128)(2,1)S(1)} %get-tuple-element.107), channel_id=1, source_target_pairs={{0,8},{1,9},{2,10},{3,11},{4,12},{5,13},{6,14},{7,15},{8,16},{9,17... | collective-permute-start | bytes 368648 | tf_op jit(solution)/shard_map/ppermute | solution.py:366
  275.9 11.3 %collective-permute-start.22 = (bf16[80,768]{1,0:T(8,128)(2,1)S(1)}, bf16[80,768]{1,0:T(8,128)(2,1)S(1)}, u32[]{:S(2)}, u32[]{:S(2)}) collective-permute-start(bf16[80,768]{1,0:T(8,128)(2,1)S(1)} %get-tuple-element.109), channel_id=1, source_target_pairs={{0,16},{1,17},{2,18},{3,19},{4,20},{5,21},{6,22},{7,23},{8,24},{9,... | collective-permute-start | bytes 368648 | tf_op jit(solution)/shard_map/ppermute | solution.py:366
  276.9 10.2 %collective-permute-start.23 = (bf16[80,768]{1,0:T(8,128)(2,1)S(1)}, bf16[80,768]{1,0:T(8,128)(2,1)S(1)}, u32[]{:S(2)}, u32[]{:S(2)}) collective-permute-start(bf16[80,768]{1,0:T(8,128)(2,1)S(1)} %get-tuple-element.108), channel_id=1, source_target_pairs={{0,24},{1,25},{2,26},{3,27},{4,28},{5,29},{6,30},{7,31},{8,0},{9,1... | collective-permute-start | bytes 368648 | tf_op jit(solution)/shard_map/ppermute | solution.py:366
  281.0 1.8 copy-start.14
Sparse Core Ops, SparseCore 0:
  11.5 101.7 all-gather.1
  249.9 31.1 reduce-scatter.1

commit v4 on v3

--- a/solution.py
+++ b/solution.py
@@ -138,7 +138,7 @@
         all_scores.append(grad_scores)
         all_grads.append(my_grads)
         all_queries.append(jnp.where(mine, queries, jnp.zeros_like(queries)))
-        grad_queries.append(dot(keys_turned[DH * head : DH * (head + 1)], grad_scores))
+        grad_queries.append(dot(keys_turned, grad_scores)[DH * head : DH * (head + 1)])
     turned = jnp.concatenate(grad_queries, axis=0) * scale
     dq_ref[...] = jnp.transpose(turned).astype(BF)
     all_probs = jnp.concatenate([probs_ref[0], probs_ref[1]], axis=1)
@@ -348,6 +348,7 @@
 
 
 CHIPS = (4, 2, 2, 2)
+KINDS = ((0, 0, 0), (0, 1, 0), (1, 0, 0), (1, 1, 0), (1, 1, CHIPS[0] // 2))
 
 
 def coordinates(index):
@@ -410,10 +411,12 @@
     )(w_qkv, vectors, bias_up)
 
 
-def gather_pieces(packed):
+def gather_square(packed):
     column = jnp.stack([packed] + [moved(packed, (step, 0, 0, 0)) for step in range(1, CHIPS[0])])
-    pieces = [column] + [moved(column, step) for step in ((0, 0, 1, 0), (0, 1, 0, 0), (0, 1, 1, 0))]
-    return pieces, [moved(piece, (0, 0, 0, 1)) for piece in pieces]
+    by_x, by_y = moved(column, NEAR[0]), moved(column, NEAR[1])
+    half = CHIPS[0] // 2
+    pieces = [column, by_x, by_y, moved(by_x[:half], NEAR[1]), moved(by_y[half:], NEAR[0])]
+    return pieces + [moved(piece, (0, 0, 0, 1)) for piece in pieces]
 
 
 NEAR = ((0, 0, 1, 0), (0, 1, 0, 0), (0, 1, 1, 0))
@@ -620,12 +623,12 @@
     up_lanes = lax.broadcasted_iota(jnp.int32, (8, up_ref.shape[1]), 1)
     vectors = jnp.zeros((8, width), F32)
     ups = jnp.zeros(up_ref.shape, F32)
-    steps = ((0, 0), (0, 1), (1, 0), (1, 1))
-    for kind, (step_y, step_x) in enumerate(steps):
-        for step_z in range(zs):
+    for kind, (step_y, step_x, first_z) in enumerate(KINDS):
+        for level in range(pieces[kind].shape[0]):
+            step_z = first_z + level
             chip = ((z + zs - step_z) % zs * ys + (y + step_y) % ys) * xs + (x + step_x) % xs
-            mine = pieces[kind][step_z].astype(F32)
-            other = pieces[len(steps) + kind][step_z].astype(F32)
+            mine = pieces[kind][level].astype(F32)
+            other = pieces[len(KINDS) + kind][level].astype(F32)
             low = jnp.where(core == 0, mine, other)
             high = jnp.where(core == 0, other, mine)
             rows = pl.ds(pl.multiple_of(chip * (cores * part), cores * part), cores * part)
@@ -1071,9 +1074,9 @@
         [bias_q, bias_v, bias_out, norm1_gain, norm1_bias, bias_down, norm2_gain, norm2_bias]
     )
     front = pack_front(w_qkv, vectors, bias_up[None])
-    mine, others = gather_pieces(front)
+    pieces = gather_square(front)
     stacked, whole_qkv, whole_vectors, whole_up_bias, hidden_turned = project(
-        place, hidden, mine + others, hidden_units, n
+        place, hidden, pieces, hidden_units, n
     )
     mixed, probs = attention_forward(bounds, stacked)
     output, left, right, grad_sum, grad_mixed, sums, up_sums = row_pass(

time: 298 us -> 292 us (0.980)
  waiting for transfers between devices: 80.3 us -> 72.8 us
  starting transfers between devices: 24.1 us -> 27.2 us
    ppermute x24 -> x26, waiting for transfers between devices: 65.2 us -> 60.1 us  [moved(): return lax.ppermute(array, 'fsdp', pairs)]
    ppermute x24 -> x26, starting transfers between devices: 24 us -> 27.1 us  [moved(): return lax.ppermute(array, 'fsdp', pairs)]
  transfers between devices with their start and end apart: 26 -> 28, of which waited for: 15 -> 16; matrix products, arithmetic and copies ran while one was open for 3% -> 3% of each run, Pallas kernels for 29% -> 30%
where the time goes in v4:
time: 292 us
  Pallas kernels  158 us (54%)
  waiting for transfers between devices  72.8 us (25%)
  starting transfers between devices  27.2 us (9%)
  between operations  14.2 us (5%)
  local copies, waits for them, and re-layouts  11.9 us (4%)
  other arithmetic  7.68 us (3%)
    ppermute x26, waiting for transfers between devices, moved(): return lax.ppermute(array, 'fsdp', pairs)  60.1 us
    pallas_call x1, Pallas kernels, row_pass(): pl.pallas_call(functools.partial(row_pass_kernel, part=part, chunk=chunk)...  46.4 us
    pallas_call x1, Pallas kernels, attention_backward(): pl.pallas_call(functools.partial(attention_backward_kernel, scale=1.0 / m...  30.2 us
    pallas_call x1, Pallas kernels, attention_forward(): pl.pallas_call(functools.partial(attention_forward_kernel, scale=1.0 / ma...  27.3 us
    ppermute x26, starting transfers between devices, moved(): return lax.ppermute(array, 'fsdp', pairs)  27.1 us
    all_gather x1, waiting for transfers between devices, meshed_layer(): lax.all_gather(pack_weights(w_down, w_up, w_out), 'fsdp', axis=0, tiled=T...  11.7 us
    pallas_call x1, Pallas kernels, up_grad(): pl.pallas_call(up_grad_kernel, grid_spec=pltpu.PrefetchScalarGridSpec(num...  10.3 us
    pallas_call x1, Pallas kernels, project(): pl.pallas_call(functools.partial(project_kernel, part=width // count, inn...  9.92 us
  transfers between devices with their start and end apart: 28, of which 16 were waited for; matrix products, arithmetic and copies ran while one was open for 3% of the time, Pallas kernels for 30%

profile of v4, /device:TPU:0, one launch (start us, length us, event | category | flops | bytes accessed | tf_op | source)
XLA Modules:
  0.0 291.5 jit_solution(5773152134734556689)
XLA Ops:
  7.2 1.7 pack_weights.1
  9.0 1.4 stack.70.vector_ref
  10.4 1.6 pack_front.1
  12.0 3.0 %collective-permute-start = (bf16[80,768]{1,0:T(8,128)(2,1)}, bf16[80,768]{1,0:T(8,128)(2,1)S(1)}, u32[]{:S(2)}, u32[]{:S(2)}) collective-permute-start(bf16[80,768]{1,0:T(8,128)(2,1)} %pack_front.1), channel_id=1, source_target_pairs={{0,8},{1,9},{2,10},{3,11},{4,12},{5,13},{6,14},{7,15},{8,16},{9,17... | collective-permute-start | bytes 368648 | tf_op jit(solution)/shard_map/ppermute | solution.py:367
  15.0 2.6 collective-permute-start.1
  17.6 1.3 collective-permute-start.2
  19.0 2.5 collective-permute-done
  21.5 4.4 %collective-permute-done.1 = bf16[80,768]{1,0:T(8,128)(2,1)S(1)} collective-permute-done((bf16[80,768]{1,0:T(8,128)(2,1)}, bf16[80,768]{1,0:T(8,128)(2,1)S(1)}, u32[]{:S(2)}, u32[]{:S(2)}) %collective-permute-start.1) | collective-permute-done | bytes 122912 | tf_op jit(solution)/shard_map/ppermute | solution.py:367
  25.9 1.0 pad_maximum_fusion.refs_0_
  26.9 1.6 collective-permute-start.3
  28.5 1.5 collective-permute-start.4
  30.0 10.0 %collective-permute-done.3.refs_1_ = bf16[4,80,768]{2,1,0:T(8,128)(2,1)S(1)} collective-permute-done((bf16[4,80,768]{2,1,0:T(8,128)(2,1)S(1)}, bf16[4,80,768]{2,1,0:T(8,128)(2,1)S(1)}, u32[]{:S(2)}, u32[]{:S(2)}) %collective-permute-start.3) | collective-permute-done | bytes 491552 | tf_op jit(solution)/shard_map/ppermute | solution.py:367
  40.0 1.6 collective-permute-start.5
  41.7 0.6 collective-permute-start.9
  42.2 1.5 collective-permute-start.6
  43.7 7.6 %collective-permute-done.5.refs_3_ = bf16[2,80,768]{2,1,0:T(8,128)(2,1)S(1)} collective-permute-done((bf16[2,80,768]{2,1,0:T(8,128)(2,1)S(1)}, bf16[2,80,768]{2,1,0:T(8,128)(2,1)S(1)}, u32[]{:S(2)}, u32[]{:S(2)}) %collective-permute-start.5) | collective-permute-done | bytes 245792 | tf_op jit(solution)/shard_map/ppermute | solution.py:367
  51.3 4.4 %collective-permute-done.6.refs_4_ = bf16[2,80,768]{2,1,0:T(8,128)(2,1)S(1)} collective-permute-done((bf16[2,80,768]{2,1,0:T(8,128)(2,1)S(1)}, bf16[2,80,768]{2,1,0:T(8,128)(2,1)S(1)}, u32[]{:S(2)}, u32[]{:S(2)}) %collective-permute-start.6) | collective-permute-done | bytes 245792 | tf_op jit(solution)/shard_map/ppermute | solution.py:367
  55.7 0.7 reduce-window.9
  56.4 0.9 collective-permute-done.11.refs_9_
  57.3 9.9 %project.1 = (bf16[1024,2304]{1,0:T(8,128)(2,1)}, bf16[768,2304]{1,0:T(8,128)(2,1)}, f32[8,768]{1,0:T(8,128)S(1)}, f32[8,3072]{1,0:T(8,128)S(1)}, bf16[768,1024]{1,0:T(8,128)(2,1)S(1)}) custom-call(s32[4]{0:T(128)S(1)} %pad_add_fusion.place_ref, bf16[1024,768]{1,0:T(8,128)(2,1)} %hidden_ref.3, bf16[4,80,768]{2,1,0:T(8,128)(2,1)S(1)} %pad_maximum_fusion.refs_0_, ...), custom_call_target="tpu_custom_call" | custom-call | tf_op jit(solution)/shard_map/project/pallas_call | solution.py:666
  67.2 1.2 copy-done.3
  68.4 0.6 copy-done.12
  69.1 0.6 copy-done.13
  69.7 27.3 %attention_forward.1 = (bf16[1024,768]{1,0:T(8,128)(2,1)}, bf16[12,1024,1024]{2,1,0:T(8,128)(2,1)}) custom-call(s32[2]{0:T(128)} %bitcast.66, bf16[1024,2304]{1,0:T(8,128)(2,1)} %get-tuple-element.61.q_ref.k_ref.v_ref, bf16[1024,2304]{1,0:T(8,128)(2,1)} %get-tuple-element.61.q_ref.k_ref.v_ref, bf16[1024,2304]{1,0:T(8,128)(2,1)} %get-tuple-element.61.q_ref.k_ref.v_ref), custom_call_target="tpu_custom_call" | custom-call | flops 786432 | bytes 786432 | tf_op jit(solution)/shard_map/attention_forward/pallas_call | solution.py:90
  96.9 11.7 %all-gather.2.cloned.1.call-done = bf16[7168,768]{1,0:T(8,128)(2,1)} async-done(((bf16[224,768]{1,0:T(8,128)(2,1)}), bf16[7168,768]{1,0:T(8,128)(2,1)}) %all-gather.2.cloned.1.call-update) | async-done | bytes 11010064 | tf_op jit(solution)/shard_map/all_gather | solution.py:1071
  108.6 46.4 %row_pass.1 = (f32[1024,768]{1,0:T(8,128)}, bf16[4608,1024]{1,0:T(8,128)(2,1)}, bf16[1024,4608]{1,0:T(8,128)(2,1)}, f32[1024,768]{1,0:T(8,128)}, bf16[1024,768]{...) custom-call(s32[2]{0:T(128)} %bitcast.67, bf16[1024,768]{1,0:T(8,128)(2,1)} %get-tuple-element.62.mixed_ref, ...), custom_call_target="tpu_custom_call" | custom-call | flops 21743271936 | bytes 31457280 | tf_op jit(solution)/shard_map/row_pass/pallas_call | solution.py:834
  155.0 10.3 %grad_w_up_out.1 = (bf16[16,5,24,768]{3,2,1,0:T(8,128)(2,1)S(1)}, bf16[16,5,24,768]{3,2,1,0:T(8,128)(2,1)S(1)}) custom-call(s32[4]{0:T(128)S(1)} %pad_add_fusion.place_ref, bf16[4608,1024]{1,0:T(8,128)(2,1)} %get-tuple-element.70.left_ref, bf16[1024,4608]{1,0:T(8,128)(2,1)} %get-tuple-element.68.right_ref), custom_call_target="tpu_custom_call" | custom-call | flops 786432 | bytes 786432 | tf_op jit(solution)/shard_map/grad_w_up_out/pallas_call | solution.py:939
  165.6 8.0 %grad_w_down.1 = (bf16[16,96,768]{2,1,0:T(8,128)(2,1)S(1)}, bf16[16,96,768]{2,1,0:T(8,128)(2,1)S(1)}) custom-call(s32[4]{0:T(128)S(1)} %pad_add_fusion.place_ref, bf16[4608,1024]{1,0:T(8,128)(2,1)} %get-tuple-element.70.left_ref, bf16[1024,4608]{1,0:T(8,128)(2,1)} %get-tuple-element.68.right_ref), custom_call_target="tpu_custom_call" | custom-call | flops 786432 | bytes 786432 | tf_op jit(solution)/shard_map/grad_w_down/pallas_call | solution.py:905
  174.0 4.3 %collective-permute-done.12.refs_1_ = bf16[16,96,768]{2,1,0:T(8,128)(2,1)S(1)} collective-permute-done((bf16[16,96,768]{2,1,0:T(8,128)(2,1)S(1)}, bf16[16,96,768]{2,1,0:T(8,128)(2,1)S(1)}, u32[]{:S(2)}, u32[]{:S(2)}) %collective-permute-start.12) | collective-permute-done | bytes 2359328 | tf_op jit(solution)/shard_map/ppermute | solution.py:367
  178.3 3.6 %first_sum.1 = (bf16[4,2,216,768]{3,2,1,0:T(8,128)(2,1)S(1)}, bf16[2,2,216,768]{3,2,1,0:T(8,128)(2,1)}, bf16[2,2,216,768]{3,2,1,0:T(8,128)(2,1)}) custom-call(s32[4]{0:T(128)S(1)} %pad_add_fusion.place_ref, bf16[16,96,768]{2,1,0:T(8,128)(2,1)S(1)} %get-tuple-element.71.refs_0_, bf16[16,96,768]{2,1,0:T(8,128)(2,1)S(1)} %collective-permute-done.12.refs_1_, ...), custom_call_target="tpu_custom_call" | custom-call | flops 1327104 | bytes 1327104 | tf_op jit(solution)/shard_map/first_sum/pallas_call | solution.py:505
  181.9 1.6 collective-permute-start.15
  183.9 30.2 %attention_backward.1 = (bf16[1024,768]{1,0:T(8,128)(2,1)}, bf16[1024,768]{1,0:T(8,128)(2,1)}, bf16[1024,768]{1,0:T(8,128)(2,1)}) custom-call(bf16[1024,2304]{1,0:T(8,128)(2,1)} %get-tuple-element.61.q_ref.k_ref.v_ref, bf16[1024,2304]{1,0:T(8,128)(2,1)} %get-tuple-element.61.q_ref.k_ref.v_ref, bf16[1024,2304]{1,0:T(8,128)(2,1)} %get-tuple-element.61.q_ref.k_ref.v_ref, ...), custom_call_target="tpu_custom_call" | custom-call | flops 786432 | bytes 786432 | tf_op jit(solution)/shard_map/attention_backward/pallas_call | solution.py:153
  214.2 0.6 collective-permute-done.14.from_x_ref
  214.8 2.4 second_sum.1
  217.2 7.2 %grad_w_qkv.1 = (bf16[16,48,768]{2,1,0:T(8,128)(2,1)S(1)}, bf16[16,48,768]{2,1,0:T(8,128)(2,1)S(1)}, bf16[16,32,768]{2,1,0:T(8,128)(2,1)S(1)}, bf16[16,32,768]{2,1,0:T(8,128)(2,1)S(1)}) custom-call(s32[4]{0:T(128)S(1)} %pad_add_fusion.place_ref, bf16[768,1024]{1,0:T(8,128)(2,1)S(1)} %copy-done.4, f32[8,768]{1,0:T(8,128)S(1)} %copy-done.8, ...), custom_call_target="tpu_custom_call" | custom-call | flops 786432 | bytes 786432 | tf_op jit(solution)/shard_map/grad_w_qkv/pallas_call | solution.py:1011
  225.0 0.8 collective-permute-start.16
  225.8 1.0 collective-permute-start.19
  226.9 1.6 collective-permute-done.18.refs_3_
  228.4 1.1 near_sum.1
  229.6 0.8 copy-done.5
  230.3 0.8 copy-done.9
  231.1 0.8 copy-done.10
  231.9 0.8 copy-done.11
  232.7 9.1 %collective-permute-done.16 = bf16[2,216,768]{2,1,0:T(8,128)(2,1)S(1)} collective-permute-done((bf16[2,216,768]{2,1,0:T(8,128)(2,1)S(1)}, bf16[2,216,768]{2,1,0:T(8,128)(2,1)S(1)}, u32[]{:S(2)}, u32[]{:S(2)}) %collective-permute-start.16) | collective-permute-done | bytes 663584 | tf_op jit(solution)/shard_map/ppermute | solution.py:367
  242.4 1.5 add_convert_fusion
  243.9 1.1 collective-permute-start.20
  245.0 1.1 collective-permute-start.21
  246.2 1.3 collective-permute-start.22
  247.5 1.6 copy-done.2
  249.1 8.0 %grad_hidden.1 = f32[1024,768]{1,0:T(8,128)} custom-call(f32[1024,768]{1,0:T(8,128)} %get-tuple-element.101.grad_sum_ref, bf16[768,2304]{1,0:T(8,128)(2,1)} %get-tuple-element.102.weight_ref, bf16[1024,768]{1,0:T(8,128)(2,1)S(1)} %copy-done, bf16[1024,768]{1,0:T(8,128)(2,1)S(1)} %copy-done.1, bf16[1024,768]{1,0:T(8,128)(2,1)S(1)} %copy-done.2), custom_call_target="tpu_custom_call" | custom-call | flops 786432 | bytes 786432 | tf_op jit(solution)/shard_map/grad_hidden/pallas_call | solution.py:1042
  257.1 1.3 collective-permute-done.20
  258.5 9.2 %collective-permute-done.21 = bf16[4,80,768]{2,1,0:T(8,128)(2,1)} collective-permute-done((bf16[4,80,768]{2,1,0:T(8,128)(2,1)}, bf16[4,80,768]{2,1,0:T(8,128)(2,1)}, u32[]{:S(2)}, u32[]{:S(2)}) %collective-permute-start.21) | collective-permute-done | bytes 491552 | tf_op jit(solution)/shard_map/ppermute | solution.py:367
  267.6 1.5 fusion
  269.2 1.3 collective-permute-start.23
  270.4 1.1 collective-permute-start.24
  271.5 2.4 collective-permute-start.25
  273.9 1.0 reduce-scatter.2.cloned.1.call-done
  274.9 1.1 convert_element_type.100
  276.0 0.7 slice_bitcast_fusion
  276.8 0.7 copy.32
  277.5 0.6 slice_bitcast_fusion.1
  278.1 3.6 %collective-permute-done.24 = bf16[80,768]{1,0:T(8,128)(2,1)S(1)} collective-permute-done((bf16[80,768]{1,0:T(8,128)(2,1)S(1)}, bf16[80,768]{1,0:T(8,128)(2,1)S(1)}, u32[]{:S(2)}, u32[]{:S(2)}) %collective-permute-start.24) | collective-permute-done | bytes 122912 | tf_op jit(solution)/shard_map/ppermute | solution.py:367
  281.7 1.2 bitcast_add_fusion
  284.0 0.7 pad_maximum_fusion.1
  (57 shorter events, 3.6 us)
Async XLA Ops:
  7.2 48.5 %copy-start.15 = (s32[2]{0:T(128)S(1)}, s32[2]{0:T(128)}, u32[]{:S(2)}) copy-start(s32[2]{0:T(128)} %param.17) | copy-start | bytes 28
  7.2 101.4 %all-gather.2.cloned.1.call-start = ((), (), s32[]{:S(2)}) async-start(), calls=%async_computation.1 | async-start | bytes 11354112 | tf_op jit(solution)/shard_map/all_gather | solution.py:1071
  9.0 265.9 %reduce-scatter.2.cloned.1.call-start = ((), (), s32[]{:S(2)}) async-start(), calls=%async_computation.2 | async-start | bytes 1658880 | tf_op jit(solution)/shard_map/reduce_scatter | solution.py:578
  12.0 9.5 %collective-permute-start = (bf16[80,768]{1,0:T(8,128)(2,1)}, bf16[80,768]{1,0:T(8,128)(2,1)S(1)}, u32[]{:S(2)}, u32[]{:S(2)}) collective-permute-start(bf16[80,768]{1,0:T(8,128)(2,1)} %pack_front.1), channel_id=1, source_target_pairs={{0,8},{1,9},{2,10},{3,11},{4,12},{5,13},{6,14},{7,15},{8,16},{9,17... | collective-permute-start | bytes 368648 | tf_op jit(solution)/shard_map/ppermute | solution.py:367
  15.0 10.9 %collective-permute-start.1 = (bf16[80,768]{1,0:T(8,128)(2,1)}, bf16[80,768]{1,0:T(8,128)(2,1)S(1)}, u32[]{:S(2)}, u32[]{:S(2)}) collective-permute-start(bf16[80,768]{1,0:T(8,128)(2,1)} %pack_front.1), channel_id=1, source_target_pairs={{0,16},{1,17},{2,18},{3,19},{4,20},{5,21},{6,22},{7,23},{8,24},{9,... | collective-permute-start | bytes 368648 | tf_op jit(solution)/shard_map/ppermute | solution.py:367
  17.6 8.3 %collective-permute-start.2 = (bf16[80,768]{1,0:T(8,128)(2,1)}, bf16[80,768]{1,0:T(8,128)(2,1)S(1)}, u32[]{:S(2)}, u32[]{:S(2)}) collective-permute-start(bf16[80,768]{1,0:T(8,128)(2,1)} %pack_front.1), channel_id=1, source_target_pairs={{0,24},{1,25},{2,26},{3,27},{4,28},{5,29},{6,30},{7,31},{8,0},{9,1... | collective-permute-start | bytes 368648 | tf_op jit(solution)/shard_map/ppermute | solution.py:367
  26.9 13.1 %collective-permute-start.3 = (bf16[4,80,768]{2,1,0:T(8,128)(2,1)S(1)}, bf16[4,80,768]{2,1,0:T(8,128)(2,1)S(1)}, u32[]{:S(2)}, u32[]{:S(2)}) collective-permute-start(bf16[4,80,768]{2,1,0:T(8,128)(2,1)S(1)} %pad_maximum_fusion.refs_0_), channel_id=1, source_target_pairs={{0,2},{1,3},{2,0},{3,1},{4,6},{5,7},{6,4},{7,5},{8,10},{9,11},{10,... | collective-permute-start | bytes 1474568 | tf_op jit(solution)/shard_map/ppermute | solution.py:367
  28.5 13.2 %collective-permute-start.4 = (bf16[4,80,768]{2,1,0:T(8,128)(2,1)S(1)}, bf16[4,80,768]{2,1,0:T(8,128)(2,1)S(1)}, u32[]{:S(2)}, u32[]{:S(2)}) collective-permute-start(bf16[4,80,768]{2,1,0:T(8,128)(2,1)S(1)} %pad_maximum_fusion.refs_0_), channel_id=1, source_target_pairs={{0,4},{1,5},{2,6},{3,7},{4,0},{5,1},{6,2},{7,3},{8,12},{9,13},{10,... | collective-permute-start | bytes 1474568 | tf_op jit(solution)/shard_map/ppermute | solution.py:367
  30.0 26.4 %collective-permute-start.7 = (bf16[4,80,768]{2,1,0:T(8,128)(2,1)S(1)}, bf16[4,80,768]{2,1,0:T(8,128)(2,1)S(1)}, u32[]{:S(2)}, u32[]{:S(2)}) collective-permute-start(bf16[4,80,768]{2,1,0:T(8,128)(2,1)S(1)} %pad_maximum_fusion.refs_0_), channel_id=1, source_target_pairs={{0,1},{1,0},{2,3},{3,2},{4,5},{5,4},{6,7},{7,6},{8,9},{9,8},{10,11... | collective-permute-start | bytes 1474568 | tf_op jit(solution)/shard_map/ppermute | solution.py:367
  40.0 11.2 %collective-permute-start.5 = (bf16[2,80,768]{2,1,0:T(8,128)(2,1)S(1)}, bf16[2,80,768]{2,1,0:T(8,128)(2,1)S(1)}, u32[]{:S(2)}, u32[]{:S(2)}) collective-permute-start(bf16[2,80,768]{2,1,0:T(8,128)(2,1)S(1)} %slice.95), channel_id=1, source_target_pairs={{0,4},{1,5},{2,6},{3,7},{4,0},{5,1},{6,2},{7,3},{8,12},{9,13},{10,... | collective-permute-start | bytes 737288 | tf_op jit(solution)/shard_map/ppermute | solution.py:367
  41.6 14.8 %collective-permute-start.8 = (bf16[4,80,768]{2,1,0:T(8,128)(2,1)S(1)}, bf16[4,80,768]{2,1,0:T(8,128)(2,1)S(1)}, u32[]{:S(2)}, u32[]{:S(2)}) collective-permute-start(bf16[4,80,768]{2,1,0:T(8,128)(2,1)S(1)} %collective-permute-done.3.refs_1_), channel_id=1, source_target_pairs={{0,1},{1,0},{2,3},{3,2},{4,5},{5,4},{6,7},{7,6},{8,9},{9,8},{10,11... | collective-permute-start | bytes 1474568 | tf_op jit(solution)/shard_map/ppermute | solution.py:367
  41.7 14.8 %collective-permute-start.9 = (bf16[4,80,768]{2,1,0:T(8,128)(2,1)S(1)}, bf16[4,80,768]{2,1,0:T(8,128)(2,1)S(1)}, u32[]{:S(2)}, u32[]{:S(2)}) collective-permute-start(bf16[4,80,768]{2,1,0:T(8,128)(2,1)S(1)} %collective-permute-done.4.refs_2_), channel_id=1, source_target_pairs={{0,1},{1,0},{2,3},{3,2},{4,5},{5,4},{6,7},{7,6},{8,9},{9,8},{10,11... | collective-permute-start | bytes 1474568 | tf_op jit(solution)/shard_map/ppermute | solution.py:367
  42.2 13.4 %collective-permute-start.6 = (bf16[2,80,768]{2,1,0:T(8,128)(2,1)S(1)}, bf16[2,80,768]{2,1,0:T(8,128)(2,1)S(1)}, u32[]{:S(2)}, u32[]{:S(2)}) collective-permute-start(bf16[2,80,768]{2,1,0:T(8,128)(2,1)S(1)} %slice.96), channel_id=1, source_target_pairs={{0,2},{1,3},{2,0},{3,1},{4,6},{5,7},{6,4},{7,5},{8,10},{9,11},{10,... | collective-permute-start | bytes 737288 | tf_op jit(solution)/shard_map/ppermute | solution.py:367
  51.3 5.2 %collective-permute-start.10 = (bf16[2,80,768]{2,1,0:T(8,128)(2,1)S(1)}, bf16[2,80,768]{2,1,0:T(8,128)(2,1)}, u32[]{:S(2)}, u32[]{:S(2)}) collective-permute-start(bf16[2,80,768]{2,1,0:T(8,128)(2,1)S(1)} %collective-permute-done.5.refs_3_), channel_id=1, source_target_pairs={{0,1},{1,0},{2,3},{3,2},{4,5},{5,4},{6,7},{7,6},{8,9},{9,8},{10,11... | collective-permute-start | bytes 737288 | tf_op jit(solution)/shard_map/ppermute | solution.py:367
  55.7 1.6 collective-permute-start.11
  67.2 1.2 copy-start.3
  68.4 0.6 copy-start.12
  69.1 0.6 copy-start.13
  165.3 13.0 %collective-permute-start.13 = (bf16[16,5,24,768]{3,2,1,0:T(8,128)(2,1)S(1)}, bf16[16,5,24,768]{3,2,1,0:T(8,128)(2,1)S(1)}, u32[]{:S(2)}, u32[]{:S(2)}) collective-permute-start(bf16[16,5,24,768]{3,2,1,0:T(8,128)(2,1)S(1)} %get-tuple-element.73), channel_id=1, source_target_pairs={{0,1},{1,0},{2,3},{3,2},{4,5},{5,4},{6,7},{7,6},{8,9},{9,8},{10,11... | collective-permute-start | bytes 8847368 | tf_op jit(solution)/shard_map/ppermute | solution.py:367
  173.7 4.6 %collective-permute-start.12 = (bf16[16,96,768]{2,1,0:T(8,128)(2,1)S(1)}, bf16[16,96,768]{2,1,0:T(8,128)(2,1)S(1)}, u32[]{:S(2)}, u32[]{:S(2)}) collective-permute-start(bf16[16,96,768]{2,1,0:T(8,128)(2,1)S(1)} %get-tuple-element.72), channel_id=1, source_target_pairs={{0,1},{1,0},{2,3},{3,2},{4,5},{5,4},{6,7},{7,6},{8,9},{9,8},{10,11... | collective-permute-start | bytes 7077896 | tf_op jit(solution)/shard_map/ppermute | solution.py:367
  181.9 32.3 %collective-permute-start.15 = (bf16[2,2,216,768]{3,2,1,0:T(8,128)(2,1)}, bf16[2,2,216,768]{3,2,1,0:T(8,128)(2,1)S(1)}, u32[]{:S(2)}, u32[]{:S(2)}) collective-permute-start(bf16[2,2,216,768]{3,2,1,0:T(8,128)(2,1)} %get-tuple-element.77), channel_id=1, source_target_pairs={{0,4},{1,5},{2,6},{3,7},{4,0},{5,1},{6,2},{7,3},{8,12},{9,13},{10,... | collective-permute-start | bytes 3981320 | tf_op jit(solution)/shard_map/ppermute | solution.py:367
  183.5 31.3 %collective-permute-start.14 = (bf16[2,2,216,768]{3,2,1,0:T(8,128)(2,1)}, bf16[2,2,216,768]{3,2,1,0:T(8,128)(2,1)}, u32[]{:S(2)}, u32[]{:S(2)}) collective-permute-start(bf16[2,2,216,768]{3,2,1,0:T(8,128)(2,1)} %get-tuple-element.75), channel_id=1, source_target_pairs={{0,2},{1,3},{2,0},{3,1},{4,6},{5,7},{6,4},{7,5},{8,10},{9,11},{10,... | collective-permute-start | bytes 3981320 | tf_op jit(solution)/shard_map/ppermute | solution.py:367
  214.8 2.4 copy-start.4
  214.8 2.4 copy-start.7
  214.8 2.4 copy-start.8
  224.4 4.0 %collective-permute-start.17 = (bf16[16,48,768]{2,1,0:T(8,128)(2,1)S(1)}, bf16[16,48,768]{2,1,0:T(8,128)(2,1)S(1)}, u32[]{:S(2)}, u32[]{:S(2)}) collective-permute-start(bf16[16,48,768]{2,1,0:T(8,128)(2,1)S(1)} %get-tuple-element.93), channel_id=1, source_target_pairs={{0,1},{1,0},{2,3},{3,2},{4,5},{5,4},{6,7},{7,6},{8,9},{9,8},{10,11... | collective-permute-start | bytes 3538952 | tf_op jit(solution)/shard_map/ppermute | solution.py:367
  224.5 4.0 %collective-permute-start.18 = (bf16[16,32,768]{2,1,0:T(8,128)(2,1)S(1)}, bf16[16,32,768]{2,1,0:T(8,128)(2,1)S(1)}, u32[]{:S(2)}, u32[]{:S(2)}) collective-permute-start(bf16[16,32,768]{2,1,0:T(8,128)(2,1)S(1)} %get-tuple-element.95), channel_id=1, source_target_pairs={{0,1},{1,0},{2,3},{3,2},{4,5},{5,4},{6,7},{7,6},{8,9},{9,8},{10,11... | collective-permute-start | bytes 2359304 | tf_op jit(solution)/shard_map/ppermute | solution.py:367
  225.0 16.9 %collective-permute-start.16 = (bf16[2,216,768]{2,1,0:T(8,128)(2,1)S(1)}, bf16[2,216,768]{2,1,0:T(8,128)(2,1)S(1)}, u32[]{:S(2)}, u32[]{:S(2)}) collective-permute-start(bf16[2,216,768]{2,1,0:T(8,128)(2,1)S(1)} %get-tuple-element.86), channel_id=1, source_target_pairs={{0,4},{1,5},{2,6},{3,7},{4,0},{5,1},{6,2},{7,3},{8,12},{9,13},{10,... | collective-permute-start | bytes 1990664 | tf_op jit(solution)/shard_map/ppermute | solution.py:367
  225.8 16.6 %collective-permute-start.19 = (bf16[2,216,768]{2,1,0:T(8,128)(2,1)S(1)}, bf16[2,216,768]{2,1,0:T(8,128)(2,1)S(1)}, u32[]{:S(2)}, u32[]{:S(2)}) collective-permute-start(bf16[2,216,768]{2,1,0:T(8,128)(2,1)S(1)} %get-tuple-element.88), channel_id=1, source_target_pairs={{0,2},{1,3},{2,0},{3,1},{4,6},{5,7},{6,4},{7,5},{8,10},{9,11},{10,... | collective-permute-start | bytes 1990664 | tf_op jit(solution)/shard_map/ppermute | solution.py:367
  229.5 0.8 copy-start.5
  230.3 0.8 copy-start.9
  231.1 0.8 copy-start.10
  231.9 0.8 copy-start.11
  242.4 5.0 %copy-start = (bf16[1024,768]{1,0:T(8,128)(2,1)S(1)}, bf16[1024,768]{1,0:T(8,128)(2,1)}, u32[]{:S(2)}) copy-start(bf16[1024,768]{1,0:T(8,128)(2,1)} %get-tuple-element.80.refs_0_) | copy-start | bytes 4718596
  242.4 5.0 %copy-start.1 = (bf16[1024,768]{1,0:T(8,128)(2,1)S(1)}, bf16[1024,768]{1,0:T(8,128)(2,1)}, u32[]{:S(2)}) copy-start(bf16[1024,768]{1,0:T(8,128)(2,1)} %get-tuple-element.81.refs_1_) | copy-start | bytes 4718596
  243.9 14.5 %collective-permute-start.20 = (bf16[4,80,768]{2,1,0:T(8,128)(2,1)}, bf16[4,80,768]{2,1,0:T(8,128)(2,1)}, u32[]{:S(2)}, u32[]{:S(2)}) collective-permute-start(bf16[4,80,768]{2,1,0:T(8,128)(2,1)} %copy-done.11), channel_id=1, source_target_pairs={{0,2},{1,3},{2,0},{3,1},{4,6},{5,7},{6,4},{7,5},{8,10},{9,11},{10,... | collective-permute-start | bytes 1474568 | tf_op jit(solution)/shard_map/ppermute | solution.py:367
  245.0 22.6 %collective-permute-start.21 = (bf16[4,80,768]{2,1,0:T(8,128)(2,1)}, bf16[4,80,768]{2,1,0:T(8,128)(2,1)}, u32[]{:S(2)}, u32[]{:S(2)}) collective-permute-start(bf16[4,80,768]{2,1,0:T(8,128)(2,1)} %copy-done.10), channel_id=1, source_target_pairs={{0,4},{1,5},{2,6},{3,7},{4,0},{5,1},{6,2},{7,3},{8,12},{9,13},{10,... | collective-permute-start | bytes 1474568 | tf_op jit(solution)/shard_map/ppermute | solution.py:367
  246.2 21.5 %collective-permute-start.22 = (bf16[4,80,768]{2,1,0:T(8,128)(2,1)}, bf16[4,80,768]{2,1,0:T(8,128)(2,1)}, u32[]{:S(2)}, u32[]{:S(2)}) collective-permute-start(bf16[4,80,768]{2,1,0:T(8,128)(2,1)} %copy-done.9), channel_id=1, source_target_pairs={{0,6},{1,7},{2,4},{3,5},{4,2},{5,3},{6,0},{7,1},{8,14},{9,15},{10,... | collective-permute-start | bytes 1474568 | tf_op jit(solution)/shard_map/ppermute | solution.py:367
  247.5 1.6 copy-start.2
  249.1 18.6 %copy-start.6 = (bf16[4,80,768]{2,1,0:T(8,128)(2,1)S(1)}, bf16[4,80,768]{2,1,0:T(8,128)(2,1)}, u32[]{:S(2)}) copy-start(bf16[4,80,768]{2,1,0:T(8,128)(2,1)} %copy-done.5) | copy-start | bytes 1474564
  269.2 9.0 %collective-permute-start.23 = (bf16[80,768]{1,0:T(8,128)(2,1)S(1)}, bf16[80,768]{1,0:T(8,128)(2,1)S(1)}, u32[]{:S(2)}, u32[]{:S(2)}) collective-permute-start(bf16[80,768]{1,0:T(8,128)(2,1)S(1)} %get-tuple-element.107), channel_id=1, source_target_pairs={{0,8},{1,9},{2,10},{3,11},{4,12},{5,13},{6,14},{7,15},{8,16},{9,17... | collective-permute-start | bytes 368648 | tf_op jit(solution)/shard_map/ppermute | solution.py:367
  270.4 11.3 %collective-permute-start.24 = (bf16[80,768]{1,0:T(8,128)(2,1)S(1)}, bf16[80,768]{1,0:T(8,128)(2,1)S(1)}, u32[]{:S(2)}, u32[]{:S(2)}) collective-permute-start(bf16[80,768]{1,0:T(8,128)(2,1)S(1)} %get-tuple-element.109), channel_id=1, source_target_pairs={{0,16},{1,17},{2,18},{3,19},{4,20},{5,21},{6,22},{7,23},{8,24},{9,... | collective-permute-start | bytes 368648 | tf_op jit(solution)/shard_map/ppermute | solution.py:367
  271.5 10.2 %collective-permute-start.25 = (bf16[80,768]{1,0:T(8,128)(2,1)S(1)}, bf16[80,768]{1,0:T(8,128)(2,1)S(1)}, u32[]{:S(2)}, u32[]{:S(2)}) collective-permute-start(bf16[80,768]{1,0:T(8,128)(2,1)S(1)} %get-tuple-element.108), channel_id=1, source_target_pairs={{0,24},{1,25},{2,26},{3,27},{4,28},{5,29},{6,30},{7,31},{8,0},{9,1... | collective-permute-start | bytes 368648 | tf_op jit(solution)/shard_map/ppermute | solution.py:367
  274.9 1.8 copy-start.14
Sparse Core Ops, SparseCore 0:
  11.5 97.0 all-gather.1
  244.0 30.8 reduce-scatter.1

commit v5 on v4

--- a/solution.py
+++ b/solution.py
@@ -956,73 +956,101 @@
     )(place, left, right)
 
 
-def qkv_grad_kernel(place_ref, turned_ref, sums_ref, up_sums_ref, *refs, part, inner_part):
-    long_refs, short_refs = refs[-4:-2], refs[-2:]
-    stack = refs[:-4]
-    each = len(stack) // 3
+def backward_and_grads_kernel(
+    place_ref, q_ref, k_ref, v_ref, mixed_ref, grad_ref, probs_ref, turned_ref, sums_ref, up_sums_ref,
+    dq_ref, dk_ref, dv_ref, *refs, scale, part, inner_part
+):
+    outs, bias_ref = refs[:-1], refs[-1]
+    stack = (dq_ref, dk_ref, dv_ref)
+    attention_backward_kernel(
+        q_ref, k_ref, v_ref, mixed_ref, grad_ref, probs_ref, *stack, scale=scale
+    )
     width, rows = turned_ref.shape
-    turned = turned_ref[...]
-    ones = jnp.ones((8, rows), BF)
-
-    def joined(left, third):
-        return jnp.concatenate(
-            [dot(left, ref[...]) for ref in stack[third * each : (third + 1) * each]], axis=1
+    pair = pl.program_id(0)
+    joined = jnp.concatenate([ref[...] for ref in stack], axis=1)
+    product = dot(turned_ref[...], joined)
+    totals = dot(jnp.ones((8, rows), BF), joined)
+    bias_ref[pair] = totals
+
+    def tile_of_third(third):
+        lanes = slice(third * PAIR, (third + 1) * PAIR)
+        return lambda owner: product[owner * part : (owner + 1) * part, lanes]
+
+    for third in range(3):
+        split_owners(
+            place_ref, outs[2 * third], outs[2 * third + 1], tile_of_third(third), width // part
         )
 
-    products = [joined(turned, third) for third in range(3)]
-    vectors = jnp.concatenate(
-        [joined(ones, 0)[0:1], joined(ones, 2)[0:1], sums_ref[0:6, :]], axis=0
-    )
-    top = lax.broadcasted_iota(jnp.int32, (8, 1), 0) == 0
-
-    def tile_of(owner):
-        cut = slice(owner * part, (owner + 1) * part)
-        own = pltpu.roll(vectors, width - owner * part, 1) if owner else vectors
-        start = owner * inner_part // PAIR * PAIR
-        long = jnp.concatenate(
-            [up_sums_ref[:, start : start + PAIR], up_sums_ref[:, start + PAIR : start + 2 * PAIR]]
-            if start + 2 * PAIR <= up_sums_ref.shape[1]
-            else [up_sums_ref[:, start : start + PAIR]] * 2,
-            axis=1,
-        )
-        shift = owner * inner_part - start
-        long = pltpu.roll(long, 2 * PAIR - shift, 1) if shift else long
-        extra = jnp.concatenate(
-            [own[:, :PAIR], jnp.where(top, long[:, :PAIR], 0.0), jnp.zeros((8, width - 2 * PAIR), F32)],
-            axis=1,
-        )
-        return jnp.concatenate([products[2][cut], extra], axis=0)
-
-    def long_tile_of(owner):
-        cut = slice(owner * part, (owner + 1) * part)
-        return jnp.concatenate([product[cut] for product in products[:2]], axis=0)
-
-    split_owners(place_ref, *long_refs, long_tile_of, width // part)
-    split_owners(place_ref, *short_refs, tile_of, width // part)
-
-
-def qkv_grad(place, turned, stack, sums, up_sums, count):
-    width, rows = turned.shape
+    @pl.when(pair == pl.num_programs(0) - 1)
+    def _():
+        count = width // PAIR
+        biases = [
+            jnp.concatenate([bias_ref[i][0:1, start : start + PAIR] for i in range(count)], axis=1)
+            for start in (0, 2 * PAIR)
+        ]
+        vectors = jnp.concatenate(biases + [sums_ref[0:6, :]], axis=0)
+        top = lax.broadcasted_iota(jnp.int32, (8, 1), 0) == 0
+
+        def tile_of(owner):
+            own = pltpu.roll(vectors, width - owner * part, 1) if owner else vectors
+            start = owner * inner_part // PAIR * PAIR
+            last = start + 2 * PAIR <= up_sums_ref.shape[1]
+            second = start + PAIR if last else start
+            long = jnp.concatenate(
+                [up_sums_ref[:, start : start + PAIR], up_sums_ref[:, second : second + PAIR]],
+                axis=1,
+            )
+            shift = owner * inner_part - start
+            long = pltpu.roll(long, 2 * PAIR - shift, 1) if shift else long
+            return jnp.concatenate(
+                [own[:, :PAIR], jnp.where(top, long[:, :PAIR], 0.0), jnp.zeros((8, width - 2 * PAIR), F32)],
+                axis=1,
+            )
+
+        split_owners(place_ref, outs[6], outs[7], tile_of, width // part)
+
+
+def backward_and_grads(place, stacked, mixed, grad_mixed, probs, turned, sums, up_sums, count):
+    rows, width = mixed.shape
+    pairs = width // PAIR
     part = width // count
-    outs = [
-        jax.ShapeDtypeStruct((count // 2, tall, width), BF)
-        for tall in (2 * part, 2 * part, part + 8, part + 8)
-    ]
-    return pl.pallas_call(
-        functools.partial(qkv_grad_kernel, part=part, inner_part=up_sums.shape[1] // count),
+    half = count // 2
+    shape = jax.ShapeDtypeStruct
+    slab = pl.BlockSpec((half, part, PAIR), lambda pair, place: (0, 0, pair))
+    extra = shape((half, 8, width), BF)
+    return pl.pallas_call(
+        functools.partial(
+            backward_and_grads_kernel,
+            scale=1.0 / math.sqrt(DH),
+            part=part,
+            inner_part=up_sums.shape[1] // count,
+        ),
         grid_spec=pltpu.PrefetchScalarGridSpec(
             num_scalar_prefetch=1,
-            grid=(1,),
-            in_specs=[whole_block(array) for array in (turned, sums, up_sums, *stack)],
-            out_specs=[whole_block(out) for out in outs],
-        ),
-        out_shape=outs,
-        compiler_params=params(48),
+            grid=(pairs,),
+            in_specs=[
+                pair_spec(rows, 0),
+                pair_spec(rows, pairs),
+                pair_spec(rows, 2 * pairs),
+                pair_spec(rows, 0),
+                pair_spec(rows, 0),
+                pl.BlockSpec((2, rows, rows), lambda pair, place: (pair, 0, 0)),
+                whole_block(turned),
+                whole_block(sums),
+                whole_block(up_sums),
+            ],
+            out_specs=[pair_spec(rows, 0)] * 3 + [slab] * 6 + [whole_block(extra)] * 2,
+            scratch_shapes=[pltpu.VMEM((pairs, 8, 3 * PAIR), F32)],
+        ),
+        out_shape=[shape((rows, width), BF)] * 3
+        + [shape((half, part, width), BF)] * 6
+        + [extra] * 2,
+        compiler_params=params(60),
         cost_estimate=pl.CostEstimate(
             flops=rows * width, bytes_accessed=rows * width, transcendentals=0
         ),
-        name="grad_w_qkv",
-    )(place, turned, sums, up_sums, *stack)
+        name="attention_backward_grads",
+    )(place, *[stacked] * 3, mixed, grad_mixed, probs, turned, sums, up_sums)
 
 
 def hidden_grad_kernel(grad_sum_ref, weight_ref, *refs):
@@ -1090,18 +1118,19 @@
     up_keep, up_came = (array.reshape(n // 2, -1, width) for array in (up_keep, up_came))
     keep, by_x, by_y = first_sum(place, (down_keep, down_came), (up_keep, up_came))
     from_x, from_y = moved(by_x, NEAR[0]), moved(by_y, NEAR[1])
-    stack = attention_backward(stacked, mixed, after(grad_mixed, by_x, by_y), probs)
+    stack = backward_and_grads(
+        place, stacked, mixed, after(grad_mixed, by_x, by_y), probs, hidden_turned, sums, up_sums, n
+    )
+    stack, qkv_halves = stack[:3], stack[3:]
     own, by_y, by_x = second_sum(place, keep, after(from_x, *stack), after(from_y, *stack))
     low, high = moved(by_y, NEAR[1]), moved(by_x, NEAR[0])
-    long_keep, long_send, short_keep, short_send = qkv_grad(
-        place, after(hidden_turned, by_x, by_y), stack, sums, up_sums, n
-    )
-    long_came, short_came = moved(long_send, core), moved(short_send, core)
-    here, *sends = near_sum(place, (long_keep, long_came), (short_keep, short_came))
+    qkv_pairs = [(qkv_halves[i], moved(qkv_halves[i + 1], core)) for i in (0, 2, 4, 6)]
+    here, *sends = near_sum(place, *qkv_pairs)
     total = far_add(own, after(low, *sends), after(high, *sends))
     grad_hidden = hidden_grad(after(grad_sum, total), whole_qkv, stack)
     total = far_scatter(total)
     qkv_parts = send_near(sends)
+    qkv_parts = [after(part, grad_hidden) for part in qkv_parts]
     qkv_mine, qkv_far = reduce_far([here] + qkv_parts, coords)
     my_up_out = total[inner_part:].reshape(wide + 1, part, width)
     my_down = total[:inner_part]

time: 292 us -> 293 us (level)
    ppermute x26 -> x28, waiting for transfers between devices: 60.1 us -> 59.1 us  [moved(): return lax.ppermute(array, 'fsdp', pairs)]
    ppermute x26 -> x28, starting transfers between devices: 27.1 us -> 27.4 us  [moved(): return lax.ppermute(array, 'fsdp', pairs)]
    pallas_call x2 -> x1, Pallas kernels: 37.4 us -> 37.7 us  [backward_and_grads(): pl.pallas_call(functools.partial(backward_and_grads_kernel, scale=1.0 / m...]
    unnamed x32 -> x42, local copies, waits for them, and re-layouts: 7.25 us -> 7.28 us
  transfers between devices with their start and end apart: 28 -> 30, of which waited for: 16 -> 17; matrix products, arithmetic and copies ran while one was open for 3% -> 3% of each run, Pallas kernels for 30% -> 33%
where the time goes in v5:
time: 293 us; the launch traced here: 292 us
  Pallas kernels  158 us (54%)
  waiting for transfers between devices  71.6 us (24%)
  starting transfers between devices  27.5 us (9%)
  between operations  14.3 us (5%)
  local copies, waits for them, and re-layouts  12.8 us (4%)
  other arithmetic  7.61 us (3%)
    ppermute x28, waiting for transfers between devices, moved(): return lax.ppermute(array, 'fsdp', pairs)  59.1 us
    pallas_call x1, Pallas kernels, row_pass(): pl.pallas_call(functools.partial(row_pass_kernel, part=part, chunk=chunk)...  46.4 us
    pallas_call x1, Pallas kernels, backward_and_grads(): pl.pallas_call(functools.partial(backward_and_grads_kernel, scale=1.0 / m...  37.7 us
    ppermute x28, starting transfers between devices, moved(): return lax.ppermute(array, 'fsdp', pairs)  27.4 us
    pallas_call x1, Pallas kernels, attention_forward(): pl.pallas_call(functools.partial(attention_forward_kernel, scale=1.0 / ma...  27.3 us
    all_gather x1, waiting for transfers between devices, meshed_layer(): lax.all_gather(pack_weights(w_down, w_up, w_out), 'fsdp', axis=0, tiled=T...  11.6 us
    pallas_call x1, Pallas kernels, up_grad(): pl.pallas_call(up_grad_kernel, grid_spec=pltpu.PrefetchScalarGridSpec(num...  10.3 us
    pallas_call x1, Pallas kernels, project(): pl.pallas_call(functools.partial(project_kernel, part=width // count, inn...  9.92 us
  transfers between devices with their start and end apart: 30, of which 17 were waited for; matrix products, arithmetic and copies ran while one was open for 3% of the time, Pallas kernels for 33%

profile of v5, /device:TPU:0, one launch (start us, length us, event | category | flops | bytes accessed | tf_op | source)
XLA Modules:
  0.0 292.2 jit_solution(2363640249760411511)
XLA Ops:
  7.2 1.7 pack_weights.1
  9.0 1.4 stack.70.vector_ref
  10.4 1.6 pack_front.1
  12.0 3.0 %collective-permute-start = (bf16[80,768]{1,0:T(8,128)(2,1)}, bf16[80,768]{1,0:T(8,128)(2,1)S(1)}, u32[]{:S(2)}, u32[]{:S(2)}) collective-permute-start(bf16[80,768]{1,0:T(8,128)(2,1)} %pack_front.1), channel_id=1, source_target_pairs={{0,8},{1,9},{2,10},{3,11},{4,12},{5,13},{6,14},{7,15},{8,16},{9,17... | collective-permute-start | bytes 368648 | tf_op jit(solution)/shard_map/ppermute | solution.py:367
  15.0 2.6 collective-permute-start.1
  17.6 1.3 collective-permute-start.2
  19.0 2.5 collective-permute-done
  21.5 4.4 %collective-permute-done.1 = bf16[80,768]{1,0:T(8,128)(2,1)S(1)} collective-permute-done((bf16[80,768]{1,0:T(8,128)(2,1)}, bf16[80,768]{1,0:T(8,128)(2,1)S(1)}, u32[]{:S(2)}, u32[]{:S(2)}) %collective-permute-start.1) | collective-permute-done | bytes 122912 | tf_op jit(solution)/shard_map/ppermute | solution.py:367
  25.9 1.0 pad_maximum_fusion.refs_0_
  26.9 1.6 collective-permute-start.3
  28.5 1.5 collective-permute-start.4
  30.0 10.0 %collective-permute-done.3.refs_1_ = bf16[4,80,768]{2,1,0:T(8,128)(2,1)S(1)} collective-permute-done((bf16[4,80,768]{2,1,0:T(8,128)(2,1)S(1)}, bf16[4,80,768]{2,1,0:T(8,128)(2,1)S(1)}, u32[]{:S(2)}, u32[]{:S(2)}) %collective-permute-start.3) | collective-permute-done | bytes 491552 | tf_op jit(solution)/shard_map/ppermute | solution.py:367
  40.0 1.6 collective-permute-start.5
  42.2 1.5 collective-permute-start.6
  43.7 7.6 %collective-permute-done.5.refs_3_ = bf16[2,80,768]{2,1,0:T(8,128)(2,1)S(1)} collective-permute-done((bf16[2,80,768]{2,1,0:T(8,128)(2,1)S(1)}, bf16[2,80,768]{2,1,0:T(8,128)(2,1)S(1)}, u32[]{:S(2)}, u32[]{:S(2)}) %collective-permute-start.5) | collective-permute-done | bytes 245792 | tf_op jit(solution)/shard_map/ppermute | solution.py:367
  51.3 4.3 %collective-permute-done.6.refs_4_ = bf16[2,80,768]{2,1,0:T(8,128)(2,1)S(1)} collective-permute-done((bf16[2,80,768]{2,1,0:T(8,128)(2,1)S(1)}, bf16[2,80,768]{2,1,0:T(8,128)(2,1)S(1)}, u32[]{:S(2)}, u32[]{:S(2)}) %collective-permute-start.6) | collective-permute-done | bytes 245792 | tf_op jit(solution)/shard_map/ppermute | solution.py:367
  55.7 0.7 reduce-window.9
  56.5 0.8 collective-permute-done.11.refs_9_
  57.3 9.9 %project.1 = (bf16[1024,2304]{1,0:T(8,128)(2,1)}, bf16[768,2304]{1,0:T(8,128)(2,1)}, f32[8,768]{1,0:T(8,128)S(1)}, f32[8,3072]{1,0:T(8,128)S(1)}, bf16[768,1024]{1,0:T(8,128)(2,1)S(1)}) custom-call(s32[4]{0:T(128)S(1)} %pad_add_fusion.place_ref, bf16[1024,768]{1,0:T(8,128)(2,1)} %hidden_ref.3, bf16[4,80,768]{2,1,0:T(8,128)(2,1)S(1)} %pad_maximum_fusion.refs_0_, ...), custom_call_target="tpu_custom_call" | custom-call | tf_op jit(solution)/shard_map/project/pallas_call | solution.py:666
  67.2 1.2 copy-done.3
  68.4 0.6 copy-done.15
  69.1 0.6 copy-done.16
  69.7 27.3 %attention_forward.1 = (bf16[1024,768]{1,0:T(8,128)(2,1)}, bf16[12,1024,1024]{2,1,0:T(8,128)(2,1)}) custom-call(s32[2]{0:T(128)} %bitcast.66, bf16[1024,2304]{1,0:T(8,128)(2,1)} %get-tuple-element.67.q_ref.k_ref.v_ref, bf16[1024,2304]{1,0:T(8,128)(2,1)} %get-tuple-element.67.q_ref.k_ref.v_ref, bf16[1024,2304]{1,0:T(8,128)(2,1)} %get-tuple-element.67.q_ref.k_ref.v_ref), custom_call_target="tpu_custom_call" | custom-call | flops 786432 | bytes 786432 | tf_op jit(solution)/shard_map/attention_forward/pallas_call | solution.py:90
  97.0 11.6 %all-gather.2.cloned.1.call-done = bf16[7168,768]{1,0:T(8,128)(2,1)} async-done(((bf16[224,768]{1,0:T(8,128)(2,1)}), bf16[7168,768]{1,0:T(8,128)(2,1)}) %all-gather.2.cloned.1.call-update) | async-done | bytes 11010064 | tf_op jit(solution)/shard_map/all_gather | solution.py:1099
  108.6 46.4 %row_pass.1 = (f32[1024,768]{1,0:T(8,128)}, bf16[4608,1024]{1,0:T(8,128)(2,1)}, bf16[1024,4608]{1,0:T(8,128)(2,1)}, f32[1024,768]{1,0:T(8,128)}, bf16[1024,768]{...) custom-call(s32[2]{0:T(128)} %bitcast.67, bf16[1024,768]{1,0:T(8,128)(2,1)} %get-tuple-element.68.mixed_ref, ...), custom_call_target="tpu_custom_call" | custom-call | flops 21743271936 | bytes 31457280 | tf_op jit(solution)/shard_map/row_pass/pallas_call | solution.py:834
  154.9 10.3 %grad_w_up_out.1 = (bf16[16,5,24,768]{3,2,1,0:T(8,128)(2,1)S(1)}, bf16[16,5,24,768]{3,2,1,0:T(8,128)(2,1)S(1)}) custom-call(s32[4]{0:T(128)S(1)} %pad_add_fusion.place_ref, bf16[4608,1024]{1,0:T(8,128)(2,1)} %get-tuple-element.76.left_ref, bf16[1024,4608]{1,0:T(8,128)(2,1)} %get-tuple-element.74.right_ref), custom_call_target="tpu_custom_call" | custom-call | flops 786432 | bytes 786432 | tf_op jit(solution)/shard_map/grad_w_up_out/pallas_call | solution.py:939
  165.6 8.0 %grad_w_down.1 = (bf16[16,96,768]{2,1,0:T(8,128)(2,1)S(1)}, bf16[16,96,768]{2,1,0:T(8,128)(2,1)S(1)}) custom-call(s32[4]{0:T(128)S(1)} %pad_add_fusion.place_ref, bf16[4608,1024]{1,0:T(8,128)(2,1)} %get-tuple-element.76.left_ref, bf16[1024,4608]{1,0:T(8,128)(2,1)} %get-tuple-element.74.right_ref), custom_call_target="tpu_custom_call" | custom-call | flops 786432 | bytes 786432 | tf_op jit(solution)/shard_map/grad_w_down/pallas_call | solution.py:905
  174.0 4.3 %collective-permute-done.12.refs_1_ = bf16[16,96,768]{2,1,0:T(8,128)(2,1)S(1)} collective-permute-done((bf16[16,96,768]{2,1,0:T(8,128)(2,1)S(1)}, bf16[16,96,768]{2,1,0:T(8,128)(2,1)S(1)}, u32[]{:S(2)}, u32[]{:S(2)}) %collective-permute-start.12) | collective-permute-done | bytes 2359328 | tf_op jit(solution)/shard_map/ppermute | solution.py:367
  178.2 3.6 %first_sum.1 = (bf16[4,2,216,768]{3,2,1,0:T(8,128)(2,1)S(1)}, bf16[2,2,216,768]{3,2,1,0:T(8,128)(2,1)}, bf16[2,2,216,768]{3,2,1,0:T(8,128)(2,1)}) custom-call(s32[4]{0:T(128)S(1)} %pad_add_fusion.place_ref, bf16[16,96,768]{2,1,0:T(8,128)(2,1)S(1)} %get-tuple-element.77.refs_0_, bf16[16,96,768]{2,1,0:T(8,128)(2,1)S(1)} %collective-permute-done.12.refs_1_, ...), custom_call_target="tpu_custom_call" | custom-call | flops 1327104 | bytes 1327104 | tf_op jit(solution)/shard_map/first_sum/pallas_call | solution.py:505
  181.8 1.5 collective-permute-start.15
  183.8 37.7 %attention_backward_grads.1 = (bf16[1024,768]{1,0:T(8,128)(2,1)}, bf16[1024,768]{1,0:T(8,128)(2,1)}, bf16[1024,768]{1,0:T(8,128)(2,1)}, bf16[16,24,768]{2,1,0:T(...) custom-call(s32[4]{0:T(128)} %copy-done.10, ...), custom_call_target="tpu_custom_call" | custom-call | flops 786432 | bytes 786432 | tf_op jit(solution)/shard_map/attention_backward_grads/pallas_call | solution.py:1021
  221.8 2.7 second_sum.1
  224.5 1.5 collective-permute-start.16
  227.1 1.4 collective-permute-done.17.refs_1_
  228.6 0.8 collective-permute-done.18.refs_3_
  229.4 0.8 collective-permute-done.19.refs_5_
  230.3 1.1 near_sum.1
  231.4 0.8 copy-done.7
  232.2 0.8 copy-done.12
  232.9 0.8 copy-done.13
  233.8 0.8 copy-done.14
  234.6 7.3 %collective-permute-done.16 = bf16[2,216,768]{2,1,0:T(8,128)(2,1)S(1)} collective-permute-done((bf16[2,216,768]{2,1,0:T(8,128)(2,1)S(1)}, bf16[2,216,768]{2,1,0:T(8,128)(2,1)S(1)}, u32[]{:S(2)}, u32[]{:S(2)}) %collective-permute-start.16) | collective-permute-done | bytes 663584 | tf_op jit(solution)/shard_map/ppermute | solution.py:367
  241.8 1.1 collective-permute-done.21
  243.0 1.4 add_convert_fusion
  244.4 0.7 collective-permute-start.22
  245.1 1.5 collective-permute-start.23
  246.6 1.4 collective-permute-start.24
  248.0 1.6 copy-done.2
  249.6 8.0 %grad_hidden.1 = f32[1024,768]{1,0:T(8,128)} custom-call(f32[1024,768]{1,0:T(8,128)} %get-tuple-element.110.grad_sum_ref, bf16[768,2304]{1,0:T(8,128)(2,1)} %get-tuple-element.111.weight_ref, bf16[1024,768]{1,0:T(8,128)(2,1)S(1)} %copy-done, bf16[1024,768]{1,0:T(8,128)(2,1)S(1)} %copy-done.1, bf16[1024,768]{1,0:T(8,128)(2,1)S(1)} %copy-done.2), custom_call_target="tpu_custom_call" | custom-call | flops 786432 | bytes 786432 | tf_op jit(solution)/shard_map/grad_hidden/pallas_call | solution.py:1070
  257.6 1.3 collective-permute-done.22
  259.0 9.3 %collective-permute-done.23 = bf16[4,80,768]{2,1,0:T(8,128)(2,1)} collective-permute-done((bf16[4,80,768]{2,1,0:T(8,128)(2,1)}, bf16[4,80,768]{2,1,0:T(8,128)(2,1)}, u32[]{:S(2)}, u32[]{:S(2)}) %collective-permute-start.23) | collective-permute-done | bytes 491552 | tf_op jit(solution)/shard_map/ppermute | solution.py:367
  268.2 1.5 fusion
  269.8 1.2 collective-permute-start.25
  271.0 1.1 collective-permute-start.26
  272.1 2.4 collective-permute-start.27
  274.5 0.8 reduce-scatter.2.cloned.1.call-done
  275.3 1.0 convert_element_type.100
  276.4 0.7 slice_bitcast_fusion
  277.1 0.9 slice.97
  278.0 0.7 copy.32
  278.8 0.6 slice_bitcast_fusion.1
  279.4 2.9 %collective-permute-done.26 = bf16[80,768]{1,0:T(8,128)(2,1)S(1)} collective-permute-done((bf16[80,768]{1,0:T(8,128)(2,1)S(1)}, bf16[80,768]{1,0:T(8,128)(2,1)S(1)}, u32[]{:S(2)}, u32[]{:S(2)}) %collective-permute-start.26) | collective-permute-done | bytes 122912 | tf_op jit(solution)/shard_map/ppermute | solution.py:367
  282.3 1.2 bitcast_add_fusion
  284.6 0.7 pad_maximum_fusion.1
  (70 shorter events, 4.4 us)
Async XLA Ops:
  7.2 48.5 %copy-start.20 = (s32[2]{0:T(128)S(1)}, s32[2]{0:T(128)}, u32[]{:S(2)}) copy-start(s32[2]{0:T(128)} %param.17) | copy-start | bytes 28
  7.2 101.4 %all-gather.2.cloned.1.call-start = ((), (), s32[]{:S(2)}) async-start(), calls=%async_computation.1 | async-start | bytes 11354112 | tf_op jit(solution)/shard_map/all_gather | solution.py:1099
  9.0 266.3 %reduce-scatter.2.cloned.1.call-start = ((), (), s32[]{:S(2)}) async-start(), calls=%async_computation.2 | async-start | bytes 1658880 | tf_op jit(solution)/shard_map/reduce_scatter | solution.py:578
  12.0 9.5 %collective-permute-start = (bf16[80,768]{1,0:T(8,128)(2,1)}, bf16[80,768]{1,0:T(8,128)(2,1)S(1)}, u32[]{:S(2)}, u32[]{:S(2)}) collective-permute-start(bf16[80,768]{1,0:T(8,128)(2,1)} %pack_front.1), channel_id=1, source_target_pairs={{0,8},{1,9},{2,10},{3,11},{4,12},{5,13},{6,14},{7,15},{8,16},{9,17... | collective-permute-start | bytes 368648 | tf_op jit(solution)/shard_map/ppermute | solution.py:367
  15.0 10.9 %collective-permute-start.1 = (bf16[80,768]{1,0:T(8,128)(2,1)}, bf16[80,768]{1,0:T(8,128)(2,1)S(1)}, u32[]{:S(2)}, u32[]{:S(2)}) collective-permute-start(bf16[80,768]{1,0:T(8,128)(2,1)} %pack_front.1), channel_id=1, source_target_pairs={{0,16},{1,17},{2,18},{3,19},{4,20},{5,21},{6,22},{7,23},{8,24},{9,... | collective-permute-start | bytes 368648 | tf_op jit(solution)/shard_map/ppermute | solution.py:367
  17.6 8.3 %collective-permute-start.2 = (bf16[80,768]{1,0:T(8,128)(2,1)}, bf16[80,768]{1,0:T(8,128)(2,1)S(1)}, u32[]{:S(2)}, u32[]{:S(2)}) collective-permute-start(bf16[80,768]{1,0:T(8,128)(2,1)} %pack_front.1), channel_id=1, source_target_pairs={{0,24},{1,25},{2,26},{3,27},{4,28},{5,29},{6,30},{7,31},{8,0},{9,1... | collective-permute-start | bytes 368648 | tf_op jit(solution)/shard_map/ppermute | solution.py:367
  26.9 13.1 %collective-permute-start.3 = (bf16[4,80,768]{2,1,0:T(8,128)(2,1)S(1)}, bf16[4,80,768]{2,1,0:T(8,128)(2,1)S(1)}, u32[]{:S(2)}, u32[]{:S(2)}) collective-permute-start(bf16[4,80,768]{2,1,0:T(8,128)(2,1)S(1)} %pad_maximum_fusion.refs_0_), channel_id=1, source_target_pairs={{0,2},{1,3},{2,0},{3,1},{4,6},{5,7},{6,4},{7,5},{8,10},{9,11},{10,... | collective-permute-start | bytes 1474568 | tf_op jit(solution)/shard_map/ppermute | solution.py:367
  28.5 13.2 %collective-permute-start.4 = (bf16[4,80,768]{2,1,0:T(8,128)(2,1)S(1)}, bf16[4,80,768]{2,1,0:T(8,128)(2,1)S(1)}, u32[]{:S(2)}, u32[]{:S(2)}) collective-permute-start(bf16[4,80,768]{2,1,0:T(8,128)(2,1)S(1)} %pad_maximum_fusion.refs_0_), channel_id=1, source_target_pairs={{0,4},{1,5},{2,6},{3,7},{4,0},{5,1},{6,2},{7,3},{8,12},{9,13},{10,... | collective-permute-start | bytes 1474568 | tf_op jit(solution)/shard_map/ppermute | solution.py:367
  30.0 26.4 %collective-permute-start.7 = (bf16[4,80,768]{2,1,0:T(8,128)(2,1)S(1)}, bf16[4,80,768]{2,1,0:T(8,128)(2,1)S(1)}, u32[]{:S(2)}, u32[]{:S(2)}) collective-permute-start(bf16[4,80,768]{2,1,0:T(8,128)(2,1)S(1)} %pad_maximum_fusion.refs_0_), channel_id=1, source_target_pairs={{0,1},{1,0},{2,3},{3,2},{4,5},{5,4},{6,7},{7,6},{8,9},{9,8},{10,11... | collective-permute-start | bytes 1474568 | tf_op jit(solution)/shard_map/ppermute | solution.py:367
  40.0 11.3 %collective-permute-start.5 = (bf16[2,80,768]{2,1,0:T(8,128)(2,1)S(1)}, bf16[2,80,768]{2,1,0:T(8,128)(2,1)S(1)}, u32[]{:S(2)}, u32[]{:S(2)}) collective-permute-start(bf16[2,80,768]{2,1,0:T(8,128)(2,1)S(1)} %slice.95), channel_id=1, source_target_pairs={{0,4},{1,5},{2,6},{3,7},{4,0},{5,1},{6,2},{7,3},{8,12},{9,13},{10,... | collective-permute-start | bytes 737288 | tf_op jit(solution)/shard_map/ppermute | solution.py:367
  41.6 14.8 %collective-permute-start.8 = (bf16[4,80,768]{2,1,0:T(8,128)(2,1)S(1)}, bf16[4,80,768]{2,1,0:T(8,128)(2,1)S(1)}, u32[]{:S(2)}, u32[]{:S(2)}) collective-permute-start(bf16[4,80,768]{2,1,0:T(8,128)(2,1)S(1)} %collective-permute-done.3.refs_1_), channel_id=1, source_target_pairs={{0,1},{1,0},{2,3},{3,2},{4,5},{5,4},{6,7},{7,6},{8,9},{9,8},{10,11... | collective-permute-start | bytes 1474568 | tf_op jit(solution)/shard_map/ppermute | solution.py:367
  41.7 14.8 %collective-permute-start.9 = (bf16[4,80,768]{2,1,0:T(8,128)(2,1)S(1)}, bf16[4,80,768]{2,1,0:T(8,128)(2,1)S(1)}, u32[]{:S(2)}, u32[]{:S(2)}) collective-permute-start(bf16[4,80,768]{2,1,0:T(8,128)(2,1)S(1)} %collective-permute-done.4.refs_2_), channel_id=1, source_target_pairs={{0,1},{1,0},{2,3},{3,2},{4,5},{5,4},{6,7},{7,6},{8,9},{9,8},{10,11... | collective-permute-start | bytes 1474568 | tf_op jit(solution)/shard_map/ppermute | solution.py:367
  42.2 13.4 %collective-permute-start.6 = (bf16[2,80,768]{2,1,0:T(8,128)(2,1)S(1)}, bf16[2,80,768]{2,1,0:T(8,128)(2,1)S(1)}, u32[]{:S(2)}, u32[]{:S(2)}) collective-permute-start(bf16[2,80,768]{2,1,0:T(8,128)(2,1)S(1)} %slice.96), channel_id=1, source_target_pairs={{0,2},{1,3},{2,0},{3,1},{4,6},{5,7},{6,4},{7,5},{8,10},{9,11},{10,... | collective-permute-start | bytes 737288 | tf_op jit(solution)/shard_map/ppermute | solution.py:367
  51.3 5.1 %collective-permute-start.10 = (bf16[2,80,768]{2,1,0:T(8,128)(2,1)S(1)}, bf16[2,80,768]{2,1,0:T(8,128)(2,1)}, u32[]{:S(2)}, u32[]{:S(2)}) collective-permute-start(bf16[2,80,768]{2,1,0:T(8,128)(2,1)S(1)} %collective-permute-done.5.refs_3_), channel_id=1, source_target_pairs={{0,1},{1,0},{2,3},{3,2},{4,5},{5,4},{6,7},{7,6},{8,9},{9,8},{10,11... | collective-permute-start | bytes 737288 | tf_op jit(solution)/shard_map/ppermute | solution.py:367
  55.7 1.6 collective-permute-start.11
  56.4 121.8 %copy-start.10 = (s32[4]{0:T(128)}, s32[4]{0:T(128)S(1)}, u32[]{:S(2)}) copy-start(s32[4]{0:T(128)S(1)} %pad_add_fusion.place_ref) | copy-start | bytes 52
  67.2 1.2 copy-start.3
  68.4 0.6 copy-start.15
  69.1 0.6 copy-start.16
  165.3 13.0 %collective-permute-start.13 = (bf16[16,5,24,768]{3,2,1,0:T(8,128)(2,1)S(1)}, bf16[16,5,24,768]{3,2,1,0:T(8,128)(2,1)S(1)}, u32[]{:S(2)}, u32[]{:S(2)}) collective-permute-start(bf16[16,5,24,768]{3,2,1,0:T(8,128)(2,1)S(1)} %get-tuple-element.79), channel_id=1, source_target_pairs={{0,1},{1,0},{2,3},{3,2},{4,5},{5,4},{6,7},{7,6},{8,9},{9,8},{10,11... | collective-permute-start | bytes 8847368 | tf_op jit(solution)/shard_map/ppermute | solution.py:367
  173.6 4.6 %collective-permute-start.12 = (bf16[16,96,768]{2,1,0:T(8,128)(2,1)S(1)}, bf16[16,96,768]{2,1,0:T(8,128)(2,1)S(1)}, u32[]{:S(2)}, u32[]{:S(2)}) collective-permute-start(bf16[16,96,768]{2,1,0:T(8,128)(2,1)S(1)} %get-tuple-element.78), channel_id=1, source_target_pairs={{0,1},{1,0},{2,3},{3,2},{4,5},{5,4},{6,7},{7,6},{8,9},{9,8},{10,11... | collective-permute-start | bytes 7077896 | tf_op jit(solution)/shard_map/ppermute | solution.py:367
  181.8 39.9 %collective-permute-start.15 = (bf16[2,2,216,768]{3,2,1,0:T(8,128)(2,1)}, bf16[2,2,216,768]{3,2,1,0:T(8,128)(2,1)S(1)}, u32[]{:S(2)}, u32[]{:S(2)}) collective-permute-start(bf16[2,2,216,768]{3,2,1,0:T(8,128)(2,1)} %get-tuple-element.83), channel_id=1, source_target_pairs={{0,4},{1,5},{2,6},{3,7},{4,0},{5,1},{6,2},{7,3},{8,12},{9,13},{10,... | collective-permute-start | bytes 3981320 | tf_op jit(solution)/shard_map/ppermute | solution.py:367
  183.3 38.4 %collective-permute-start.14 = (bf16[2,2,216,768]{3,2,1,0:T(8,128)(2,1)}, bf16[2,2,216,768]{3,2,1,0:T(8,128)(2,1)}, u32[]{:S(2)}, u32[]{:S(2)}) collective-permute-start(bf16[2,2,216,768]{3,2,1,0:T(8,128)(2,1)} %get-tuple-element.81), channel_id=1, source_target_pairs={{0,2},{1,3},{2,0},{3,1},{4,6},{5,7},{6,4},{7,5},{8,10},{9,11},{10,... | collective-permute-start | bytes 3981320 | tf_op jit(solution)/shard_map/ppermute | solution.py:367
  183.8 37.8 %copy-start.11 = (s32[4]{0:T(128)S(1)}, s32[4]{0:T(128)}, u32[]{:S(2)}) copy-start(s32[4]{0:T(128)} %copy-done.10) | copy-start | bytes 52
  221.6 5.5 %collective-permute-start.20 = (bf16[16,8,768]{2,1,0:T(8,128)(2,1)}, bf16[16,8,768]{2,1,0:T(8,128)(2,1)S(1)}, u32[]{:S(2)}, u32[]{:S(2)}) collective-permute-start(bf16[16,8,768]{2,1,0:T(8,128)(2,1)} %get-tuple-element.103), channel_id=1, source_target_pairs={{0,1},{1,0},{2,3},{3,2},{4,5},{5,4},{6,7},{7,6},{8,9},{9,8},{10,11... | collective-permute-start | bytes 589832 | tf_op jit(solution)/shard_map/ppermute | solution.py:367
  221.7 4.9 %copy-start.19 = (bf16[16,24,768]{2,1,0:T(8,128)(2,1)S(1)}, bf16[16,24,768]{2,1,0:T(8,128)(2,1)}, u32[]{:S(2)}) copy-start(bf16[16,24,768]{2,1,0:T(8,128)(2,1)} %get-tuple-element.97) | copy-start | bytes 1769476
  221.7 4.9 %copy-start.18 = (bf16[16,24,768]{2,1,0:T(8,128)(2,1)S(1)}, bf16[16,24,768]{2,1,0:T(8,128)(2,1)}, u32[]{:S(2)}) copy-start(bf16[16,24,768]{2,1,0:T(8,128)(2,1)} %get-tuple-element.99) | copy-start | bytes 1769476
  221.7 5.4 %copy-start.17 = (bf16[16,24,768]{2,1,0:T(8,128)(2,1)S(1)}, bf16[16,24,768]{2,1,0:T(8,128)(2,1)}, u32[]{:S(2)}) copy-start(bf16[16,24,768]{2,1,0:T(8,128)(2,1)} %get-tuple-element.101) | copy-start | bytes 1769476
  221.7 8.5 %copy-start.4 = (bf16[16,24,768]{2,1,0:T(8,128)(2,1)S(1)}, bf16[16,24,768]{2,1,0:T(8,128)(2,1)}, u32[]{:S(2)}) copy-start(bf16[16,24,768]{2,1,0:T(8,128)(2,1)} %get-tuple-element.96.refs_0_) | copy-start | bytes 1769476
  221.7 8.5 %copy-start.5 = (bf16[16,24,768]{2,1,0:T(8,128)(2,1)S(1)}, bf16[16,24,768]{2,1,0:T(8,128)(2,1)}, u32[]{:S(2)}) copy-start(bf16[16,24,768]{2,1,0:T(8,128)(2,1)} %get-tuple-element.98.refs_2_) | copy-start | bytes 1769476
  221.7 8.5 %copy-start.6 = (bf16[16,24,768]{2,1,0:T(8,128)(2,1)S(1)}, bf16[16,24,768]{2,1,0:T(8,128)(2,1)}, u32[]{:S(2)}) copy-start(bf16[16,24,768]{2,1,0:T(8,128)(2,1)} %get-tuple-element.100.refs_4_) | copy-start | bytes 1769476
  221.7 8.5 %copy-start.9 = (bf16[16,8,768]{2,1,0:T(8,128)(2,1)S(1)}, bf16[16,8,768]{2,1,0:T(8,128)(2,1)}, u32[]{:S(2)}) copy-start(bf16[16,8,768]{2,1,0:T(8,128)(2,1)} %get-tuple-element.102.refs_6_) | copy-start | bytes 589828
  224.5 17.4 %collective-permute-start.16 = (bf16[2,216,768]{2,1,0:T(8,128)(2,1)S(1)}, bf16[2,216,768]{2,1,0:T(8,128)(2,1)S(1)}, u32[]{:S(2)}, u32[]{:S(2)}) collective-permute-start(bf16[2,216,768]{2,1,0:T(8,128)(2,1)S(1)} %get-tuple-element.95), channel_id=1, source_target_pairs={{0,4},{1,5},{2,6},{3,7},{4,0},{5,1},{6,2},{7,3},{8,12},{9,13},{10,... | collective-permute-start | bytes 1990664 | tf_op jit(solution)/shard_map/ppermute | solution.py:367
  225.9 17.0 %collective-permute-start.21 = (bf16[2,216,768]{2,1,0:T(8,128)(2,1)S(1)}, bf16[2,216,768]{2,1,0:T(8,128)(2,1)S(1)}, u32[]{:S(2)}, u32[]{:S(2)}) collective-permute-start(bf16[2,216,768]{2,1,0:T(8,128)(2,1)S(1)} %get-tuple-element.108), channel_id=1, source_target_pairs={{0,2},{1,3},{2,0},{3,1},{4,6},{5,7},{6,4},{7,5},{8,10},{9,11},{10,... | collective-permute-start | bytes 1990664 | tf_op jit(solution)/shard_map/ppermute | solution.py:367
  226.5 2.0 collective-permute-start.17
  226.6 2.8 collective-permute-start.18
  227.1 3.2 %collective-permute-start.19 = (bf16[16,24,768]{2,1,0:T(8,128)(2,1)S(1)}, bf16[16,24,768]{2,1,0:T(8,128)(2,1)S(1)}, u32[]{:S(2)}, u32[]{:S(2)}) collective-permute-start(bf16[16,24,768]{2,1,0:T(8,128)(2,1)S(1)} %copy-done.17), channel_id=1, source_target_pairs={{0,1},{1,0},{2,3},{3,2},{4,5},{5,4},{6,7},{7,6},{8,9},{9,8},{10,11... | collective-permute-start | bytes 1769480 | tf_op jit(solution)/shard_map/ppermute | solution.py:367
  231.4 0.8 copy-start.7
  232.2 0.8 copy-start.12
  232.9 0.8 copy-start.13
  233.8 0.8 copy-start.14
  242.9 5.0 %copy-start = (bf16[1024,768]{1,0:T(8,128)(2,1)S(1)}, bf16[1024,768]{1,0:T(8,128)(2,1)}, u32[]{:S(2)}) copy-start(bf16[1024,768]{1,0:T(8,128)(2,1)} %get-tuple-element.89.refs_0_) | copy-start | bytes 4718596
  243.0 5.0 %copy-start.1 = (bf16[1024,768]{1,0:T(8,128)(2,1)S(1)}, bf16[1024,768]{1,0:T(8,128)(2,1)}, u32[]{:S(2)}) copy-start(bf16[1024,768]{1,0:T(8,128)(2,1)} %get-tuple-element.90.refs_1_) | copy-start | bytes 4718596
  244.4 14.5 %collective-permute-start.22 = (bf16[4,80,768]{2,1,0:T(8,128)(2,1)}, bf16[4,80,768]{2,1,0:T(8,128)(2,1)}, u32[]{:S(2)}, u32[]{:S(2)}) collective-permute-start(bf16[4,80,768]{2,1,0:T(8,128)(2,1)} %copy-done.14), channel_id=1, source_target_pairs={{0,2},{1,3},{2,0},{3,1},{4,6},{5,7},{6,4},{7,5},{8,10},{9,11},{10,... | collective-permute-start | bytes 1474568 | tf_op jit(solution)/shard_map/ppermute | solution.py:367
  245.1 23.1 %collective-permute-start.23 = (bf16[4,80,768]{2,1,0:T(8,128)(2,1)}, bf16[4,80,768]{2,1,0:T(8,128)(2,1)}, u32[]{:S(2)}, u32[]{:S(2)}) collective-permute-start(bf16[4,80,768]{2,1,0:T(8,128)(2,1)} %copy-done.13), channel_id=1, source_target_pairs={{0,4},{1,5},{2,6},{3,7},{4,0},{5,1},{6,2},{7,3},{8,12},{9,13},{10,... | collective-permute-start | bytes 1474568 | tf_op jit(solution)/shard_map/ppermute | solution.py:367
  246.6 21.6 %collective-permute-start.24 = (bf16[4,80,768]{2,1,0:T(8,128)(2,1)}, bf16[4,80,768]{2,1,0:T(8,128)(2,1)}, u32[]{:S(2)}, u32[]{:S(2)}) collective-permute-start(bf16[4,80,768]{2,1,0:T(8,128)(2,1)} %copy-done.12), channel_id=1, source_target_pairs={{0,6},{1,7},{2,4},{3,5},{4,2},{5,3},{6,0},{7,1},{8,14},{9,15},{10,... | collective-permute-start | bytes 1474568 | tf_op jit(solution)/shard_map/ppermute | solution.py:367
  248.0 1.6 copy-start.2
  249.6 18.6 %copy-start.8 = (bf16[4,80,768]{2,1,0:T(8,128)(2,1)S(1)}, bf16[4,80,768]{2,1,0:T(8,128)(2,1)}, u32[]{:S(2)}) copy-start(bf16[4,80,768]{2,1,0:T(8,128)(2,1)} %copy-done.7) | copy-start | bytes 1474564
  269.8 9.6 %collective-permute-start.25 = (bf16[80,768]{1,0:T(8,128)(2,1)S(1)}, bf16[80,768]{1,0:T(8,128)(2,1)S(1)}, u32[]{:S(2)}, u32[]{:S(2)}) collective-permute-start(bf16[80,768]{1,0:T(8,128)(2,1)S(1)} %get-tuple-element.119), channel_id=1, source_target_pairs={{0,8},{1,9},{2,10},{3,11},{4,12},{5,13},{6,14},{7,15},{8,16},{9,17... | collective-permute-start | bytes 368648 | tf_op jit(solution)/shard_map/ppermute | solution.py:367
  271.0 11.3 %collective-permute-start.26 = (bf16[80,768]{1,0:T(8,128)(2,1)S(1)}, bf16[80,768]{1,0:T(8,128)(2,1)S(1)}, u32[]{:S(2)}, u32[]{:S(2)}) collective-permute-start(bf16[80,768]{1,0:T(8,128)(2,1)S(1)} %get-tuple-element.121), channel_id=1, source_target_pairs={{0,16},{1,17},{2,18},{3,19},{4,20},{5,21},{6,22},{7,23},{8,24},{9,... | collective-permute-start | bytes 368648 | tf_op jit(solution)/shard_map/ppermute | solution.py:367
  272.1 10.2 %collective-permute-start.27 = (bf16[80,768]{1,0:T(8,128)(2,1)S(1)}, bf16[80,768]{1,0:T(8,128)(2,1)S(1)}, u32[]{:S(2)}, u32[]{:S(2)}) collective-permute-start(bf16[80,768]{1,0:T(8,128)(2,1)S(1)} %get-tuple-element.120), channel_id=1, source_target_pairs={{0,24},{1,25},{2,26},{3,27},{4,28},{5,29},{6,30},{7,31},{8,0},{9,1... | collective-permute-start | bytes 368648 | tf_op jit(solution)/shard_map/ppermute | solution.py:367
Sparse Core Ops, SparseCore 0:
  11.5 97.0 all-gather.1
  244.5 30.7 reduce-scatter.1
